TPU v7x, 32 devices: a whole 2x2x4 slice. The times are simulated.
32 devices in a mesh: cfg: 2 (over y), tm: 4 (over z), space: 2 (over x), spin: 2 (over core).
Axes of the slice: x: 2, y: 2, z: 4, core: 2. Of those that a mesh axis runs over, the one named last changes fastest.
Arguments:
- eigenvectors: bfloat16 [8, 2, 3, 16, 2, 2, 128], P(('cfg', 'tm'), None, None, 'space'), parts along dimension 0, may hold values from -6 to 6
- gauge_links: bfloat16 [8, 3, 2, 3, 3, 16, 4], P(('cfg', 'tm'), None, None, None, None, 'space'), parts along dimension 0, may hold values from -2.4375 to 2.4375
- perambulators: bfloat16 [8, 512, 1024], P(('cfg', 'tm'), ('space', 'spin')), parts along dimension 0, may hold values from -0.1875 to 0.1875
- source_times: int32 [16], replicated, may hold values from 0 to 3
- insert_offsets: int32 [4], replicated, may hold values from 0 to 2
- derivative_dirs: int32 [3], replicated, may hold values from 0 to 2, each once
Outputs:
- elementals: float32 [8, 128, 3, 2, 128], P(('cfg', 'tm'), 'space', None, None, 'spin'), parts along dimension 0
- chain_products: bfloat16 [8, 512, 1024], P(('cfg', 'tm'), ('space', 'spin')), parts along dimension 0
- correlator: float32 [32, 2], P('cfg'), parts along dimension 0
There are 2 independent parts, one for each index of `cfg`. A program takes and returns all parts, laid end to end along the dimension named above; an argument that names none is the same for every part. Nothing has to cross between parts.
Inputs may be any that keep to these rules, and one draw needn't show every extreme that they name: `derivative_dirs`: each of 0, 1, 2 appears once.
All inputs are finite; a program needn't handle non-finite values.
Results may differ from a plain program's by a relative error of at most 0.012.
Values may be sent and summed in bfloat16 or wider, within the bound.
No kernel may reach another device: no remote copies, remote signals or barrier semaphores. Data moves between devices by JAX's collectives and lax.ppermute only.
A program may use at most 64 MiB of HBM per device.

v0:
```python
import math

import jax
import jax.numpy as jnp
import numpy as np
from jax import lax
from jax.sharding import PartitionSpec as P


def shifted(block, axis, distance):
    devices = range(lax.axis_size(axis))
    route = [((i - distance) % len(devices), i) for i in devices]
    return lax.ppermute(block, axis, route)


def gamma_tables():
    sigma_real = np.zeros((3, 2, 2), np.float32)
    sigma_imag = np.zeros((3, 2, 2), np.float32)
    sigma_real[0] = [[0.0, 1.0], [1.0, 0.0]]
    sigma_imag[1] = [[0.0, -1.0], [1.0, 0.0]]
    sigma_real[2] = [[1.0, 0.0], [0.0, -1.0]]
    gamma_real = np.zeros((3, 4, 4), np.float32)
    gamma_imag = np.zeros((3, 4, 4), np.float32)
    gamma_real[:, 0:2, 2:4] = sigma_imag
    gamma_imag[:, 0:2, 2:4] = -sigma_real
    gamma_real[:, 2:4, 0:2] = -sigma_imag
    gamma_imag[:, 2:4, 0:2] = sigma_real
    return (gamma_real, gamma_imag)


def color_product(matrix, vectors):
    return jnp.sum(matrix[:, :, :, :, :, None] * vectors[None], axis=1)


def times_links(link_field, vectors):
    real_part = color_product(link_field[0], vectors[0]) - color_product(link_field[1], vectors[1])
    imag_part = color_product(link_field[0], vectors[1]) + color_product(link_field[1], vectors[0])
    return jnp.stack([real_part, imag_part])


def times_adjoint(link_field, vectors):
    swapped = jnp.swapaxes(link_field, 1, 2)
    real_part = color_product(swapped[0], vectors[0]) + color_product(swapped[1], vectors[1])
    imag_part = color_product(swapped[0], vectors[1]) - color_product(swapped[1], vectors[0])
    return jnp.stack([real_part, imag_part])


def block_matrix(real_part, imag_part):
    upper_half = jnp.concatenate([real_part, imag_part], axis=1)
    lower_half = jnp.concatenate([-imag_part, real_part], axis=1)
    return jnp.concatenate([upper_half, lower_half], axis=0)


def row_block(matrix_rows):
    matrix_order = matrix_rows.shape[1] // 2
    return block_matrix(matrix_rows[:, :matrix_order], matrix_rows[:, matrix_order:])


def operator_matrix(elementals_wide, derivative_dirs):
    gamma_real, gamma_imag = gamma_tables()
    select = (derivative_dirs[:, None] == jnp.arange(3, dtype=jnp.int32)[None, :]).astype(
        jnp.float32
    )
    mixed_real = jnp.einsum(
        "km,kpq->mpq", select, jnp.asarray(gamma_real), precision=lax.Precision.HIGHEST
    )
    mixed_imag = jnp.einsum(
        "km,kpq->mpq", select, jnp.asarray(gamma_imag), precision=lax.Precision.HIGHEST
    )
    elem_real = elementals_wide[:, :, 0, :]
    elem_imag = elementals_wide[:, :, 1, :]
    pattern = "mpq,amb->paqb"
    real_part = jnp.einsum(
        pattern, mixed_real, elem_real, precision=lax.Precision.HIGHEST
    ) - jnp.einsum(pattern, mixed_imag, elem_imag, precision=lax.Precision.HIGHEST)
    imag_part = jnp.einsum(
        pattern, mixed_real, elem_imag, precision=lax.Precision.HIGHEST
    ) + jnp.einsum(pattern, mixed_imag, elem_real, precision=lax.Precision.HIGHEST)
    matrix_order = 4 * elementals_wide.shape[0]
    real_part = real_part.reshape((matrix_order, matrix_order)).astype(jnp.bfloat16)
    imag_part = imag_part.reshape((matrix_order, matrix_order)).astype(jnp.bfloat16)
    return block_matrix(real_part, imag_part)


def row_trace(product, first_row):
    row_count, width = product.shape
    matrix_order = width // 2
    diagonal = (
        jnp.arange(matrix_order, dtype=jnp.int32)[None, :]
        == first_row + jnp.arange(row_count, dtype=jnp.int32)[:, None]
    ).astype(jnp.float32)
    return jnp.stack(
        [
            jnp.sum(product[:, :matrix_order] * diagonal),
            jnp.sum(product[:, matrix_order:] * diagonal),
        ]
    )


def correlate(traces, source_times, insert_offsets):
    slot_count = traces.shape[0]
    counts = jnp.sum(
        (insert_offsets[:, None] == jnp.arange(3, dtype=jnp.int32)[None, :]).astype(jnp.float32),
        axis=0,
    )
    weighted = jnp.sum(traces * counts[None, :, None], axis=1)
    picker = (source_times[:, None] == jnp.arange(slot_count, dtype=jnp.int32)[None, :]).astype(
        jnp.float32
    )
    return jnp.dot(picker, weighted, precision=lax.Precision.HIGHEST)


def on_device(
    eigenvectors, gauge_links, perambulators, source_times, insert_offsets, derivative_dirs
):
    vectors = eigenvectors[0]
    link_block = gauge_links[0]
    peram_rows = perambulators[0]
    planes, side_cells, mode_count = (vectors.shape[2], vectors.shape[3], vectors.shape[5])
    spin_count = lax.axis_size("spin")
    space_count = lax.axis_size("space")
    half_modes = mode_count // spin_count
    chosen = lax.dynamic_slice_in_dim(vectors, lax.axis_index("spin") * half_modes, half_modes, 5)
    chosen_wide = chosen.astype(jnp.float32)
    norm_scale = 1.0 / math.sqrt(24.0 * planes * space_count * side_cells * side_cells)
    upper_plane = shifted(chosen[:, :, :1], "space", -1)
    columns = []
    for direction in range(3):
        spatial_axis = 4 - direction
        link_field = (
            link_block[direction]
            .reshape((2, 3, 3, planes, side_cells, side_cells))
            .astype(jnp.float32)
        )
        adjoint = times_adjoint(link_field, chosen_wide).astype(jnp.bfloat16)
        if direction == 2:
            forward_field = jnp.concatenate([chosen[:, :, 1:], upper_plane], axis=2).astype(
                jnp.float32
            )
            lower_plane = shifted(adjoint[:, :, planes - 1 :], "space", 1)
            behind = jnp.concatenate([lower_plane, adjoint[:, :, : planes - 1]], axis=2)
        else:
            forward_field = jnp.roll(chosen_wide, -1, axis=spatial_axis)
            behind = jnp.roll(adjoint, 1, axis=spatial_axis)
        behind_wide = lax.optimization_barrier(behind).astype(jnp.float32)
        derived = (times_links(link_field, forward_field) - behind_wide).astype(jnp.bfloat16)
        columns.append(derived.reshape((-1, half_modes)))
        columns.append(jnp.concatenate([derived[1], -derived[0]], axis=0).reshape((-1, half_modes)))
    stacked = jnp.stack(columns, axis=1).reshape((columns[0].shape[0], -1))
    flat_vectors = vectors.reshape((-1, mode_count))
    partial_sum = lax.dot_general(
        flat_vectors, stacked, (((0,), (0,)), ((), ())), preferred_element_type=jnp.float32
    )
    partial_sum = (partial_sum * norm_scale).reshape((mode_count, 3, 2, half_modes))
    summed = lax.psum(partial_sum, "space")
    share_rows = mode_count // space_count
    elementals = lax.dynamic_slice_in_dim(
        summed, lax.axis_index("space") * share_rows, share_rows, 0
    )
    full_rounded = lax.all_gather(summed.astype(jnp.bfloat16), "spin", axis=3, tiled=True)
    operator = operator_matrix(full_rounded.astype(jnp.float32), derivative_dirs)
    matrix_order = peram_rows.shape[1] // 2
    row_count = peram_rows.shape[0]
    first_row = lax.axis_index(("space", "spin")) * row_count
    first_product = jnp.dot(peram_rows, operator, preferred_element_type=jnp.float32) * (
        1.0 / math.sqrt(matrix_order)
    )
    first_rounded = first_product.astype(jnp.bfloat16)
    next_rows = shifted(first_rounded, "tm", -1)
    gathered = lax.all_gather(first_rounded, ("space", "spin"), axis=0, tiled=True)
    right_block = row_block(gathered)
    second_product = jnp.dot(next_rows, right_block, preferred_element_type=jnp.float32)
    second_rounded = second_product.astype(jnp.bfloat16)
    next_products = shifted(second_rounded, "tm", -1)
    third_product = jnp.dot(next_products, right_block, preferred_element_type=jnp.float32)
    local_traces = jnp.stack(
        [
            row_trace(first_product, first_row),
            row_trace(second_product, first_row),
            row_trace(third_product, first_row),
        ]
    )
    slot_count = lax.axis_size("tm")
    placed = (jnp.arange(slot_count, dtype=jnp.int32) == lax.axis_index("tm")).astype(jnp.float32)
    traces = lax.psum(placed[:, None, None] * local_traces[None], ("tm", "space", "spin"))
    correlator = correlate(traces, source_times, insert_offsets)
    chain_products = (third_product * math.sqrt(matrix_order)).astype(jnp.bfloat16)
    return (elementals[None], chain_products[None], correlator)


def solution(mesh):
    in_specs = (
        P(("cfg", "tm"), None, None, "space", None, None, None),
        P(("cfg", "tm"), None, None, None, None, "space", None),
        P(("cfg", "tm"), ("space", "spin"), None),
        P(),
        P(),
        P(),
    )
    out_specs = (
        P(("cfg", "tm"), "space", None, None, "spin"),
        P(("cfg", "tm"), ("space", "spin"), None),
        P("cfg", None),
    )
    return jax.shard_map(
        on_device, mesh=mesh, in_specs=in_specs, out_specs=out_specs, check_vma=False
    )
```

profile of v0, /device:TPU:0, one launch (start us, length us, event | category | flops | bytes accessed | tf_op | source)
XLA Modules:
  0.0 128.6 jit_solution(14775452391624116234)
XLA Ops:
  7.2 0.9 constant_dynamic-slice_fusion
  9.4 3.0 %collective-permute-start.1 = (bf16[2,3,1,2,2,64]{5,2,4,3,1,0:T(2,128)(2,1)S(1)}, bf16[2,3,1,2,2,64]{5,2,4,3,1,0:T(2,128)(2,1)S(1)}, u32[]{:S(2)}, u32[]{:S(2)}) collective-permute-start(bf16[2,3,1,2,2,64]{5,2,4,3,1,0:T(2,128)(2,1)S(1)} %pad_maximum_fusion.8), channel_id=1, source_target_pairs={{2,0},{0,2},{3,1},{1,3},{6,4},{4,6},{7,5},{5,7},{10,8},{8,10},{11,... | collective-permute-start | bytes 9224 | tf_op jit(solution)/shard_map/ppermute | solution.py:13
  14.1 2.1 %collective-permute-done = bf16[2,3,1,2,2,64]{5,2,4,3,1,0:T(2,128)(2,1)S(1)} collective-permute-done((bf16[2,3,1,2,2,64]{5,2,4,3,1,0:T(2,128)(2,1)S(1)}, bf16[2,3,1,2,2,64]{5,2,4,3,1,0:T(2,128)(2,1)S(1)}, u32[]{:S(2)}, u32[]{:S(2)}) %collective-permute-start) | collective-permute-done | bytes 3104 | tf_op jit(solution)/shard_map/ppermute | solution.py:13
  17.0 0.9 convolution_multiply_fusion
  18.4 22.3 %all-reduce.2.cloned.1.call-done = f32[128,3,2,64]{0,3,2,1:T(8,128)} async-done(((f32[128,3,2,64]{0,3,2,1:T(8,128)}), f32[128,3,2,64]{0,3,2,1:T(8,128)}) %all-reduce.2.cloned.1.call-update) | async-done | bytes 196624 | tf_op jit(solution)/shard_map/psum | solution.py:155
  40.7 0.9 convert_element_type.105
  41.8 1.9 %all_gather.6 = bf16[128,3,2,128]{0,2,1,3:T(2,128)(2,1)S(1)} all-gather(bf16[128,3,2,64]{0,2,1,3:T(2,128)(2,1)S(1)} %copy.186), channel_id=1, replica_groups=mesh['cfg'=2,'tm'=4,'space'=2,'spin'=2] {'spin'}, dimensions={3}, use_global_device_ids=true | all-gather | bytes 294912 | tf_op jit(solution)/shard_map/all_gather | solution.py:160
  44.3 1.0 fusion.27
  45.3 1.0 fusion.10
  46.7 0.9 fusion.25
  47.6 1.0 fusion.11
  49.0 1.5 %fusion.73 = (bf16[128,1024]{0,1:T(8,128)(2,1)}, f32[128,1024]{0,1:T(8,128)S(1)}) fusion(bf16[1,128,1024]{2,1,0:T(8,128)(2,1)S(1)} %copy-done, bf16[512,512]{1,0:T(8,128)(2,1)S(1)} %bitcast.176, bf16[512,512]{1,0:T(8,128)(2,1)S(1)} %fusion.64, bf16[512,512]{1,0:T(8,128)(2,1)S(1)} %bitcast.175), kind=kOutput, calls=%fused_computation.181 | convolution fusion | flops 277086208 | bytes 2621440 | tf_op jit(solution)/shard_map/dot_general | solution.py:165
  50.6 3.3 %collective-permute-start.2 = (bf16[128,1024]{0,1:T(8,128)(2,1)}, bf16[128,1024]{0,1:T(8,128)(2,1)S(1)}, u32[]{:S(2)}, u32[]{:S(2)}) collective-permute-start(bf16[128,1024]{0,1:T(8,128)(2,1)} %get-tuple-element.106), channel_id=1, source_target_pairs={{4,0},{8,4},{12,8},{0,12},{5,1},{9,5},{13,9},{1,13},{6,2},{10,6},{... | collective-permute-start | bytes 786440 | tf_op jit(solution)/shard_map/ppermute | solution.py:13
  53.9 13.6 %all-gather.2.cloned.1.call-done = bf16[512,1024]{0,1:T(8,128)(2,1)} async-done(((bf16[128,1024]{0,1:T(8,128)(2,1)}), bf16[512,1024]{0,1:T(8,128)(2,1)}) %all-gather.2.cloned.1.call-update) | async-done | bytes 1048592 | tf_op jit(solution)/shard_map/all_gather | solution.py:170
  67.4 1.4 %slice_negate_fusion = (bf16[512,512]{0,1:T(8,128)(2,1)S(1)}, bf16[512,512]{0,1:T(8,128)(2,1)S(1)}) fusion(bf16[512,1024]{0,1:T(8,128)(2,1)} %all-gather.2.cloned.1.call-done), kind=kLoop, calls=%fused_computation.24 | loop fusion | flops 262144 | bytes 2097152 | tf_op jit(solution)/shard_map/neg | solution.py:50
  69.0 1.5 %fusion.74 = (bf16[128,1024]{1,0:T(8,128)(2,1)}, f32[128,1024]{1,0:T(8,128)S(1)}) fusion(bf16[128,1024]{0,1:T(8,128)(2,1)S(1)} %collective-permute-done.2, bf16[512,512]{0,1:T(8,128)(2,1)S(1)} %get-tuple-element.64, bf16[512,512]{0,1:T(8,128)(2,1)S(1)} %get-tuple-element.63, bf16[512,1024]{0,1:T(8,128)(2,1)S(1)} %copy-done.1), kind=kOutput, calls=%fused_computation.182 | convolution fusion | flops 274857984 | bytes 3145728 | tf_op jit(solution)/shard_map/dot_general | solution.py:172
  70.5 3.3 %collective-permute-start.3 = (bf16[128,1024]{1,0:T(8,128)(2,1)}, bf16[128,1024]{1,0:T(8,128)(2,1)}, u32[]{:S(2)}, u32[]{:S(2)}) collective-permute-start(bf16[128,1024]{1,0:T(8,128)(2,1)} %get-tuple-element.108), channel_id=1, source_target_pairs={{4,0},{8,4},{12,8},{0,12},{5,1},{9,5},{13,9},{1,13},{6,2},{10,6},{... | collective-permute-start | bytes 786440 | tf_op jit(solution)/shard_map/ppermute | solution.py:13
  75.1 5.1 %collective-permute-done.3 = bf16[128,1024]{1,0:T(8,128)(2,1)} collective-permute-done((bf16[128,1024]{1,0:T(8,128)(2,1)}, bf16[128,1024]{1,0:T(8,128)(2,1)}, u32[]{:S(2)}, u32[]{:S(2)}) %collective-permute-start.3) | collective-permute-done | bytes 262176 | tf_op jit(solution)/shard_map/ppermute | solution.py:13
  80.1 1.9 %fusion.18 = f32[128,1024]{1,0:T(8,128)S(1)} fusion(bf16[128,1024]{1,0:T(8,128)(2,1)} %collective-permute-done.3, bf16[512,512]{0,1:T(8,128)(2,1)} %copy-done.3, bf16[512,512]{0,1:T(8,128)(2,1)S(1)} %get-tuple-element.63, bf16[512,1024]{0,1:T(8,128)(2,1)S(1)} %copy-done.1), kind=kOutput, calls=%fused_computation.20 | convolution fusion | flops 274726912 | bytes 2883584 | tf_op jit(solution)/shard_map/dot_general | solution.py:175
  82.4 0.9 fusion.22
  83.2 1.4 %maximum_bitcast_fusion = f32[1,2]{1,0:T(1,128)S(1)} fusion(f32[1]{0:T(128)} %bitcast.78, f32[1]{0:T(128)} %bitcast.77), kind=kLoop, calls=%fused_computation.163 | loop fusion | flops 2 | bytes 16 | tf_op jit(solution)/shard_map/stack | solution.py:176
  84.6 1.3 %maximum_bitcast_fusion.1 = f32[1,2]{1,0:T(1,128)S(1)} fusion(f32[1]{0:T(128)} %bitcast.81, f32[1]{0:T(128)} %bitcast.80), kind=kLoop, calls=%fused_computation.164 | loop fusion | flops 2 | bytes 16 | tf_op jit(solution)/shard_map/stack | solution.py:176
  86.0 1.3 %maximum_bitcast_fusion.2 = f32[1,2]{1,0:T(1,128)S(1)} fusion(f32[1]{0:T(128)} %bitcast.84, f32[1]{0:T(128)} %bitcast.83), kind=kLoop, calls=%fused_computation.165 | loop fusion | flops 2 | bytes 16 | tf_op jit(solution)/shard_map/stack | solution.py:176
  88.1 32.8 %psum.15 = f32[4,3,2]{0,2,1:T(2,128)S(1)} all-reduce(f32[4,3,2]{0,2,1:T(2,128)S(1)} %broadcast_multiply_fusion), channel_id=1, replica_groups=mesh['cfg'=2,'tm'=4,'space'=2,'spin'=2] {'tm','space','spin'}, use_global_device_ids=true, to_apply=%region_31.32 | all-reduce | flops 24 | bytes 192 | tf_op jit(solution)/shard_map/psum | solution.py:185
  (110 shorter events, 8.6 us)
Async XLA Ops:
  7.2 41.8 %copy-start = (bf16[1,128,1024]{2,1,0:T(8,128)(2,1)S(1)}, bf16[1,128,1024]{2,1,0:T(8,128)(2,1)}, u32[]{:S(2)}) copy-start(bf16[1,128,1024]{2,1,0:T(8,128)(2,1)} %param.10) | copy-start | bytes 786436
  7.2 33.5 %all-reduce.2.cloned.1.call-start = ((), (), s32[]{:S(2)}) async-start(), calls=%async_computation | async-start | bytes 393216 | tf_op jit(solution)/shard_map/psum | solution.py:155
  9.4 4.7 %collective-permute-start.1 = (bf16[2,3,1,2,2,64]{5,2,4,3,1,0:T(2,128)(2,1)S(1)}, bf16[2,3,1,2,2,64]{5,2,4,3,1,0:T(2,128)(2,1)S(1)}, u32[]{:S(2)}, u32[]{:S(2)}) collective-permute-start(bf16[2,3,1,2,2,64]{5,2,4,3,1,0:T(2,128)(2,1)S(1)} %pad_maximum_fusion.8), channel_id=1, source_target_pairs={{2,0},{0,2},{3,1},{1,3},{6,4},{4,6},{7,5},{5,7},{10,8},{8,10},{11,... | collective-permute-start | bytes 9224 | tf_op jit(solution)/shard_map/ppermute | solution.py:13
  12.4 3.8 %collective-permute-start = (bf16[2,3,1,2,2,64]{5,2,4,3,1,0:T(2,128)(2,1)S(1)}, bf16[2,3,1,2,2,64]{5,2,4,3,1,0:T(2,128)(2,1)S(1)}, u32[]{:S(2)}, u32[]{:S(2)}) collective-permute-start(bf16[2,3,1,2,2,64]{5,2,4,3,1,0:T(2,128)(2,1)S(1)} %slice.278), channel_id=1, source_target_pairs={{2,0},{0,2},{3,1},{1,3},{6,4},{4,6},{7,5},{5,7},{10,8},{8,10},{11,... | collective-permute-start | bytes 9224 | tf_op jit(solution)/shard_map/ppermute | solution.py:13
  16.2 0.8 copy-start.4
  16.4 1.6 %copy-start.6 = (f32[3,4,4]{2,0,1:T(4,128)S(1)}, f32[3,4,4]{2,0,1:T(4,128)}, u32[]{:S(2)}) copy-start(f32[3,4,4]{2,0,1:T(4,128)} %constant.38.clone) | copy-start | bytes 580
  16.5 1.6 %copy-start.7 = (s32[3]{0:T(128)S(1)}, s32[3]{0:T(128)}, u32[]{:S(2)}) copy-start(s32[3]{0:T(128)} %param.13) | copy-start | bytes 40
  16.5 1.8 %copy-start.5 = (f32[3,4,4]{2,0,1:T(4,128)S(1)}, f32[3,4,4]{2,0,1:T(4,128)}, u32[]{:S(2)}) copy-start(f32[3,4,4]{2,0,1:T(4,128)} %constant.39.clone) | copy-start | bytes 580
  17.9 49.5 %all-gather.2.cloned.1.call-start = ((), (), s32[]{:S(2)}) async-start(), calls=%async_computation.1 | async-start | bytes 1310720 | tf_op jit(solution)/shard_map/all_gather | solution.py:170
  48.9 1.5 %copy-start.8 = (s32[4]{0:T(128)S(1)}, s32[4]{0:T(128)}, u32[]{:S(2)}) copy-start(s32[4]{0:T(128)} %param.12) | copy-start | bytes 52
  50.6 18.2 %collective-permute-start.2 = (bf16[128,1024]{0,1:T(8,128)(2,1)}, bf16[128,1024]{0,1:T(8,128)(2,1)S(1)}, u32[]{:S(2)}, u32[]{:S(2)}) collective-permute-start(bf16[128,1024]{0,1:T(8,128)(2,1)} %get-tuple-element.106), channel_id=1, source_target_pairs={{4,0},{8,4},{12,8},{0,12},{5,1},{9,5},{13,9},{1,13},{6,2},{10,6},{... | collective-permute-start | bytes 786440 | tf_op jit(solution)/shard_map/ppermute | solution.py:13
  67.4 1.5 %copy-start.1 = (bf16[512,1024]{0,1:T(8,128)(2,1)S(1)}, bf16[512,1024]{0,1:T(8,128)(2,1)}, u32[]{:S(2)}) copy-start(bf16[512,1024]{0,1:T(8,128)(2,1)} %all-gather.2.cloned.1.call-done) | copy-start | bytes 3145732
  68.8 1.7 %copy-start.3 = (bf16[512,512]{0,1:T(8,128)(2,1)}, bf16[512,512]{0,1:T(8,128)(2,1)S(1)}, u32[]{:S(2)}) copy-start(bf16[512,512]{0,1:T(8,128)(2,1)S(1)} %get-tuple-element.64) | copy-start | bytes 1572868
  69.0 4.9 %copy-start.2 = (f32[128,3,2,64]{0,3,2,1:T(8,128)S(1)}, f32[128,3,2,64]{0,3,2,1:T(8,128)}, u32[]{:S(2)}) copy-start(f32[128,3,2,64]{0,3,2,1:T(8,128)} %all-reduce.2.cloned.1.call-done) | copy-start | bytes 589828
  70.5 9.6 %collective-permute-start.3 = (bf16[128,1024]{1,0:T(8,128)(2,1)}, bf16[128,1024]{1,0:T(8,128)(2,1)}, u32[]{:S(2)}, u32[]{:S(2)}) collective-permute-start(bf16[128,1024]{1,0:T(8,128)(2,1)} %get-tuple-element.108), channel_id=1, source_target_pairs={{4,0},{8,4},{12,8},{0,12},{5,1},{9,5},{13,9},{1,13},{6,2},{10,6},{... | collective-permute-start | bytes 786440 | tf_op jit(solution)/shard_map/ppermute | solution.py:13
  82.4 38.6 %copy-start.9 = (s32[16]{0:T(128)S(1)}, s32[16]{0:T(128)}, u32[]{:S(2)}) copy-start(s32[16]{0:T(128)} %param.11) | copy-start | bytes 196
Sparse Core Ops, SparseCore 0:
  18.1 22.6 all-reduce.1
  50.6 16.8 all-gather.1
where the time goes:
time: 129 us
  waiting for transfers between devices  43.6 us (34%)
  blocking collectives  34.7 us (27%)
  between operations  14.8 us (11%)
  matrix products  10.9 us (8%)
  other arithmetic  10.2 us (8%)
  starting transfers between devices  9.81 us (8%)
  local copies, waits for them, and re-layouts  4.58 us (4%)
    psum x1, blocking collectives, on_device(): lax.psum(placed[:, None, None] * local_traces[None], ('tm', 'space', 'spi...  32.8 us
    psum x1, waiting for transfers between devices, on_device(): summed = lax.psum(partial_sum, 'space')  22.3 us
    all_gather x1, waiting for transfers between devices, on_device(): lax.all_gather(first_rounded, ('space', 'spin'), axis=0, tiled=True)  13.6 us
    ppermute x4, starting transfers between devices, shifted(): return lax.ppermute(block, axis, route)  9.73 us
    ppermute x4, waiting for transfers between devices, shifted(): return lax.ppermute(block, axis, route)  7.7 us
    another operation x4, other arithmetic, on_device(): jnp.stack([row_trace(first_product, first_row), row_trace(second_product,...  4.04 us
  transfers between devices with their start and end apart: 6, of which 5 were waited for; matrix products, arithmetic and copies ran while one was open for 3% of the time, Pallas kernels for 0%

commit v1 on v0

v1 whole, which is shorter than its diff:
```python
import functools
import math

import jax
import jax.numpy as jnp
from jax import lax
from jax.experimental import pallas as pl
from jax.experimental.pallas import tpu as pltpu

from jax.sharding import PartitionSpec as P

F32 = jnp.float32
BF16 = jnp.bfloat16


def from_offset(block, axis, distance):
    count = lax.axis_size(axis)
    return lax.ppermute(block, axis, [((i + distance) % count, i) for i in range(count)])


def from_diagonal(block, slot_step, space_step):
    slots, spaces = lax.axis_size("tm"), lax.axis_size("space")
    route = []
    for slot in range(slots):
        for place in range(spaces):
            source = ((slot + slot_step) % slots) * spaces + (place + space_step) % spaces
            route.append((source, slot * spaces + place))
    return lax.ppermute(block, ("tm", "space"), route)


def vmem_call(kernel, out_shape, scratch, flops, smem=()):
    def call(*operands):
        specs = [
            pl.BlockSpec(memory_space=pltpu.SMEM if i in smem else pltpu.VMEM)
            for i in range(len(operands))
        ]
        outs = jax.tree.map(lambda _: pl.BlockSpec(memory_space=pltpu.VMEM), out_shape)
        return pl.pallas_call(
            kernel,
            out_shape=out_shape,
            in_specs=specs,
            out_specs=outs,
            scratch_shapes=scratch,
            compiler_params=pltpu.CompilerParams(vmem_limit_bytes=40 * 1024 * 1024),
            cost_estimate=pl.CostEstimate(
                flops=flops, bytes_accessed=1 << 20, transcendentals=0
            ),
        )(*operands)

    return call


def moved(field, distance):
    rows = field.shape[0]
    return pltpu.roll(field, distance % rows, 0) if distance % rows else field


def ahead_of(field, stride, side):
    row = lax.broadcasted_iota(jnp.int32, field.shape, 0)
    last = (row // stride) % side == side - 1
    return jnp.where(last, moved(field, (side - 1) * stride), moved(field, -stride))


def behind_of(field, stride, side):
    row = lax.broadcasted_iota(jnp.int32, field.shape, 0)
    start = (row // stride) % side == 0
    return jnp.where(start, moved(field, (1 - side) * stride), moved(field, stride))


def elementals_kernel(cells, side, scale, slabs, dirs_ref, *refs):
    slab_refs, (elem_ref, oper_ref, rhs_ref, pick_ref) = refs[:-4], refs[-4:]
    slot_count = len(slab_refs) // slabs
    modes = elem_ref.shape[-1]
    for slot in range(slot_count):
        mine = slab_refs[slot * slabs : (slot + 1) * slabs]
        fields = [
            jnp.concatenate([ref[k * cells : (k + 1) * cells, :] for ref in mine], axis=0)
            for k in range(6)
        ]
        vectors = jnp.concatenate(fields, axis=0)
        links = jnp.concatenate([ref[6 * cells : 7 * cells, :] for ref in mine], axis=0).astype(F32)
        sites = slabs * cells
        wide = [field.astype(F32) for field in fields]
        for direction in range(3):
            stride = side**direction
            across = side if direction < 2 else sites // stride
            forward = [ahead_of(field, stride, across) for field in wide]
            terms = [[None] * 3 for _ in range(4)]
            for colour in range(3):
                for other in range(3):
                    at = direction * 18 + colour * 3 + other
                    link_real = links[:, at : at + 1]
                    link_imag = links[:, at + 9 : at + 10]
                    ahead_real, ahead_imag = forward[other], forward[3 + other]
                    here_real, here_imag = wide[colour], wide[3 + colour]
                    for kind, to, term in (
                        (0, colour, link_real * ahead_real - link_imag * ahead_imag),
                        (1, colour, link_real * ahead_imag + link_imag * ahead_real),
                        (2, other, link_real * here_real + link_imag * here_imag),
                        (3, other, link_real * here_imag - link_imag * here_real),
                    ):
                        held = terms[kind][to]
                        terms[kind][to] = term if held is None else held + term
            left, right = 2 * direction * modes, (2 * direction + 1) * modes
            for colour in range(3):
                parts = []
                for kind in range(2):
                    adjoint = terms[2 + kind][colour].astype(BF16).astype(F32)
                    parts.append(terms[kind][colour] - behind_of(adjoint, stride, across))
                real_part, imag_part = parts[0], parts[1]
                low, high = colour * sites, (3 + colour) * sites
                rhs_ref[low : low + sites, left : left + modes] = real_part.astype(BF16)
                rhs_ref[high : high + sites, left : left + modes] = imag_part.astype(BF16)
                rhs_ref[low : low + sites, right : right + modes] = imag_part.astype(BF16)
                rhs_ref[high : high + sites, right : right + modes] = (-real_part).astype(BF16)
        product = lax.dot_general(
            vectors, rhs_ref[...], (((0,), (0,)), ((), ())), preferred_element_type=F32
        )
        for direction in range(3):
            left = 2 * direction * modes
            real_part = product[:, left : left + modes] * scale
            imag_part = product[:, left + modes : left + 2 * modes] * scale
            if slot == 0:
                elem_ref[direction, 0] = real_part
                elem_ref[direction, 1] = imag_part
            pick_ref[direction, 0] = real_part.astype(BF16).astype(F32)
            pick_ref[direction, 1] = imag_part.astype(BF16).astype(F32)
        zero_real, zero_imag = pick_ref[dirs_ref[0], 0], pick_ref[dirs_ref[0], 1]
        one_real, one_imag = pick_ref[dirs_ref[1], 0], pick_ref[dirs_ref[1], 1]
        two_real, two_imag = pick_ref[dirs_ref[2], 0], pick_ref[dirs_ref[2], 1]
        sum_real = [[two_real, zero_real + one_imag], [zero_real - one_imag, -two_real]]
        sum_imag = [[two_imag, zero_imag - one_real], [zero_imag + one_real, -two_imag]]
        for p in range(2):
            for q in range(2):
                top, bottom = p * modes, (2 + p) * modes
                left, right = q * modes, (2 + q) * modes
                real_part = sum_real[p][q].astype(BF16)
                imag_part = sum_imag[p][q].astype(BF16)
                oper_ref[slot, top : top + modes, left : left + modes] = -imag_part
                oper_ref[slot, top : top + modes, right : right + modes] = real_part
                oper_ref[slot, bottom : bottom + modes, left : left + modes] = -real_part
                oper_ref[slot, bottom : bottom + modes, right : right + modes] = -imag_part


def times_operator(rows, operator):
    half = rows.shape[1] // 4
    upper = jnp.concatenate([rows[:, half : 2 * half], rows[:, 3 * half :]], axis=1)
    lower = jnp.concatenate([rows[:, :half], rows[:, 2 * half : 3 * half]], axis=1)
    both = jnp.dot(
        jnp.concatenate([upper, lower], axis=0), operator, preferred_element_type=F32
    )
    scale = 1.0 / math.sqrt(2.0 * half)
    count = rows.shape[0]
    above = both[:count] * scale
    below = both[count:] * (-scale)
    return jnp.concatenate([above[:, :half], below[:, :half], above[:, half:], below[:, half:]], 1)


def times_rows(left, right):
    order = left.shape[1] // 2
    count = left.shape[0]
    both = jnp.dot(
        jnp.concatenate([left[:, :order], left[:, order:]], axis=0),
        right,
        preferred_element_type=F32,
    )
    real_part = both[:count, :order] - both[count:, order:]
    imag_part = both[:count, order:] + both[count:, :order]
    return real_part, imag_part


def diagonal_sum(part, first_row):
    row = lax.broadcasted_iota(jnp.int32, part.shape, 0) + first_row
    column = lax.broadcasted_iota(jnp.int32, part.shape, 1)
    kept = jnp.where(row == column, part, 0.0)
    return jnp.sum(jnp.sum(kept, axis=0, keepdims=True), axis=1, keepdims=True)


def at_lanes(shape, values):
    lane = lax.broadcasted_iota(jnp.int32, shape, 1)
    total = jnp.zeros(shape, F32)
    for at, value in values:
        total = total + jnp.where(lane == at, value, 0.0)
    return total


def own_block(spaces, spins, space_step, spin_step):
    place = lax.rem(lax.axis_index("space") + space_step, spaces)
    spin = lax.rem(lax.axis_index("spin") + spin_step, spins)
    return place * spins + spin


def second_kernel(spaces, spins, oper_ref, next_ref, *refs):
    block_refs, (first_ref, second_ref, trace_ref) = refs[:-3], refs[-3:]
    count = next_ref.shape[0]
    order = next_ref.shape[1] // 2
    first_row = own_block(spaces, spins, 0, 0) * count
    for at, block_ref in enumerate(block_refs):
        product = times_operator(block_ref[...], oper_ref[0])
        start = pl.multiple_of(own_block(spaces, spins, at // spins, at % spins) * count, count)
        first_ref[pl.ds(start, count), :] = product.astype(BF16)
        if at == 0:
            first_real = diagonal_sum(product[:, :order], first_row)
            first_imag = diagonal_sum(product[:, order:], first_row)
    left = times_operator(next_ref[...], oper_ref[1]).astype(BF16)
    real_part, imag_part = times_rows(left, first_ref[...])
    second_ref[:, :order] = real_part.astype(BF16)
    second_ref[:, order:] = imag_part.astype(BF16)
    trace_ref[...] = at_lanes(
        trace_ref.shape,
        [
            (0, first_real),
            (1, first_imag),
            (2, diagonal_sum(real_part, first_row)),
            (3, diagonal_sum(imag_part, first_row)),
        ],
    )


def third_kernel(spaces, spins, second_ref, first_ref, early_ref, chain_ref, trace_ref):
    count = second_ref.shape[0]
    order = second_ref.shape[1] // 2
    first_row = own_block(spaces, spins, 0, 0) * count
    real_part, imag_part = times_rows(second_ref[...], first_ref[...])
    scale = math.sqrt(order)
    chain_ref[:, :order] = (real_part * scale).astype(BF16)
    chain_ref[:, order:] = (imag_part * scale).astype(BF16)
    late = at_lanes(
        early_ref.shape,
        [(4, diagonal_sum(real_part, first_row)), (5, diagonal_sum(imag_part, first_row))],
    )
    row = lax.broadcasted_iota(jnp.int32, trace_ref.shape, 0)
    values = jnp.broadcast_to((early_ref[...] + late)[0:1], trace_ref.shape)
    trace_ref[...] = jnp.where(row == lax.axis_index("tm"), values, 0.0)


def correlator_kernel(offsets_ref, times_ref, *refs):
    part_refs, out_ref = refs[:-1], refs[-1]
    traces = part_refs[0][...]
    for part_ref in part_refs[1:]:
        traces = traces + part_ref[...]
    lane = lax.broadcasted_iota(jnp.int32, (1, traces.shape[1]), 1)
    counts = jnp.zeros((1, traces.shape[1]), F32)
    for j in range(offsets_ref.shape[0]):
        counts = counts + jnp.where(lane // 2 == offsets_ref[j], 1.0, 0.0)
    weighted = traces * counts
    row = lax.broadcasted_iota(jnp.int32, (traces.shape[0], times_ref.shape[1]), 0)
    chosen = row == times_ref[...]
    for part in range(2):
        keep = (lane % 2 == part) & (lane < 6)
        column = jnp.sum(jnp.where(keep, weighted, 0.0), axis=1, keepdims=True)
        out_ref[part : part + 1, :] = jnp.sum(
            jnp.where(chosen, column, 0.0), axis=0, keepdims=True
        )


def on_device(
    eigenvectors, gauge_links, perambulators, source_times, insert_offsets, derivative_dirs
):
    spaces, spins, slots = lax.axis_size("space"), lax.axis_size("spin"), lax.axis_size("tm")
    planes, side, modes = eigenvectors.shape[3], eigenvectors.shape[4], eigenvectors.shape[6]
    cells = planes * side * side
    own_rows = perambulators[0]
    count, width = own_rows.shape
    order = width // 2

    vectors = eigenvectors.reshape((6 * cells, modes))
    links = gauge_links.reshape((54, cells)).T
    links = jnp.pad(links, ((0, 0), (0, modes - 54)))
    pack = jnp.concatenate([vectors, links], axis=0)

    slabs = [pack] + [from_offset(pack, "space", step) for step in range(1, spaces)]
    slabs.append(from_offset(pack, "tm", 1))
    slabs += [from_diagonal(pack, 1, step) for step in range(1, spaces)]

    next_rows = from_offset(own_rows, "tm", 1)
    blocks = []
    for space_step in range(spaces):
        block = own_rows if space_step == 0 else from_offset(own_rows, "space", space_step)
        blocks.append(block)
        for spin_step in range(1, spins):
            blocks.append(from_offset(block, "spin", spin_step))

    norm_scale = 1.0 / math.sqrt(6.0 * 4.0 * planes * spaces * side * side)
    elements, operators = vmem_call(
        functools.partial(elementals_kernel, cells, side, norm_scale, spaces),
        (
            jax.ShapeDtypeStruct((3, 2, modes, modes), F32),
            jax.ShapeDtypeStruct((2, 4 * modes, 4 * modes), BF16),
        ),
        [
            pltpu.VMEM((6 * cells * spaces, 6 * modes), BF16),
            pltpu.VMEM((3, 2, modes, modes), F32),
        ],
        10**8,
        smem=(0,),
    )(derivative_dirs, *slabs)

    first, second, early = vmem_call(
        functools.partial(second_kernel, spaces, spins),
        (
            jax.ShapeDtypeStruct((order, width), BF16),
            jax.ShapeDtypeStruct((count, width), BF16),
            jax.ShapeDtypeStruct((8, 128), F32),
        ),
        [],
        10**9,
    )(operators, next_rows, *blocks)

    next_second = from_offset(second, "tm", 1)

    rows, columns = modes // spaces, modes // spins
    share = lax.dynamic_slice(
        elements,
        (0, 0, lax.axis_index("space") * rows, lax.axis_index("spin") * columns),
        (3, 2, rows, columns),
    )
    elementals = jnp.transpose(share, (2, 0, 1, 3))

    chain, traces = vmem_call(
        functools.partial(third_kernel, spaces, spins),
        (
            jax.ShapeDtypeStruct((count, width), BF16),
            jax.ShapeDtypeStruct((-(-slots // 8) * 8, 128), F32),
        ),
        [],
        3 * 10**8,
    )(next_second, first, early)

    group = spaces * spins
    parts = [traces] + [from_offset(traces, ("space", "spin"), step) for step in range(1, group)]
    traces = functools.reduce(lambda a, b: a + b, parts)
    if slots & (slots - 1):
        parts = [lax.psum(traces, "tm")]
    else:
        step = 1
        while step < slots:
            other = lax.ppermute(traces, "tm", [(i ^ step, i) for i in range(slots)])
            parts = [traces, other]
            traces = traces + other
            step *= 2
    correlator = vmem_call(
        correlator_kernel,
        jax.ShapeDtypeStruct((2, source_times.shape[0]), F32),
        [],
        10**5,
        smem=(0,),
    )(insert_offsets, source_times[None, :], *parts)
    return (elementals[None], chain[None], correlator.T)


def solution(mesh):
    in_specs = (
        P(("cfg", "tm"), None, None, "space", None, None, None),
        P(("cfg", "tm"), None, None, None, None, "space", None),
        P(("cfg", "tm"), ("space", "spin"), None),
        P(),
        P(),
        P(),
    )
    out_specs = (
        P(("cfg", "tm"), "space", None, None, "spin"),
        P(("cfg", "tm"), ("space", "spin"), None),
        P("cfg", None),
    )
    return jax.shard_map(
        on_device, mesh=mesh, in_specs=in_specs, out_specs=out_specs, check_vma=False
    )
```

time: 129 us -> 50.8 us (0.39)
  blocking collectives: 34.7 us -> 0 us
  waiting for transfers between devices: 43.6 us -> 17.9 us
  between operations: 14.8 us -> 0.71 us
  starting transfers between devices: 9.81 us -> 22.5 us
  matrix products: 10.9 us -> 0 us
  other arithmetic: 10.2 us -> 0.02 us
  Pallas kernels: 0 us -> 6.49 us
  local copies, waits for them, and re-layouts: 4.58 us -> 2.96 us
    psum x1 -> x0, blocking collectives: 32.8 us -> none  [on_device(): lax.psum(placed[:, None, None] * local_traces[None], ('tm', 'space', 'spi...]
    psum x1 -> x0, waiting for transfers between devices: 22.3 us -> none  [on_device(): summed = lax.psum(partial_sum, 'space')]
    all_gather x1 -> x0, waiting for transfers between devices: 13.6 us -> none  [on_device(): lax.all_gather(first_rounded, ('space', 'spin'), axis=0, tiled=True)]
    ppermute x4 -> x13, starting transfers between devices: 9.73 us -> 22.5 us  [the longest x10 14.8 us: from_offset(): lax.ppermute(block, axis, [((i + distance) % count, i) for i in range(cou...]
    dot_general x11 -> x0, matrix products: 10.9 us -> none  [the longest x1 1.93 us: on_device(): jnp.dot(next_products, right_block, preferred_element_type=jnp.float32)]
    ppermute x4 -> x13, waiting for transfers between devices: 7.7 us -> 17.9 us  [the longest x10 11.8 us: from_offset(): lax.ppermute(block, axis, [((i + distance) % count, i) for i in range(cou...]
    pallas_call x0 -> x4, Pallas kernels: none -> 6.49 us  [call(): pl.pallas_call(kernel, out_shape=out_shape, in_specs=specs, out_specs=out...]
    another operation x6 -> x0, other arithmetic: 4.05 us -> none  [the longest x4 4.04 us: on_device(): jnp.stack([row_trace(first_product, first_row), row_trace(second_product,...]
  transfers between devices with their start and end apart: 6 -> 13, of which waited for: 5 -> 10; matrix products, arithmetic and copies ran while one was open for 3% -> 5% of each run, Pallas kernels for 0% -> 5%
where the time goes in v1:
time: 50.8 us; the launch traced here: 50.6 us
  starting transfers between devices  22.5 us (44%)
  waiting for transfers between devices  17.9 us (35%)
  Pallas kernels  6.49 us (13%)
  local copies, waits for them, and re-layouts  2.96 us (6%)
  between operations  0.71 us (1%)
    ppermute x10, starting transfers between devices, from_offset(): lax.ppermute(block, axis, [((i + distance) % count, i) for i in range(cou...  14.8 us
    ppermute x10, waiting for transfers between devices, from_offset(): lax.ppermute(block, axis, [((i + distance) % count, i) for i in range(cou...  11.8 us
    pallas_call x4, Pallas kernels, call(): pl.pallas_call(kernel, out_shape=out_shape, in_specs=specs, out_specs=out...  6.49 us
    ppermute x1, starting transfers between devices, from_diagonal(): return lax.ppermute(block, ('tm', 'space'), route)  4.83 us
    ppermute x2, waiting for transfers between devices, on_device(): other = lax.ppermute(traces, 'tm', [(i ^ step, i) for i in range(slots)])  4.33 us
    ppermute x2, starting transfers between devices, on_device(): other = lax.ppermute(traces, 'tm', [(i ^ step, i) for i in range(slots)])  2.82 us
    unnamed x12, local copies, waits for them, and re-layouts  2.62 us
    ppermute x1, waiting for transfers between devices, from_diagonal(): return lax.ppermute(block, ('tm', 'space'), route)  1.78 us
  transfers between devices with their start and end apart: 13, of which 10 were waited for; matrix products, arithmetic and copies ran while one was open for 5% of the time, Pallas kernels for 5%

profile of v1, /device:TPU:0, one launch (start us, length us, event | category | flops | bytes accessed | tf_op | source)
XLA Modules:
  0.0 50.6 jit_solution(7968897383928885377)
XLA Ops:
  0.6 3.0 %collective-permute-start.5 = (bf16[128,1024]{1,0:T(8,128)(2,1)}, bf16[128,1024]{1,0:T(8,128)(2,1)S(1)}, u32[]{:S(2)}, u32[]{:S(2)}) collective-permute-start(bf16[128,1024]{1,0:T(8,128)(2,1)} %bitcast.13), channel_id=1, source_target_pairs={{2,0},{0,2},{3,1},{1,3},{6,4},{4,6},{7,5},{5,7},{10,8},{8,10},{11,... | collective-permute-start | bytes 786440 | tf_op jit(solution)/shard_map/ppermute | solution.py:18
  3.6 3.6 %collective-permute-start.3 = (bf16[128,1024]{1,0:T(8,128)(2,1)}, bf16[128,1024]{1,0:T(8,128)(2,1)S(1)}, u32[]{:S(2)}, u32[]{:S(2)}) collective-permute-start(bf16[128,1024]{1,0:T(8,128)(2,1)} %bitcast.15), channel_id=1, source_target_pairs={{4,0},{8,4},{12,8},{0,12},{5,1},{9,5},{13,9},{1,13},{6,2},{10,6},{... | collective-permute-start | bytes 786440 | tf_op jit(solution)/shard_map/ppermute | solution.py:18
  7.2 2.9 %collective-permute-done.5.refs_2_ = bf16[128,1024]{1,0:T(8,128)(2,1)S(1)} collective-permute-done((bf16[128,1024]{1,0:T(8,128)(2,1)}, bf16[128,1024]{1,0:T(8,128)(2,1)S(1)}, u32[]{:S(2)}, u32[]{:S(2)}) %collective-permute-start.5) | collective-permute-done | bytes 262176 | tf_op jit(solution)/shard_map/ppermute | solution.py:18
  10.2 1.2 %copy.11 = bf16[1,3,2,3,3,8,4]{6,5,4,3,2,1,0:T(8,128)(2,1)S(1)} copy(bf16[1,3,2,3,3,8,4]{5,6,4,3,2,1,0:T(4,128)(2,1)} %param.7) | data formatting | bytes 6912 | tf_op args[1]
  11.6 0.6 %copy-done.4 = bf16[1,2,3,8,2,2,128]{6,5,4,3,2,1,0:T(2,128)(2,1)S(1)} copy-done((bf16[1,2,3,8,2,2,128]{6,5,4,3,2,1,0:T(2,128)(2,1)S(1)}, bf16[1,2,3,8,2,2,128]{6,5,4,3,2,1,0:T(2,128)(2,1)}, u32[]{:S(2)}) %copy-start.4) | copy-done | bytes 49176
  12.2 4.8 %collective-permute-start.2 = (bf16[224,128]{1,0:T(8,128)(2,1)S(1)}, bf16[224,128]{1,0:T(8,128)(2,1)S(1)}, u32[]{:S(2)}, u32[]{:S(2)}) collective-permute-start(bf16[224,128]{1,0:T(8,128)(2,1)S(1)} %fusion.1.refs_0_), channel_id=1, source_target_pairs={{6,0},{4,2},{10,4},{8,6},{14,8},{12,10},{2,12},{0,14},{7,1},{5,3},... | collective-permute-start | bytes 172040 | tf_op jit(solution)/shard_map/ppermute | solution.py:28
  17.5 1.8 %collective-permute-done.2.refs_3_ = bf16[224,128]{1,0:T(8,128)(2,1)S(1)} collective-permute-done((bf16[224,128]{1,0:T(8,128)(2,1)S(1)}, bf16[224,128]{1,0:T(8,128)(2,1)S(1)}, u32[]{:S(2)}, u32[]{:S(2)}) %collective-permute-start.2) | collective-permute-done | bytes 57376 | tf_op jit(solution)/shard_map/ppermute | solution.py:28
  19.2 0.5 %collective-permute-start = (bf16[224,128]{1,0:T(8,128)(2,1)S(1)}, bf16[224,128]{1,0:T(8,128)(2,1)S(1)}, u32[]{:S(2)}, u32[]{:S(2)}) collective-permute-start(bf16[224,128]{1,0:T(8,128)(2,1)S(1)} %fusion.1.refs_0_), channel_id=1, source_target_pairs={{2,0},{0,2},{3,1},{1,3},{6,4},{4,6},{7,5},{5,7},{10,8},{8,10},{11,... | collective-permute-start | bytes 172040 | tf_op jit(solution)/shard_map/ppermute | solution.py:18
  19.8 1.4 %collective-permute-done.1.refs_2_ = bf16[224,128]{1,0:T(8,128)(2,1)S(1)} collective-permute-done((bf16[224,128]{1,0:T(8,128)(2,1)S(1)}, bf16[224,128]{1,0:T(8,128)(2,1)S(1)}, u32[]{:S(2)}, u32[]{:S(2)}) %collective-permute-start.1) | collective-permute-done | bytes 57376 | tf_op jit(solution)/shard_map/ppermute | solution.py:18
  21.2 2.2 %collective-permute-done.refs_1_ = bf16[224,128]{1,0:T(8,128)(2,1)S(1)} collective-permute-done((bf16[224,128]{1,0:T(8,128)(2,1)S(1)}, bf16[224,128]{1,0:T(8,128)(2,1)S(1)}, u32[]{:S(2)}, u32[]{:S(2)}) %collective-permute-start) | collective-permute-done | bytes 57376 | tf_op jit(solution)/shard_map/ppermute | solution.py:18
  23.4 2.7 %shard_map.85 = (f32[3,2,128,128]{3,2,1,0:T(8,128)S(1)}, bf16[2,512,512]{2,1,0:T(8,128)(2,1)S(1)}) custom-call(s32[3]{0:T(128)S(1)} %copy-done.3, bf16[224,128]{1,0:T(8,128)(2,1)S(1)} %fusion.1.refs_0_, bf16[224,128]{1,0:T(8,128)(2,1)S(1)} %collective-permute-done.refs_1_, bf16[224,128]{1,0:T(8,128)(2,1)S(1)} %collective-permute-done.1.refs_2_, ...), custom_call_target="tpu_custom_call" | custom-call | flops 100000000 | bytes 1048576 | tf_op jit(solution)/shard_map/pallas_call | solution.py:38
  26.2 1.4 %shard_map.86 = (bf16[512,1024]{1,0:T(8,128)(2,1)S(1)}, bf16[128,1024]{1,0:T(8,128)(2,1)S(1)}, f32[8,128]{1,0:T(8,128)S(1)}) custom-call(bf16[2,512,512]{2,1,0:T(8,128)(2,1)S(1)} %get-tuple-element.11.oper_ref, bf16[128,1024]{1,0:T(8,128)(2,1)S(1)} %collective-permute-done.3.next_ref, bf16[128,1024]{1,0:T(8,128)(2,1)S(1)} %bitcast.16, ...), custom_call_target="tpu_custom_call" | custom-call | flops 1000000000 | bytes 1048576 | tf_op jit(solution)/shard_map/pallas_call | solution.py:38
  27.6 4.3 %collective-permute-start.7 = (bf16[128,1024]{1,0:T(8,128)(2,1)S(1)}, bf16[128,1024]{1,0:T(8,128)(2,1)S(1)}, u32[]{:S(2)}, u32[]{:S(2)}) collective-permute-start(bf16[128,1024]{1,0:T(8,128)(2,1)S(1)} %get-tuple-element.12), channel_id=1, source_target_pairs={{4,0},{8,4},{12,8},{0,12},{5,1},{9,5},{13,9},{1,13},{6,2},{10,6},{... | collective-permute-start | bytes 786440 | tf_op jit(solution)/shard_map/ppermute | solution.py:18
  31.8 3.9 %collective-permute-done.7.second_ref = bf16[128,1024]{1,0:T(8,128)(2,1)S(1)} collective-permute-done((bf16[128,1024]{1,0:T(8,128)(2,1)S(1)}, bf16[128,1024]{1,0:T(8,128)(2,1)S(1)}, u32[]{:S(2)}, u32[]{:S(2)}) %collective-permute-start.7) | collective-permute-done | bytes 262176 | tf_op jit(solution)/shard_map/ppermute | solution.py:18
  35.8 1.2 %shard_map.87 = (bf16[128,1024]{1,0:T(8,128)(2,1)}, f32[8,128]{1,0:T(8,128)S(1)}) custom-call(bf16[128,1024]{1,0:T(8,128)(2,1)S(1)} %collective-permute-done.7.second_ref, bf16[512,1024]{1,0:T(8,128)(2,1)S(1)} %get-tuple-element.13.first_ref, f32[8,128]{1,0:T(8,128)S(1)} %get-tuple-element.14.early_ref), custom_call_target="tpu_custom_call" | custom-call | flops 300000000 | bytes 1048576 | tf_op jit(solution)/shard_map/pallas_call | solution.py:38
  36.9 1.5 %collective-permute-start.9 = (f32[8,128]{1,0:T(8,128)S(1)}, f32[8,128]{1,0:T(8,128)S(1)}, u32[]{:S(2)}, u32[]{:S(2)}) collective-permute-start(f32[8,128]{1,0:T(8,128)S(1)} %get-tuple-element.16), channel_id=1, source_target_pairs={{2,0},{3,1},{0,2},{1,3},{6,4},{7,5},{4,6},{5,7},{10,8},{11,9},{8,1... | collective-permute-start | bytes 12296 | tf_op jit(solution)/shard_map/ppermute | solution.py:18
  38.5 1.4 %collective-permute-start.8 = (f32[8,128]{1,0:T(8,128)S(1)}, f32[8,128]{1,0:T(8,128)S(1)}, u32[]{:S(2)}, u32[]{:S(2)}) collective-permute-start(f32[8,128]{1,0:T(8,128)S(1)} %get-tuple-element.16), channel_id=1, source_target_pairs={{1,0},{2,1},{3,2},{0,3},{5,4},{6,5},{7,6},{4,7},{9,8},{10,9},{11,1... | collective-permute-start | bytes 12296 | tf_op jit(solution)/shard_map/ppermute | solution.py:18
  40.0 0.6 %collective-permute-done.9 = f32[8,128]{1,0:T(8,128)S(1)} collective-permute-done((f32[8,128]{1,0:T(8,128)S(1)}, f32[8,128]{1,0:T(8,128)S(1)}, u32[]{:S(2)}, u32[]{:S(2)}) %collective-permute-start.9) | collective-permute-done | bytes 4128 | tf_op jit(solution)/shard_map/ppermute | solution.py:18
  40.6 0.6 %collective-permute-done.8 = f32[8,128]{1,0:T(8,128)S(1)} collective-permute-done((f32[8,128]{1,0:T(8,128)S(1)}, f32[8,128]{1,0:T(8,128)S(1)}, u32[]{:S(2)}, u32[]{:S(2)}) %collective-permute-start.8) | collective-permute-done | bytes 4128 | tf_op jit(solution)/shard_map/ppermute | solution.py:18
  41.2 3.6 %collective-permute-done.11 = f32[8,128]{1,0:T(8,128)S(1)} collective-permute-done((f32[8,128]{1,0:T(8,128)S(1)}, f32[8,128]{1,0:T(8,128)S(1)}, u32[]{:S(2)}, u32[]{:S(2)}) %collective-permute-start.11) | collective-permute-done | bytes 4128 | tf_op jit(solution)/shard_map/ppermute | solution.py:338
  44.8 2.8 %collective-permute-start.12 = (f32[8,128]{1,0:T(8,128)S(1)}, f32[8,128]{1,0:T(8,128)S(1)}, u32[]{:S(2)}, u32[]{:S(2)}) collective-permute-start(f32[8,128]{1,0:T(8,128)S(1)} %add.25.refs_0_), channel_id=1, source_target_pairs={{8,0},{12,4},{0,8},{4,12},{9,1},{13,5},{1,9},{5,13},{10,2},{14,6},... | collective-permute-start | bytes 12296 | tf_op jit(solution)/shard_map/ppermute | solution.py:338
  47.8 0.8 %copy.13 = f32[1,64,3,2,64]{4,3,2,1,0:T(2,128)} copy(f32[1,64,3,2,64]{4,1,3,2,0:T(8,128)S(1)} %dynamic-slice_bitcast_fusion) | data formatting | bytes 196608
  48.6 0.7 %collective-permute-done.12.refs_1_ = f32[8,128]{1,0:T(8,128)S(1)} collective-permute-done((f32[8,128]{1,0:T(8,128)S(1)}, f32[8,128]{1,0:T(8,128)S(1)}, u32[]{:S(2)}, u32[]{:S(2)}) %collective-permute-start.12) | collective-permute-done | bytes 4128 | tf_op jit(solution)/shard_map/ppermute | solution.py:338
  49.4 1.2 %shard_map.88 = f32[2,16]{1,0:T(2,128)} custom-call(s32[4]{0:T(128)S(1)} %copy-done, s32[1,16]{1,0:T(1,128)S(1)} %bitcast.12, f32[8,128]{1,0:T(8,128)S(1)} %add.25.refs_0_, f32[8,128]{1,0:T(8,128)S(1)} %collective-permute-done.12.refs_1_), custom_call_target="tpu_custom_call" | custom-call | flops 100000 | bytes 1048576 | tf_op jit(solution)/shard_map/pallas_call | solution.py:38
  (24 shorter events, 0.9 us)
Async XLA Ops:
  0.6 9.5 %collective-permute-start.5 = (bf16[128,1024]{1,0:T(8,128)(2,1)}, bf16[128,1024]{1,0:T(8,128)(2,1)S(1)}, u32[]{:S(2)}, u32[]{:S(2)}) collective-permute-start(bf16[128,1024]{1,0:T(8,128)(2,1)} %bitcast.13), channel_id=1, source_target_pairs={{2,0},{0,2},{3,1},{1,3},{6,4},{4,6},{7,5},{5,7},{10,8},{8,10},{11,... | collective-permute-start | bytes 786440 | tf_op jit(solution)/shard_map/ppermute | solution.py:18
  3.6 22.5 %collective-permute-start.4 = (bf16[128,1024]{1,0:T(8,128)(2,1)}, bf16[128,1024]{1,0:T(8,128)(2,1)S(1)}, u32[]{:S(2)}, u32[]{:S(2)}) collective-permute-start(bf16[128,1024]{1,0:T(8,128)(2,1)} %bitcast.14), channel_id=1, source_target_pairs={{1,0},{0,1},{3,2},{2,3},{5,4},{4,5},{7,6},{6,7},{9,8},{8,9},{11,10... | collective-permute-start | bytes 786440 | tf_op jit(solution)/shard_map/ppermute | solution.py:18
  3.6 22.5 %collective-permute-start.3 = (bf16[128,1024]{1,0:T(8,128)(2,1)}, bf16[128,1024]{1,0:T(8,128)(2,1)S(1)}, u32[]{:S(2)}, u32[]{:S(2)}) collective-permute-start(bf16[128,1024]{1,0:T(8,128)(2,1)} %bitcast.15), channel_id=1, source_target_pairs={{4,0},{8,4},{12,8},{0,12},{5,1},{9,5},{13,9},{1,13},{6,2},{10,6},{... | collective-permute-start | bytes 786440 | tf_op jit(solution)/shard_map/ppermute | solution.py:18
  10.2 16.0 %collective-permute-start.6 = (bf16[128,1024]{1,0:T(8,128)(2,1)S(1)}, bf16[128,1024]{1,0:T(8,128)(2,1)S(1)}, u32[]{:S(2)}, u32[]{:S(2)}) collective-permute-start(bf16[128,1024]{1,0:T(8,128)(2,1)S(1)} %collective-permute-done.5.refs_2_), channel_id=1, source_target_pairs={{1,0},{0,1},{3,2},{2,3},{5,4},{4,5},{7,6},{6,7},{9,8},{8,9},{11,10... | collective-permute-start | bytes 786440 | tf_op jit(solution)/shard_map/ppermute | solution.py:18
  11.4 0.8 %copy-start.4 = (bf16[1,2,3,8,2,2,128]{6,5,4,3,2,1,0:T(2,128)(2,1)S(1)}, bf16[1,2,3,8,2,2,128]{6,5,4,3,2,1,0:T(2,128)(2,1)}, u32[]{:S(2)}) copy-start(bf16[1,2,3,8,2,2,128]{6,5,4,3,2,1,0:T(2,128)(2,1)} %param.6) | copy-start | bytes 147460
  11.4 12.0 %copy-start.3 = (s32[3]{0:T(128)S(1)}, s32[3]{0:T(128)}, u32[]{:S(2)}) copy-start(s32[3]{0:T(128)} %dirs_ref.1) | copy-start | bytes 40
  11.5 14.7 %copy-start.2 = (bf16[1,128,1024]{2,1,0:T(8,128)(2,1)S(1)}, bf16[1,128,1024]{2,1,0:T(8,128)(2,1)}, u32[]{:S(2)}) copy-start(bf16[1,128,1024]{2,1,0:T(8,128)(2,1)} %param.8) | copy-start | bytes 786436
  12.2 7.1 %collective-permute-start.2 = (bf16[224,128]{1,0:T(8,128)(2,1)S(1)}, bf16[224,128]{1,0:T(8,128)(2,1)S(1)}, u32[]{:S(2)}, u32[]{:S(2)}) collective-permute-start(bf16[224,128]{1,0:T(8,128)(2,1)S(1)} %fusion.1.refs_0_), channel_id=1, source_target_pairs={{6,0},{4,2},{10,4},{8,6},{14,8},{12,10},{2,12},{0,14},{7,1},{5,3},... | collective-permute-start | bytes 172040 | tf_op jit(solution)/shard_map/ppermute | solution.py:28
  17.0 4.2 %collective-permute-start.1 = (bf16[224,128]{1,0:T(8,128)(2,1)S(1)}, bf16[224,128]{1,0:T(8,128)(2,1)S(1)}, u32[]{:S(2)}, u32[]{:S(2)}) collective-permute-start(bf16[224,128]{1,0:T(8,128)(2,1)S(1)} %fusion.1.refs_0_), channel_id=1, source_target_pairs={{4,0},{8,4},{12,8},{0,12},{5,1},{9,5},{13,9},{1,13},{6,2},{10,6},{... | collective-permute-start | bytes 172040 | tf_op jit(solution)/shard_map/ppermute | solution.py:18
  19.2 4.2 %collective-permute-start = (bf16[224,128]{1,0:T(8,128)(2,1)S(1)}, bf16[224,128]{1,0:T(8,128)(2,1)S(1)}, u32[]{:S(2)}, u32[]{:S(2)}) collective-permute-start(bf16[224,128]{1,0:T(8,128)(2,1)S(1)} %fusion.1.refs_0_), channel_id=1, source_target_pairs={{2,0},{0,2},{3,1},{1,3},{6,4},{4,6},{7,5},{5,7},{10,8},{8,10},{11,... | collective-permute-start | bytes 172040 | tf_op jit(solution)/shard_map/ppermute | solution.py:18
  27.6 8.2 %collective-permute-start.7 = (bf16[128,1024]{1,0:T(8,128)(2,1)S(1)}, bf16[128,1024]{1,0:T(8,128)(2,1)S(1)}, u32[]{:S(2)}, u32[]{:S(2)}) collective-permute-start(bf16[128,1024]{1,0:T(8,128)(2,1)S(1)} %get-tuple-element.12), channel_id=1, source_target_pairs={{4,0},{8,4},{12,8},{0,12},{5,1},{9,5},{13,9},{1,13},{6,2},{10,6},{... | collective-permute-start | bytes 786440 | tf_op jit(solution)/shard_map/ppermute | solution.py:18
  36.9 3.0 %collective-permute-start.10 = (f32[8,128]{1,0:T(8,128)S(1)}, f32[8,128]{1,0:T(8,128)S(1)}, u32[]{:S(2)}, u32[]{:S(2)}) collective-permute-start(f32[8,128]{1,0:T(8,128)S(1)} %get-tuple-element.16), channel_id=1, source_target_pairs={{3,0},{0,1},{1,2},{2,3},{7,4},{4,5},{5,6},{6,7},{11,8},{8,9},{9,10... | collective-permute-start | bytes 12296 | tf_op jit(solution)/shard_map/ppermute | solution.py:18
  36.9 3.6 %collective-permute-start.9 = (f32[8,128]{1,0:T(8,128)S(1)}, f32[8,128]{1,0:T(8,128)S(1)}, u32[]{:S(2)}, u32[]{:S(2)}) collective-permute-start(f32[8,128]{1,0:T(8,128)S(1)} %get-tuple-element.16), channel_id=1, source_target_pairs={{2,0},{3,1},{0,2},{1,3},{6,4},{7,5},{4,6},{5,7},{10,8},{11,9},{8,1... | collective-permute-start | bytes 12296 | tf_op jit(solution)/shard_map/ppermute | solution.py:18
  38.5 2.8 %collective-permute-start.8 = (f32[8,128]{1,0:T(8,128)S(1)}, f32[8,128]{1,0:T(8,128)S(1)}, u32[]{:S(2)}, u32[]{:S(2)}) collective-permute-start(f32[8,128]{1,0:T(8,128)S(1)} %get-tuple-element.16), channel_id=1, source_target_pairs={{1,0},{2,1},{3,2},{0,3},{5,4},{6,5},{7,6},{4,7},{9,8},{10,9},{11,1... | collective-permute-start | bytes 12296 | tf_op jit(solution)/shard_map/ppermute | solution.py:18
  41.2 3.6 %collective-permute-start.11 = (f32[8,128]{1,0:T(8,128)S(1)}, f32[8,128]{1,0:T(8,128)S(1)}, u32[]{:S(2)}, u32[]{:S(2)}) collective-permute-start(f32[8,128]{1,0:T(8,128)S(1)} %add_add_fusion), channel_id=1, source_target_pairs={{4,0},{0,4},{12,8},{8,12},{5,1},{1,5},{13,9},{9,13},{6,2},{2,6},{1... | collective-permute-start | bytes 12296 | tf_op jit(solution)/shard_map/ppermute | solution.py:338
  44.8 4.5 %collective-permute-start.12 = (f32[8,128]{1,0:T(8,128)S(1)}, f32[8,128]{1,0:T(8,128)S(1)}, u32[]{:S(2)}, u32[]{:S(2)}) collective-permute-start(f32[8,128]{1,0:T(8,128)S(1)} %add.25.refs_0_), channel_id=1, source_target_pairs={{8,0},{12,4},{0,8},{4,12},{9,1},{13,5},{1,9},{5,13},{10,2},{14,6},... | collective-permute-start | bytes 12296 | tf_op jit(solution)/shard_map/ppermute | solution.py:338
  48.6 0.7 %copy-start = (s32[4]{0:T(128)S(1)}, s32[4]{0:T(128)}, u32[]{:S(2)}) copy-start(s32[4]{0:T(128)} %offsets_ref.1) | copy-start | bytes 52
  48.6 0.7 %copy-start.1 = (s32[16]{0:T(128)S(1)}, s32[16]{0:T(128)}, u32[]{:S(2)}) copy-start(s32[16]{0:T(128)} %param.9) | copy-start | bytes 196

commit v2 on v1

v2 whole, which is shorter than its diff:
```python
import functools
import math

import jax
import jax.numpy as jnp
from jax import lax
from jax.experimental import pallas as pl
from jax.experimental.pallas import tpu as pltpu

from jax.sharding import PartitionSpec as P

F32 = jnp.float32
BF16 = jnp.bfloat16
PIECES = 2


def from_offset(block, axis, distance):
    count = lax.axis_size(axis)
    return lax.ppermute(block, axis, [((i + distance) % count, i) for i in range(count)])


def vmem_call(kernel, out_shape, scratch, flops, smem=()):
    def call(*operands):
        specs = [
            pl.BlockSpec(memory_space=pltpu.SMEM if i in smem else pltpu.VMEM)
            for i in range(len(operands))
        ]
        outs = jax.tree.map(lambda _: pl.BlockSpec(memory_space=pltpu.VMEM), out_shape)
        return pl.pallas_call(
            kernel,
            out_shape=out_shape,
            in_specs=specs,
            out_specs=outs,
            scratch_shapes=scratch,
            compiler_params=pltpu.CompilerParams(vmem_limit_bytes=16 * 1024 * 1024),
            cost_estimate=pl.CostEstimate(
                flops=flops, bytes_accessed=1 << 20, transcendentals=0
            ),
        )(*operands)

    return call


def moved(field, distance):
    rows = field.shape[0]
    return pltpu.roll(field, distance % rows, 0) if distance % rows else field


def ahead_of(field, stride, side):
    row = lax.broadcasted_iota(jnp.int32, field.shape, 0)
    last = (row // stride) % side == side - 1
    return jnp.where(last, moved(field, (side - 1) * stride), moved(field, -stride))


def behind_of(field, stride, side):
    row = lax.broadcasted_iota(jnp.int32, field.shape, 0)
    start = (row // stride) % side == 0
    return jnp.where(start, moved(field, (1 - side) * stride), moved(field, stride))


def elementals_kernel(cells, side, scale, slabs, spins, dirs_ref, rows_ref, *refs):
    slab_refs, out_refs = refs[:slabs], refs[slabs:]
    elem_ref, oper_ref, first_ref, trace_ref, rhs_ref, pick_ref = out_refs
    modes = pick_ref.shape[-1]
    sites = slabs * cells
    fields = [
        jnp.concatenate([ref[k * cells : (k + 1) * cells, :] for ref in slab_refs], axis=0)
        for k in range(6)
    ]
    vectors = jnp.concatenate(fields, axis=0)
    links = jnp.concatenate([ref[6 * cells : 7 * cells, :] for ref in slab_refs], axis=0)
    links = links.astype(F32)
    wide = [field.astype(F32) for field in fields]
    for direction in range(3):
        stride = side**direction
        across = side if direction < 2 else sites // stride
        forward = [ahead_of(field, stride, across) for field in wide]
        terms = [[None] * 3 for _ in range(4)]
        for colour in range(3):
            for other in range(3):
                at = direction * 18 + colour * 3 + other
                link_real = links[:, at : at + 1]
                link_imag = links[:, at + 9 : at + 10]
                ahead_real, ahead_imag = forward[other], forward[3 + other]
                here_real, here_imag = wide[colour], wide[3 + colour]
                for kind, to, term in (
                    (0, colour, link_real * ahead_real - link_imag * ahead_imag),
                    (1, colour, link_real * ahead_imag + link_imag * ahead_real),
                    (2, other, link_real * here_real + link_imag * here_imag),
                    (3, other, link_real * here_imag - link_imag * here_real),
                ):
                    held = terms[kind][to]
                    terms[kind][to] = term if held is None else held + term
        left, right = 2 * direction * modes, (2 * direction + 1) * modes
        for colour in range(3):
            parts = []
            for kind in range(2):
                adjoint = terms[2 + kind][colour].astype(BF16).astype(F32)
                parts.append(terms[kind][colour] - behind_of(adjoint, stride, across))
            real_part, imag_part = parts[0], parts[1]
            low, high = colour * sites, (3 + colour) * sites
            rhs_ref[low : low + sites, left : left + modes] = real_part.astype(BF16)
            rhs_ref[high : high + sites, left : left + modes] = imag_part.astype(BF16)
            rhs_ref[low : low + sites, right : right + modes] = imag_part.astype(BF16)
            rhs_ref[high : high + sites, right : right + modes] = (-real_part).astype(BF16)
    product = lax.dot_general(
        vectors, rhs_ref[...], (((0,), (0,)), ((), ())), preferred_element_type=F32
    )
    for direction in range(3):
        left = 2 * direction * modes
        real_part = product[:, left : left + modes] * scale
        imag_part = product[:, left + modes : left + 2 * modes] * scale
        elem_ref[direction, 0] = real_part
        elem_ref[direction, 1] = imag_part
        pick_ref[direction, 0] = real_part.astype(BF16).astype(F32)
        pick_ref[direction, 1] = imag_part.astype(BF16).astype(F32)
    zero_real, zero_imag = pick_ref[dirs_ref[0], 0], pick_ref[dirs_ref[0], 1]
    one_real, one_imag = pick_ref[dirs_ref[1], 0], pick_ref[dirs_ref[1], 1]
    two_real, two_imag = pick_ref[dirs_ref[2], 0], pick_ref[dirs_ref[2], 1]
    sum_real = [[two_real, zero_real + one_imag], [zero_real - one_imag, -two_real]]
    sum_imag = [[two_imag, zero_imag - one_real], [zero_imag + one_real, -two_imag]]
    for p in range(2):
        for q in range(2):
            top, bottom = p * modes, (2 + p) * modes
            left, right = q * modes, (2 + q) * modes
            real_part = sum_real[p][q].astype(BF16)
            imag_part = sum_imag[p][q].astype(BF16)
            oper_ref[top : top + modes, left : left + modes] = -imag_part
            oper_ref[top : top + modes, right : right + modes] = real_part
            oper_ref[bottom : bottom + modes, left : left + modes] = -real_part
            oper_ref[bottom : bottom + modes, right : right + modes] = -imag_part
    count, width = rows_ref.shape
    first_row = own_block(slabs, spins, 0, 0) * count
    product = times_operator(rows_ref[...], oper_ref[...])
    first_ref[...] = product.astype(BF16)
    trace_ref[...] = at_lanes(
        trace_ref.shape,
        [
            (0, diagonal_sum(product[:, : width // 2], first_row)),
            (1, diagonal_sum(product[:, width // 2 :], first_row)),
        ],
    )


def times_operator(rows, operator):
    half = rows.shape[1] // 4
    upper = jnp.concatenate([rows[:, half : 2 * half], rows[:, 3 * half :]], axis=1)
    lower = jnp.concatenate([rows[:, :half], rows[:, 2 * half : 3 * half]], axis=1)
    both = jnp.dot(
        jnp.concatenate([upper, lower], axis=0), operator, preferred_element_type=F32
    )
    scale = 1.0 / math.sqrt(2.0 * half)
    count = rows.shape[0]
    above = both[:count] * scale
    below = both[count:] * (-scale)
    return jnp.concatenate([above[:, :half], below[:, :half], above[:, half:], below[:, half:]], 1)


def times_rows(left, right):
    order = left.shape[1] // 2
    count = left.shape[0]
    both = jnp.dot(
        jnp.concatenate([left[:, :order], left[:, order:]], axis=0),
        right,
        preferred_element_type=F32,
    )
    real_part = both[:count, :order] - both[count:, order:]
    imag_part = both[:count, order:] + both[count:, :order]
    return real_part, imag_part


def diagonal_sum(part, first_row):
    row = lax.broadcasted_iota(jnp.int32, part.shape, 0) + first_row
    column = lax.broadcasted_iota(jnp.int32, part.shape, 1)
    kept = jnp.where(row == column, part, 0.0)
    return jnp.sum(jnp.sum(kept, axis=0, keepdims=True), axis=1, keepdims=True)


def at_lanes(shape, values):
    lane = lax.broadcasted_iota(jnp.int32, shape, 1)
    total = jnp.zeros(shape, F32)
    for at, value in values:
        total = total + jnp.where(lane == at, value, 0.0)
    return total


def own_block(spaces, spins, space_step, spin_step):
    place = lax.rem(lax.axis_index("space") + space_step, spaces)
    spin = lax.rem(lax.axis_index("spin") + spin_step, spins)
    return place * spins + spin


def first_kernel(spaces, spins, oper_ref, own_ref, *refs):
    block_refs, first_ref = refs[:-1], refs[-1]
    count = own_ref.shape[0]
    start = pl.multiple_of(own_block(spaces, spins, 0, 0) * count, count)
    first_ref[pl.ds(start, count), :] = own_ref[...]
    at = 1
    left = list(block_refs)
    while left:
        rows = left.pop(0)[...]
        while rows.shape[0] < count:
            rows = jnp.concatenate([rows, left.pop(0)[...]], axis=0)
        product = times_operator(rows, oper_ref[...])
        start = pl.multiple_of(own_block(spaces, spins, at // spins, at % spins) * count, count)
        first_ref[pl.ds(start, count), :] = product.astype(BF16)
        at += 1


def second_kernel(spaces, spins, next_ref, first_ref, early_ref, second_ref, trace_ref):
    count = next_ref.shape[0]
    order = next_ref.shape[1] // 2
    first_row = own_block(spaces, spins, 0, 0) * count
    real_part, imag_part = times_rows(next_ref[...], first_ref[...])
    second_ref[:, :order] = real_part.astype(BF16)
    second_ref[:, order:] = imag_part.astype(BF16)
    trace_ref[...] = early_ref[...] + at_lanes(
        trace_ref.shape,
        [(2, diagonal_sum(real_part, first_row)), (3, diagonal_sum(imag_part, first_row))],
    )


def third_kernel(spaces, spins, second_ref, first_ref, early_ref, chain_ref, trace_ref):
    count = second_ref.shape[0]
    order = second_ref.shape[1] // 2
    first_row = own_block(spaces, spins, 0, 0) * count
    real_part, imag_part = times_rows(second_ref[...], first_ref[...])
    scale = math.sqrt(order)
    chain_ref[:, :order] = (real_part * scale).astype(BF16)
    chain_ref[:, order:] = (imag_part * scale).astype(BF16)
    late = at_lanes(
        early_ref.shape,
        [(4, diagonal_sum(real_part, first_row)), (5, diagonal_sum(imag_part, first_row))],
    )
    row = lax.broadcasted_iota(jnp.int32, trace_ref.shape, 0)
    values = jnp.broadcast_to((early_ref[...] + late)[0:1], trace_ref.shape)
    trace_ref[...] = jnp.where(row == lax.axis_index("tm"), values, 0.0)


def correlator_kernel(offsets_ref, times_ref, *refs):
    part_refs, out_ref = refs[:-1], refs[-1]
    traces = part_refs[0][...]
    for part_ref in part_refs[1:]:
        traces = traces + part_ref[...]
    lane = lax.broadcasted_iota(jnp.int32, (1, traces.shape[1]), 1)
    counts = jnp.zeros((1, traces.shape[1]), F32)
    for j in range(offsets_ref.shape[0]):
        counts = counts + jnp.where(lane // 2 == offsets_ref[j], 1.0, 0.0)
    weighted = traces * counts
    row = lax.broadcasted_iota(jnp.int32, (traces.shape[0], times_ref.shape[1]), 0)
    chosen = row == times_ref[...]
    for part in range(2):
        keep = (lane % 2 == part) & (lane < 6)
        column = jnp.sum(jnp.where(keep, weighted, 0.0), axis=1, keepdims=True)
        out_ref[part : part + 1, :] = jnp.sum(
            jnp.where(chosen, column, 0.0), axis=0, keepdims=True
        )


def on_device(
    eigenvectors, gauge_links, perambulators, source_times, insert_offsets, derivative_dirs
):
    spaces, spins, slots = lax.axis_size("space"), lax.axis_size("spin"), lax.axis_size("tm")
    planes, side, modes = eigenvectors.shape[3], eigenvectors.shape[4], eigenvectors.shape[6]
    cells = planes * side * side
    own_rows = perambulators[0]
    count, width = own_rows.shape
    order = width // 2

    vectors = eigenvectors.reshape((6 * cells, modes))
    links = gauge_links.reshape((54, cells)).T
    links = jnp.pad(links, ((0, 0), (0, modes - 54)))
    pack = jnp.concatenate([vectors, links], axis=0)
    slabs = [pack] + [from_offset(pack, "space", step) for step in range(1, spaces)]
    far_rows = [from_offset(own_rows, "space", step) for step in range(1, spaces)]

    norm_scale = 1.0 / math.sqrt(6.0 * 4.0 * planes * spaces * side * side)
    rows_shape = jax.ShapeDtypeStruct((count, width), BF16)
    trace_shape = jax.ShapeDtypeStruct((8, 128), F32)
    elements, operator, own_first, early = vmem_call(
        functools.partial(elementals_kernel, cells, side, norm_scale, spaces, spins),
        (
            jax.ShapeDtypeStruct((3, 2, modes, modes), F32),
            jax.ShapeDtypeStruct((4 * modes, 4 * modes), BF16),
            rows_shape,
            trace_shape,
        ),
        [
            pltpu.VMEM((6 * cells * spaces, 6 * modes), BF16),
            pltpu.VMEM((3, 2, modes, modes), F32),
        ],
        10**10,
        smem=(0,),
    )(derivative_dirs, own_rows, *slabs)

    next_first = from_offset(own_first, "tm", 1)

    far_rows, held_first = lax.optimization_barrier((far_rows, own_first))
    blocks = []
    for at, block in enumerate([own_rows] + far_rows):
        blocks += [block]
        pieces = PIECES if at else 1
        for step in range(1, spins):
            for piece in range(pieces):
                low, high = piece * count // pieces, (piece + 1) * count // pieces
                blocks += [from_offset(block[low:high], "spin", step)]
    blocks = blocks[1:]
    first = vmem_call(
        functools.partial(first_kernel, spaces, spins),
        jax.ShapeDtypeStruct((order, width), BF16),
        [],
        10**6,
    )(operator, held_first, *blocks)

    second, early = vmem_call(
        functools.partial(second_kernel, spaces, spins),
        (rows_shape, trace_shape),
        [],
        3 * 10**8,
    )(next_first, first, early)

    next_second = from_offset(second, "tm", 1)

    rows, columns = modes // spaces, modes // spins
    share = lax.dynamic_slice(
        elements,
        (0, 0, lax.axis_index("space") * rows, lax.axis_index("spin") * columns),
        (3, 2, rows, columns),
    )
    elementals = jnp.transpose(share, (2, 0, 1, 3))

    chain, traces = vmem_call(
        functools.partial(third_kernel, spaces, spins),
        (
            jax.ShapeDtypeStruct((count, width), BF16),
            jax.ShapeDtypeStruct((-(-slots // 8) * 8, 128), F32),
        ),
        [],
        3 * 10**8,
    )(next_second, first, early)

    group = spaces * spins
    parts = [traces] + [from_offset(traces, ("space", "spin"), step) for step in range(1, group)]
    traces = functools.reduce(lambda a, b: a + b, parts)
    if slots & (slots - 1):
        parts = [lax.psum(traces, "tm")]
    else:
        step = 1
        while step < slots:
            other = lax.ppermute(traces, "tm", [(i ^ step, i) for i in range(slots)])
            parts = [traces, other]
            traces = traces + other
            step *= 2
    correlator = vmem_call(
        correlator_kernel,
        jax.ShapeDtypeStruct((2, source_times.shape[0]), F32),
        [],
        10**5,
        smem=(0,),
    )(insert_offsets, source_times[None, :], *parts)
    return (elementals[None], chain[None], correlator.T)


def solution(mesh):
    in_specs = (
        P(("cfg", "tm"), None, None, "space", None, None, None),
        P(("cfg", "tm"), None, None, None, None, "space", None),
        P(("cfg", "tm"), ("space", "spin"), None),
        P(),
        P(),
        P(),
    )
    out_specs = (
        P(("cfg", "tm"), "space", None, None, "spin"),
        P(("cfg", "tm"), ("space", "spin"), None),
        P("cfg", None),
    )
    return jax.shard_map(
        on_device, mesh=mesh, in_specs=in_specs, out_specs=out_specs, check_vma=False
    )
```

time: 50.8 us -> 42.2 us (0.83)
  starting transfers between devices: 22.5 us -> 17.8 us
  waiting for transfers between devices: 17.9 us -> 14.9 us
  Pallas kernels: 6.49 us -> 5.56 us
    ppermute x1 -> x0, starting transfers between devices: 4.83 us -> none  [from_diagonal(): return lax.ppermute(block, ('tm', 'space'), route)]
    ppermute x1 -> x0, waiting for transfers between devices: 1.78 us -> none  [from_diagonal(): return lax.ppermute(block, ('tm', 'space'), route)]
    ppermute x10, waiting for transfers between devices: 11.8 us -> 10.6 us  [from_offset(): lax.ppermute(block, axis, [((i + distance) % count, i) for i in range(cou...]
    pallas_call x4 -> x5, Pallas kernels: 6.49 us -> 5.56 us  [call(): pl.pallas_call(kernel, out_shape=out_shape, in_specs=specs, out_specs=out...]
  transfers between devices with their start and end apart: 13 -> 12, of which waited for: 10 -> 11; matrix products, arithmetic and copies ran while one was open for 5% -> 2% of each run, Pallas kernels for 5% -> 6%
where the time goes in v2:
time: 42.2 us; the launch traced here: 42 us
  starting transfers between devices  17.8 us (42%)
  waiting for transfers between devices  14.9 us (35%)
  Pallas kernels  5.56 us (13%)
  local copies, waits for them, and re-layouts  3.04 us (7%)
  between operations  0.7 us (2%)
    ppermute x10, starting transfers between devices, from_offset(): lax.ppermute(block, axis, [((i + distance) % count, i) for i in range(cou...  15 us
    ppermute x10, waiting for transfers between devices, from_offset(): lax.ppermute(block, axis, [((i + distance) % count, i) for i in range(cou...  10.6 us
    pallas_call x5, Pallas kernels, call(): pl.pallas_call(kernel, out_shape=out_shape, in_specs=specs, out_specs=out...  5.56 us
    ppermute x2, waiting for transfers between devices, on_device(): other = lax.ppermute(traces, 'tm', [(i ^ step, i) for i in range(slots)])  4.33 us
    ppermute x2, starting transfers between devices, on_device(): other = lax.ppermute(traces, 'tm', [(i ^ step, i) for i in range(slots)])  2.82 us
    unnamed x12, local copies, waits for them, and re-layouts  2.68 us
  transfers between devices with their start and end apart: 12, of which 11 were waited for; matrix products, arithmetic and copies ran while one was open for 2% of the time, Pallas kernels for 6%

profile of v2, /device:TPU:0, one launch (start us, length us, event | category | flops | bytes accessed | tf_op | source)
XLA Modules:
  0.0 42.0 jit_solution(12681835325139478525)
XLA Ops:
  0.6 1.3 %copy.11 = bf16[1,3,2,3,3,8,4]{6,5,4,3,2,1,0:T(8,128)(2,1)S(1)} copy(bf16[1,3,2,3,3,8,4]{5,6,4,3,2,1,0:T(4,128)(2,1)} %param.7) | data formatting | bytes 6912 | tf_op args[1]
  2.1 0.6 %copy-done.4 = bf16[1,2,3,8,2,2,128]{6,5,4,3,2,1,0:T(2,128)(2,1)S(1)} copy-done((bf16[1,2,3,8,2,2,128]{6,5,4,3,2,1,0:T(2,128)(2,1)S(1)}, bf16[1,2,3,8,2,2,128]{6,5,4,3,2,1,0:T(2,128)(2,1)}, u32[]{:S(2)}) %copy-start.4) | copy-done | bytes 49176
  2.7 3.0 %collective-permute-start = (bf16[224,128]{1,0:T(8,128)(2,1)S(1)}, bf16[224,128]{1,0:T(8,128)(2,1)S(1)}, u32[]{:S(2)}, u32[]{:S(2)}) collective-permute-start(bf16[224,128]{1,0:T(8,128)(2,1)S(1)} %fusion.1.refs_0_), channel_id=1, source_target_pairs={{2,0},{0,2},{3,1},{1,3},{6,4},{4,6},{7,5},{5,7},{10,8},{8,10},{11,... | collective-permute-start | bytes 172040 | tf_op jit(solution)/shard_map/ppermute | solution.py:19
  5.9 2.1 %collective-permute-done.refs_1_ = bf16[224,128]{1,0:T(8,128)(2,1)S(1)} collective-permute-done((bf16[224,128]{1,0:T(8,128)(2,1)S(1)}, bf16[224,128]{1,0:T(8,128)(2,1)S(1)}, u32[]{:S(2)}, u32[]{:S(2)}) %collective-permute-start) | collective-permute-done | bytes 57376 | tf_op jit(solution)/shard_map/ppermute | solution.py:19
  8.0 2.1 %shard_map.85 = (f32[3,2,128,128]{3,2,1,0:T(8,128)S(1)}, bf16[512,512]{1,0:T(8,128)(2,1)S(1)}, bf16[128,1024]{1,0:T(8,128)(2,1)S(1)}, f32[8,128]{1,0:T(8,128)S(1)}) custom-call(s32[3]{0:T(128)S(1)} %copy-done.3, bf16[128,1024]{1,0:T(8,128)(2,1)S(1)} %bitcast.15, bf16[224,128]{1,0:T(8,128)(2,1)S(1)} %fusion.1.refs_0_, ...), custom_call_target="tpu_custom_call" | custom-call | flops 10000000000 | bytes 1048576 | tf_op jit(solution)/shard_map/pallas_call | solution.py:29
  10.1 4.0 %collective-permute-start.1 = (bf16[128,1024]{1,0:T(8,128)(2,1)S(1)}, bf16[128,1024]{1,0:T(8,128)(2,1)S(1)}, u32[]{:S(2)}, u32[]{:S(2)}) collective-permute-start(bf16[128,1024]{1,0:T(8,128)(2,1)S(1)} %get-tuple-element.16.own_ref), channel_id=1, source_target_pairs={{4,0},{8,4},{12,8},{0,12},{5,1},{9,5},{13,9},{1,13},{6,2},{10,6},{... | collective-permute-start | bytes 786440 | tf_op jit(solution)/shard_map/ppermute | solution.py:19
  14.1 0.4 collective-permute-done.2.refs_1_
  14.6 0.5 %collective-permute-start.4 = (bf16[64,1024]{1,0:T(8,128)(2,1)S(1)}, bf16[64,1024]{1,0:T(8,128)(2,1)S(1)}, u32[]{:S(2)}, u32[]{:S(2)}) collective-permute-start(bf16[64,1024]{1,0:T(8,128)(2,1)S(1)} %get-tuple-element.30), channel_id=1, source_target_pairs={{1,0},{0,1},{3,2},{2,3},{5,4},{4,5},{7,6},{6,7},{9,8},{8,9},{11,10... | collective-permute-start | bytes 393224 | tf_op jit(solution)/shard_map/ppermute | solution.py:19
  15.1 0.8 %collective-permute-done.5.refs_3_ = bf16[64,1024]{1,0:T(8,128)(2,1)S(1)} collective-permute-done((bf16[64,1024]{1,0:T(8,128)(2,1)S(1)}, bf16[64,1024]{1,0:T(8,128)(2,1)S(1)}, u32[]{:S(2)}, u32[]{:S(2)}) %collective-permute-start.5) | collective-permute-done | bytes 131104 | tf_op jit(solution)/shard_map/ppermute | solution.py:19
  16.1 0.6 %shard_map.86.first_ref = bf16[512,1024]{1,0:T(8,128)(2,1)S(1)} custom-call(bf16[512,512]{1,0:T(8,128)(2,1)S(1)} %get-tuple-element.15.oper_ref, bf16[128,1024]{1,0:T(8,128)(2,1)S(1)} %get-tuple-element.16.own_ref, bf16[128,1024]{1,0:T(8,128)(2,1)S(1)} %collective-permute-done.3.refs_0_, bf16[128,1024]{1,0:T(8,128)(2,1)S(1)} %collective-permute-done.2.refs_1_, ...), custom_call_target="tpu_custom_call" | custom-call | flops 1000000 | bytes 1048576 | tf_op jit(solution)/shard_map/pallas_call | solution.py:29
  16.7 1.9 %collective-permute-done.1.next_ref = bf16[128,1024]{1,0:T(8,128)(2,1)S(1)} collective-permute-done((bf16[128,1024]{1,0:T(8,128)(2,1)S(1)}, bf16[128,1024]{1,0:T(8,128)(2,1)S(1)}, u32[]{:S(2)}, u32[]{:S(2)}) %collective-permute-start.1) | collective-permute-done | bytes 262176 | tf_op jit(solution)/shard_map/ppermute | solution.py:19
  18.5 0.5 %shard_map.87 = (bf16[128,1024]{1,0:T(8,128)(2,1)S(1)}, f32[8,128]{1,0:T(8,128)S(1)}) custom-call(bf16[128,1024]{1,0:T(8,128)(2,1)S(1)} %collective-permute-done.1.next_ref, bf16[512,1024]{1,0:T(8,128)(2,1)S(1)} %shard_map.86.first_ref, f32[8,128]{1,0:T(8,128)S(1)} %get-tuple-element.18.early_ref), custom_call_target="tpu_custom_call" | custom-call | flops 300000000 | bytes 1048576 | tf_op jit(solution)/shard_map/pallas_call | solution.py:29
  19.0 4.3 %collective-permute-start.6 = (bf16[128,1024]{1,0:T(8,128)(2,1)S(1)}, bf16[128,1024]{1,0:T(8,128)(2,1)S(1)}, u32[]{:S(2)}, u32[]{:S(2)}) collective-permute-start(bf16[128,1024]{1,0:T(8,128)(2,1)S(1)} %get-tuple-element.19), channel_id=1, source_target_pairs={{4,0},{8,4},{12,8},{0,12},{5,1},{9,5},{13,9},{1,13},{6,2},{10,6},{... | collective-permute-start | bytes 786440 | tf_op jit(solution)/shard_map/ppermute | solution.py:19
  23.3 3.9 %collective-permute-done.6.second_ref = bf16[128,1024]{1,0:T(8,128)(2,1)S(1)} collective-permute-done((bf16[128,1024]{1,0:T(8,128)(2,1)S(1)}, bf16[128,1024]{1,0:T(8,128)(2,1)S(1)}, u32[]{:S(2)}, u32[]{:S(2)}) %collective-permute-start.6) | collective-permute-done | bytes 262176 | tf_op jit(solution)/shard_map/ppermute | solution.py:19
  27.2 1.2 %shard_map.88 = (bf16[128,1024]{1,0:T(8,128)(2,1)}, f32[8,128]{1,0:T(8,128)S(1)}) custom-call(bf16[128,1024]{1,0:T(8,128)(2,1)S(1)} %collective-permute-done.6.second_ref, bf16[512,1024]{1,0:T(8,128)(2,1)S(1)} %shard_map.86.first_ref, f32[8,128]{1,0:T(8,128)S(1)} %get-tuple-element.20.early_ref), custom_call_target="tpu_custom_call" | custom-call | flops 300000000 | bytes 1048576 | tf_op jit(solution)/shard_map/pallas_call | solution.py:29
  28.4 1.5 %collective-permute-start.8 = (f32[8,128]{1,0:T(8,128)S(1)}, f32[8,128]{1,0:T(8,128)S(1)}, u32[]{:S(2)}, u32[]{:S(2)}) collective-permute-start(f32[8,128]{1,0:T(8,128)S(1)} %get-tuple-element.22), channel_id=1, source_target_pairs={{2,0},{3,1},{0,2},{1,3},{6,4},{7,5},{4,6},{5,7},{10,8},{11,9},{8,1... | collective-permute-start | bytes 12296 | tf_op jit(solution)/shard_map/ppermute | solution.py:19
  29.9 1.4 %collective-permute-start.7 = (f32[8,128]{1,0:T(8,128)S(1)}, f32[8,128]{1,0:T(8,128)S(1)}, u32[]{:S(2)}, u32[]{:S(2)}) collective-permute-start(f32[8,128]{1,0:T(8,128)S(1)} %get-tuple-element.22), channel_id=1, source_target_pairs={{1,0},{2,1},{3,2},{0,3},{5,4},{6,5},{7,6},{4,7},{9,8},{10,9},{11,1... | collective-permute-start | bytes 12296 | tf_op jit(solution)/shard_map/ppermute | solution.py:19
  31.4 0.6 %collective-permute-done.8 = f32[8,128]{1,0:T(8,128)S(1)} collective-permute-done((f32[8,128]{1,0:T(8,128)S(1)}, f32[8,128]{1,0:T(8,128)S(1)}, u32[]{:S(2)}, u32[]{:S(2)}) %collective-permute-start.8) | collective-permute-done | bytes 4128 | tf_op jit(solution)/shard_map/ppermute | solution.py:19
  32.0 0.7 %collective-permute-done.7 = f32[8,128]{1,0:T(8,128)S(1)} collective-permute-done((f32[8,128]{1,0:T(8,128)S(1)}, f32[8,128]{1,0:T(8,128)S(1)}, u32[]{:S(2)}, u32[]{:S(2)}) %collective-permute-start.7) | collective-permute-done | bytes 4128 | tf_op jit(solution)/shard_map/ppermute | solution.py:19
  32.7 3.6 %collective-permute-done.10 = f32[8,128]{1,0:T(8,128)S(1)} collective-permute-done((f32[8,128]{1,0:T(8,128)S(1)}, f32[8,128]{1,0:T(8,128)S(1)}, u32[]{:S(2)}, u32[]{:S(2)}) %collective-permute-start.10) | collective-permute-done | bytes 4128 | tf_op jit(solution)/shard_map/ppermute | solution.py:350
  36.3 2.8 %collective-permute-start.11 = (f32[8,128]{1,0:T(8,128)S(1)}, f32[8,128]{1,0:T(8,128)S(1)}, u32[]{:S(2)}, u32[]{:S(2)}) collective-permute-start(f32[8,128]{1,0:T(8,128)S(1)} %add.25.refs_0_), channel_id=1, source_target_pairs={{8,0},{12,4},{0,8},{4,12},{9,1},{13,5},{1,9},{5,13},{10,2},{14,6},... | collective-permute-start | bytes 12296 | tf_op jit(solution)/shard_map/ppermute | solution.py:350
  39.3 0.8 %copy.13 = f32[1,64,3,2,64]{4,3,2,1,0:T(2,128)} copy(f32[1,64,3,2,64]{4,1,3,2,0:T(8,128)S(1)} %dynamic-slice_bitcast_fusion) | data formatting | bytes 196608
  40.1 0.7 %collective-permute-done.11.refs_1_ = f32[8,128]{1,0:T(8,128)S(1)} collective-permute-done((f32[8,128]{1,0:T(8,128)S(1)}, f32[8,128]{1,0:T(8,128)S(1)}, u32[]{:S(2)}, u32[]{:S(2)}) %collective-permute-start.11) | collective-permute-done | bytes 4128 | tf_op jit(solution)/shard_map/ppermute | solution.py:350
  40.8 1.2 %shard_map.89 = f32[2,16]{1,0:T(2,128)} custom-call(s32[4]{0:T(128)S(1)} %copy-done, s32[1,16]{1,0:T(1,128)S(1)} %bitcast.12, f32[8,128]{1,0:T(8,128)S(1)} %add.25.refs_0_, f32[8,128]{1,0:T(8,128)S(1)} %collective-permute-done.11.refs_1_), custom_call_target="tpu_custom_call" | custom-call | flops 100000 | bytes 1048576 | tf_op jit(solution)/shard_map/pallas_call | solution.py:29
  (24 shorter events, 0.9 us)
Async XLA Ops:
  0.6 5.1 %copy-start.2 = (bf16[1,128,1024]{2,1,0:T(8,128)(2,1)S(1)}, bf16[1,128,1024]{2,1,0:T(8,128)(2,1)}, u32[]{:S(2)}) copy-start(bf16[1,128,1024]{2,1,0:T(8,128)(2,1)} %param.8) | copy-start | bytes 786436
  1.9 0.8 %copy-start.4 = (bf16[1,2,3,8,2,2,128]{6,5,4,3,2,1,0:T(2,128)(2,1)S(1)}, bf16[1,2,3,8,2,2,128]{6,5,4,3,2,1,0:T(2,128)(2,1)}, u32[]{:S(2)}) copy-start(bf16[1,2,3,8,2,2,128]{6,5,4,3,2,1,0:T(2,128)(2,1)} %param.6) | copy-start | bytes 147460
  2.7 5.3 %copy-start.3 = (s32[3]{0:T(128)S(1)}, s32[3]{0:T(128)}, u32[]{:S(2)}) copy-start(s32[3]{0:T(128)} %dirs_ref.1) | copy-start | bytes 40
  2.7 5.3 %collective-permute-start = (bf16[224,128]{1,0:T(8,128)(2,1)S(1)}, bf16[224,128]{1,0:T(8,128)(2,1)S(1)}, u32[]{:S(2)}, u32[]{:S(2)}) collective-permute-start(bf16[224,128]{1,0:T(8,128)(2,1)S(1)} %fusion.1.refs_0_), channel_id=1, source_target_pairs={{2,0},{0,2},{3,1},{1,3},{6,4},{4,6},{7,5},{5,7},{10,8},{8,10},{11,... | collective-permute-start | bytes 172040 | tf_op jit(solution)/shard_map/ppermute | solution.py:19
  5.7 9.3 %collective-permute-start.3 = (bf16[128,1024]{1,0:T(8,128)(2,1)S(1)}, bf16[128,1024]{1,0:T(8,128)(2,1)S(1)}, u32[]{:S(2)}, u32[]{:S(2)}) collective-permute-start(bf16[128,1024]{1,0:T(8,128)(2,1)S(1)} %bitcast.13), channel_id=1, source_target_pairs={{1,0},{0,1},{3,2},{2,3},{5,4},{4,5},{7,6},{6,7},{9,8},{8,9},{11,10... | collective-permute-start | bytes 786440 | tf_op jit(solution)/shard_map/ppermute | solution.py:19
  5.7 8.7 %collective-permute-start.2 = (bf16[128,1024]{1,0:T(8,128)(2,1)S(1)}, bf16[128,1024]{1,0:T(8,128)(2,1)S(1)}, u32[]{:S(2)}, u32[]{:S(2)}) collective-permute-start(bf16[128,1024]{1,0:T(8,128)(2,1)S(1)} %bitcast.14), channel_id=1, source_target_pairs={{2,0},{0,2},{3,1},{1,3},{6,4},{4,6},{7,5},{5,7},{10,8},{8,10},{11,... | collective-permute-start | bytes 786440 | tf_op jit(solution)/shard_map/ppermute | solution.py:19
  10.1 8.4 %collective-permute-start.1 = (bf16[128,1024]{1,0:T(8,128)(2,1)S(1)}, bf16[128,1024]{1,0:T(8,128)(2,1)S(1)}, u32[]{:S(2)}, u32[]{:S(2)}) collective-permute-start(bf16[128,1024]{1,0:T(8,128)(2,1)S(1)} %get-tuple-element.16.own_ref), channel_id=1, source_target_pairs={{4,0},{8,4},{12,8},{0,12},{5,1},{9,5},{13,9},{1,13},{6,2},{10,6},{... | collective-permute-start | bytes 786440 | tf_op jit(solution)/shard_map/ppermute | solution.py:19
  14.5 1.4 %collective-permute-start.5 = (bf16[64,1024]{1,0:T(8,128)(2,1)S(1)}, bf16[64,1024]{1,0:T(8,128)(2,1)S(1)}, u32[]{:S(2)}, u32[]{:S(2)}) collective-permute-start(bf16[64,1024]{1,0:T(8,128)(2,1)S(1)} %get-tuple-element.29), channel_id=1, source_target_pairs={{1,0},{0,1},{3,2},{2,3},{5,4},{4,5},{7,6},{6,7},{9,8},{8,9},{11,10... | collective-permute-start | bytes 393224 | tf_op jit(solution)/shard_map/ppermute | solution.py:19
  14.6 1.5 %collective-permute-start.4 = (bf16[64,1024]{1,0:T(8,128)(2,1)S(1)}, bf16[64,1024]{1,0:T(8,128)(2,1)S(1)}, u32[]{:S(2)}, u32[]{:S(2)}) collective-permute-start(bf16[64,1024]{1,0:T(8,128)(2,1)S(1)} %get-tuple-element.30), channel_id=1, source_target_pairs={{1,0},{0,1},{3,2},{2,3},{5,4},{4,5},{7,6},{6,7},{9,8},{8,9},{11,10... | collective-permute-start | bytes 393224 | tf_op jit(solution)/shard_map/ppermute | solution.py:19
  19.0 8.2 %collective-permute-start.6 = (bf16[128,1024]{1,0:T(8,128)(2,1)S(1)}, bf16[128,1024]{1,0:T(8,128)(2,1)S(1)}, u32[]{:S(2)}, u32[]{:S(2)}) collective-permute-start(bf16[128,1024]{1,0:T(8,128)(2,1)S(1)} %get-tuple-element.19), channel_id=1, source_target_pairs={{4,0},{8,4},{12,8},{0,12},{5,1},{9,5},{13,9},{1,13},{6,2},{10,6},{... | collective-permute-start | bytes 786440 | tf_op jit(solution)/shard_map/ppermute | solution.py:19
  28.4 3.0 %collective-permute-start.9 = (f32[8,128]{1,0:T(8,128)S(1)}, f32[8,128]{1,0:T(8,128)S(1)}, u32[]{:S(2)}, u32[]{:S(2)}) collective-permute-start(f32[8,128]{1,0:T(8,128)S(1)} %get-tuple-element.22), channel_id=1, source_target_pairs={{3,0},{0,1},{1,2},{2,3},{7,4},{4,5},{5,6},{6,7},{11,8},{8,9},{9,10... | collective-permute-start | bytes 12296 | tf_op jit(solution)/shard_map/ppermute | solution.py:19
  28.4 3.6 %collective-permute-start.8 = (f32[8,128]{1,0:T(8,128)S(1)}, f32[8,128]{1,0:T(8,128)S(1)}, u32[]{:S(2)}, u32[]{:S(2)}) collective-permute-start(f32[8,128]{1,0:T(8,128)S(1)} %get-tuple-element.22), channel_id=1, source_target_pairs={{2,0},{3,1},{0,2},{1,3},{6,4},{7,5},{4,6},{5,7},{10,8},{11,9},{8,1... | collective-permute-start | bytes 12296 | tf_op jit(solution)/shard_map/ppermute | solution.py:19
  29.9 2.8 %collective-permute-start.7 = (f32[8,128]{1,0:T(8,128)S(1)}, f32[8,128]{1,0:T(8,128)S(1)}, u32[]{:S(2)}, u32[]{:S(2)}) collective-permute-start(f32[8,128]{1,0:T(8,128)S(1)} %get-tuple-element.22), channel_id=1, source_target_pairs={{1,0},{2,1},{3,2},{0,3},{5,4},{6,5},{7,6},{4,7},{9,8},{10,9},{11,1... | collective-permute-start | bytes 12296 | tf_op jit(solution)/shard_map/ppermute | solution.py:19
  32.7 3.6 %collective-permute-start.10 = (f32[8,128]{1,0:T(8,128)S(1)}, f32[8,128]{1,0:T(8,128)S(1)}, u32[]{:S(2)}, u32[]{:S(2)}) collective-permute-start(f32[8,128]{1,0:T(8,128)S(1)} %add_add_fusion), channel_id=1, source_target_pairs={{4,0},{0,4},{12,8},{8,12},{5,1},{1,5},{13,9},{9,13},{6,2},{2,6},{1... | collective-permute-start | bytes 12296 | tf_op jit(solution)/shard_map/ppermute | solution.py:350
  36.3 4.5 %collective-permute-start.11 = (f32[8,128]{1,0:T(8,128)S(1)}, f32[8,128]{1,0:T(8,128)S(1)}, u32[]{:S(2)}, u32[]{:S(2)}) collective-permute-start(f32[8,128]{1,0:T(8,128)S(1)} %add.25.refs_0_), channel_id=1, source_target_pairs={{8,0},{12,4},{0,8},{4,12},{9,1},{13,5},{1,9},{5,13},{10,2},{14,6},... | collective-permute-start | bytes 12296 | tf_op jit(solution)/shard_map/ppermute | solution.py:350
  40.1 0.7 %copy-start = (s32[4]{0:T(128)S(1)}, s32[4]{0:T(128)}, u32[]{:S(2)}) copy-start(s32[4]{0:T(128)} %offsets_ref.1) | copy-start | bytes 52
  40.1 0.7 %copy-start.1 = (s32[16]{0:T(128)S(1)}, s32[16]{0:T(128)}, u32[]{:S(2)}) copy-start(s32[16]{0:T(128)} %param.9) | copy-start | bytes 196

commit v3 on v2

--- a/solution.py
+++ b/solution.py
@@ -58,51 +58,121 @@
     return jnp.where(start, moved(field, (1 - side) * stride), moved(field, stride))
 
 
-def elementals_kernel(cells, side, scale, slabs, spins, dirs_ref, rows_ref, *refs):
-    slab_refs, out_refs = refs[:slabs], refs[slabs:]
-    elem_ref, oper_ref, first_ref, trace_ref, rhs_ref, pick_ref = out_refs
-    modes = pick_ref.shape[-1]
+def site_links(links_ref, wide_ref, turned_ref):
+    coefficients, cross, planes = links_ref.shape
+    wide_ref[...] = links_ref[...].astype(F32)
+    for at in range(cross):
+        rows = pl.ds(at, planes, stride=cross)
+        turned_ref[rows, :coefficients] = wide_ref[:, at, :].T
+    return turned_ref[...]
+
+
+def link_at(links, direction, colour, other):
+    at = direction * 18 + colour * 3 + other
+    return links[:, at : at + 1], links[:, at + 9 : at + 10]
+
+
+def added(total, term):
+    return term if total is None else total + term
+
+
+def times_links(links, direction, vectors):
+    parts = [None] * 6
+    for colour in range(3):
+        for other in range(3):
+            real, imag = link_at(links, direction, colour, other)
+            real_part, imag_part = vectors[other], vectors[3 + other]
+            parts[colour] = added(parts[colour], real * real_part - imag * imag_part)
+            parts[3 + colour] = added(parts[3 + colour], real * imag_part + imag * real_part)
+    return parts
+
+
+def times_adjoint(links, direction, vectors):
+    parts = [None] * 6
+    for colour in range(3):
+        for other in range(3):
+            real, imag = link_at(links, direction, colour, other)
+            real_part, imag_part = vectors[colour], vectors[3 + colour]
+            parts[other] = added(parts[other], real * real_part + imag * imag_part)
+            parts[3 + other] = added(parts[3 + other], real * imag_part - imag * real_part)
+    return [part.astype(BF16) for part in parts]
+
+
+def across_slab(links, direction, vectors, side):
+    stride = side**direction
+    forward = times_links(links, direction, [ahead_of(v, stride, side) for v in vectors])
+    adjoint = times_adjoint(links, direction, vectors)
+    return [
+        (part - behind_of(back.astype(F32), stride, side)).astype(BF16)
+        for part, back in zip(forward, adjoint)
+    ]
+
+
+def slab_fields(ref):
+    cells = ref.shape[0] // 6
+    return [ref[k * cells : (k + 1) * cells, :].astype(F32) for k in range(6)]
+
+
+def slab_kernel(side, vectors_ref, links_ref, copy_ref, turned_ref, out_ref, wide_ref):
+    vectors = slab_fields(vectors_ref)
+    links = site_links(links_ref, wide_ref, turned_ref)
+    cells = links.shape[0]
+    copy_ref[...] = vectors_ref[...]
+    parts = across_slab(links, 0, vectors, side) + across_slab(links, 1, vectors, side)
+    parts += times_adjoint(links, 2, vectors)
+    for at, part in enumerate(parts):
+        out_ref[at * cells : (at + 1) * cells, :] = part
+
+
+def elementals_kernel(side, scale, slabs, early_ref, *refs):
+    vector_refs, link_refs, out_refs = refs[:slabs], refs[slabs : 2 * slabs], refs[2 * slabs :]
+    elem_ref, rhs_ref, wide_ref, turned_ref = out_refs
+    modes = elem_ref.shape[-1]
+    cells = link_refs[0].shape[0]
     sites = slabs * cells
-    fields = [
-        jnp.concatenate([ref[k * cells : (k + 1) * cells, :] for ref in slab_refs], axis=0)
-        for k in range(6)
-    ]
-    vectors = jnp.concatenate(fields, axis=0)
-    links = jnp.concatenate([ref[6 * cells : 7 * cells, :] for ref in slab_refs], axis=0)
-    links = links.astype(F32)
-    wide = [field.astype(F32) for field in fields]
-    for direction in range(3):
-        stride = side**direction
-        across = side if direction < 2 else sites // stride
-        forward = [ahead_of(field, stride, across) for field in wide]
-        terms = [[None] * 3 for _ in range(4)]
-        for colour in range(3):
-            for other in range(3):
-                at = direction * 18 + colour * 3 + other
-                link_real = links[:, at : at + 1]
-                link_imag = links[:, at + 9 : at + 10]
-                ahead_real, ahead_imag = forward[other], forward[3 + other]
-                here_real, here_imag = wide[colour], wide[3 + colour]
-                for kind, to, term in (
-                    (0, colour, link_real * ahead_real - link_imag * ahead_imag),
-                    (1, colour, link_real * ahead_imag + link_imag * ahead_real),
-                    (2, other, link_real * here_real + link_imag * here_imag),
-                    (3, other, link_real * here_imag - link_imag * here_real),
-                ):
-                    held = terms[kind][to]
-                    terms[kind][to] = term if held is None else held + term
+
+    def put(slab, direction, parts):
         left, right = 2 * direction * modes, (2 * direction + 1) * modes
         for colour in range(3):
-            parts = []
-            for kind in range(2):
-                adjoint = terms[2 + kind][colour].astype(BF16).astype(F32)
-                parts.append(terms[kind][colour] - behind_of(adjoint, stride, across))
-            real_part, imag_part = parts[0], parts[1]
-            low, high = colour * sites, (3 + colour) * sites
-            rhs_ref[low : low + sites, left : left + modes] = real_part.astype(BF16)
-            rhs_ref[high : high + sites, left : left + modes] = imag_part.astype(BF16)
-            rhs_ref[low : low + sites, right : right + modes] = imag_part.astype(BF16)
-            rhs_ref[high : high + sites, right : right + modes] = (-real_part).astype(BF16)
+            low = colour * sites + slab * cells
+            high = low + 3 * sites
+            real_part, imag_part = parts[colour], parts[3 + colour]
+            rhs_ref[low : low + cells, left : left + modes] = real_part
+            rhs_ref[high : high + cells, left : left + modes] = imag_part
+            rhs_ref[low : low + cells, right : right + modes] = imag_part
+            rhs_ref[high : high + cells, right : right + modes] = -real_part
+
+    early = [early_ref[at * cells : (at + 1) * cells, :] for at in range(18)]
+    put(0, 0, early[:6])
+    put(0, 1, early[6:12])
+    vectors = [slab_fields(ref) for ref in vector_refs]
+    links = [link_refs[0][...]]
+    links += [
+        site_links(ref, wide_ref.at[at], turned_ref.at[at])
+        for at, ref in enumerate(link_refs[1:])
+    ]
+    adjoint = [early[12:]]
+    for slab in range(1, slabs):
+        put(slab, 0, across_slab(links[slab], 0, vectors[slab], side))
+        put(slab, 1, across_slab(links[slab], 1, vectors[slab], side))
+        adjoint.append(times_adjoint(links[slab], 2, vectors[slab]))
+    plane = side * side
+    for slab in range(slabs):
+        after, before = (slab + 1) % slabs, (slab - 1) % slabs
+        ahead = [
+            jnp.concatenate([here[plane:], there[:plane]], axis=0)
+            for here, there in zip(vectors[slab], vectors[after])
+        ]
+        forward = times_links(links[slab], 2, ahead)
+        parts = []
+        for k in range(6):
+            here, there = adjoint[slab][k].astype(F32), adjoint[before][k].astype(F32)
+            behind = jnp.concatenate([there[cells - plane :], here[: cells - plane]], axis=0)
+            parts.append((forward[k] - behind).astype(BF16))
+        put(slab, 2, parts)
+
+    fields = [ref[k * cells : (k + 1) * cells, :] for k in range(6) for ref in vector_refs]
+    vectors = jnp.concatenate(fields, axis=0)
     product = lax.dot_general(
         vectors, rhs_ref[...], (((0,), (0,)), ((), ())), preferred_element_type=F32
     )
@@ -112,11 +182,18 @@
         imag_part = product[:, left + modes : left + 2 * modes] * scale
         elem_ref[direction, 0] = real_part
         elem_ref[direction, 1] = imag_part
-        pick_ref[direction, 0] = real_part.astype(BF16).astype(F32)
-        pick_ref[direction, 1] = imag_part.astype(BF16).astype(F32)
-    zero_real, zero_imag = pick_ref[dirs_ref[0], 0], pick_ref[dirs_ref[0], 1]
-    one_real, one_imag = pick_ref[dirs_ref[1], 0], pick_ref[dirs_ref[1], 1]
-    two_real, two_imag = pick_ref[dirs_ref[2], 0], pick_ref[dirs_ref[2], 1]
+
+
+def operator_kernel(
+    spaces, spins, dirs_ref, elem_ref, rows_ref, oper_ref, first_ref, trace_ref, copy_ref
+):
+    modes = elem_ref.shape[-1]
+    copy_ref[...] = rows_ref[...]
+    picked = []
+    for k in range(3):
+        for part in range(2):
+            picked.append(elem_ref[dirs_ref[k], part].astype(BF16).astype(F32))
+    zero_real, zero_imag, one_real, one_imag, two_real, two_imag = picked
     sum_real = [[two_real, zero_real + one_imag], [zero_real - one_imag, -two_real]]
     sum_imag = [[two_imag, zero_imag - one_real], [zero_imag + one_real, -two_imag]]
     for p in range(2):
@@ -130,7 +207,7 @@
             oper_ref[bottom : bottom + modes, left : left + modes] = -real_part
             oper_ref[bottom : bottom + modes, right : right + modes] = -imag_part
     count, width = rows_ref.shape
-    first_row = own_block(slabs, spins, 0, 0) * count
+    first_row = own_block(spaces, spins, 0, 0) * count
     product = times_operator(rows_ref[...], oper_ref[...])
     first_ref[...] = product.astype(BF16)
     trace_ref[...] = at_lanes(
@@ -220,41 +297,57 @@
     )
 
 
-def third_kernel(spaces, spins, second_ref, first_ref, early_ref, chain_ref, trace_ref):
-    count = second_ref.shape[0]
+def turn_kernel(spaces, spins, offsets_ref, times_ref, first_ref, elem_ref, *refs):
+    out_ref, weights_ref, share_ref, wide_ref = refs
+    count, width = out_ref.shape
+    order, lanes = width // 2, wide_ref.shape[0]
+    first_row = own_block(spaces, spins, 0, 0) * count
+    start = pl.multiple_of(first_row // lanes * lanes, lanes)
+    for part in range(2):
+        block = first_ref[:, pl.ds(pl.multiple_of(start + part * order, lanes), lanes)]
+        wide_ref[:, part * order : (part + 1) * order] = block.astype(F32).T
+    rows = pl.ds(pl.multiple_of(first_row - start, count), count)
+    out_ref[...] = wide_ref[rows, :].astype(BF16)
+    lane = lax.broadcasted_iota(jnp.int32, weights_ref.shape, 1)
+    row = lax.broadcasted_iota(jnp.int32, weights_ref.shape, 0)
+    counts = jnp.zeros(weights_ref.shape, F32)
+    for j in range(offsets_ref.shape[0]):
+        counts = counts + jnp.where(lane // 2 == offsets_ref[j], 1.0, 0.0)
+    counts = jnp.where((lane < 6) & (lane % 2 == row), counts, 0.0)
+    weights_ref[...] = counts
+    here = jnp.where(times_ref[...] == lax.axis_index("tm"), 1.0, 0.0)
+    weights_ref[2:3, : here.shape[1]] = here
+    rows, columns = share_ref.shape[0], share_ref.shape[3]
+    modes = elem_ref.shape[3]
+    top = pl.multiple_of(lax.axis_index("space") * rows, rows)
+    turn = lax.rem(modes - lax.axis_index("spin") * columns, modes)
+    for direction in range(3):
+        for part in range(2):
+            block = elem_ref[direction, part, pl.ds(top, rows), :]
+            share_ref[:, direction, part, :] = pltpu.roll(block, turn, 1)[:, :columns]
+
+
+def whole_sum(values):
+    return jnp.sum(jnp.sum(values, axis=0, keepdims=True), axis=1, keepdims=True)
+
+
+def share_kernel(weights_ref, second_ref, turned_ref, early_ref, out_ref):
     order = second_ref.shape[1] // 2
-    first_row = own_block(spaces, spins, 0, 0) * count
+    left_real, left_imag = second_ref[:, :order].astype(F32), second_ref[:, order:].astype(F32)
+    right_real, right_imag = turned_ref[:, :order].astype(F32), turned_ref[:, order:].astype(F32)
+    real_part = whole_sum(left_real * right_real - left_imag * right_imag)
+    imag_part = whole_sum(left_real * right_imag + left_imag * right_real)
+    traces = early_ref[0:1, :] + at_lanes((1, 128), [(4, real_part), (5, imag_part)])
+    values = jnp.sum(traces * weights_ref[0:2, :], axis=1, keepdims=True)
+    out_ref[...] = values * weights_ref[2:3, : out_ref.shape[1]]
+
+
+def third_kernel(second_ref, first_ref, chain_ref):
+    order = second_ref.shape[1] // 2
     real_part, imag_part = times_rows(second_ref[...], first_ref[...])
     scale = math.sqrt(order)
     chain_ref[:, :order] = (real_part * scale).astype(BF16)
     chain_ref[:, order:] = (imag_part * scale).astype(BF16)
-    late = at_lanes(
-        early_ref.shape,
-        [(4, diagonal_sum(real_part, first_row)), (5, diagonal_sum(imag_part, first_row))],
-    )
-    row = lax.broadcasted_iota(jnp.int32, trace_ref.shape, 0)
-    values = jnp.broadcast_to((early_ref[...] + late)[0:1], trace_ref.shape)
-    trace_ref[...] = jnp.where(row == lax.axis_index("tm"), values, 0.0)
-
-
-def correlator_kernel(offsets_ref, times_ref, *refs):
-    part_refs, out_ref = refs[:-1], refs[-1]
-    traces = part_refs[0][...]
-    for part_ref in part_refs[1:]:
-        traces = traces + part_ref[...]
-    lane = lax.broadcasted_iota(jnp.int32, (1, traces.shape[1]), 1)
-    counts = jnp.zeros((1, traces.shape[1]), F32)
-    for j in range(offsets_ref.shape[0]):
-        counts = counts + jnp.where(lane // 2 == offsets_ref[j], 1.0, 0.0)
-    weighted = traces * counts
-    row = lax.broadcasted_iota(jnp.int32, (traces.shape[0], times_ref.shape[1]), 0)
-    chosen = row == times_ref[...]
-    for part in range(2):
-        keep = (lane % 2 == part) & (lane < 6)
-        column = jnp.sum(jnp.where(keep, weighted, 0.0), axis=1, keepdims=True)
-        out_ref[part : part + 1, :] = jnp.sum(
-            jnp.where(chosen, column, 0.0), axis=0, keepdims=True
-        )
 
 
 def on_device(
@@ -267,37 +360,53 @@
     count, width = own_rows.shape
     order = width // 2
 
-    vectors = eigenvectors.reshape((6 * cells, modes))
-    links = gauge_links.reshape((54, cells)).T
-    links = jnp.pad(links, ((0, 0), (0, modes - 54)))
-    pack = jnp.concatenate([vectors, links], axis=0)
-    slabs = [pack] + [from_offset(pack, "space", step) for step in range(1, spaces)]
+    field = eigenvectors.reshape((6 * cells, modes))
+    fields = [field] + [from_offset(field, "space", step) for step in range(1, spaces)]
+    link = jnp.swapaxes(gauge_links.reshape((54, planes, side * side)), 1, 2)
+    links = [link] + [from_offset(link, "space", step) for step in range(1, spaces)]
     far_rows = [from_offset(own_rows, "space", step) for step in range(1, spaces)]
+    fields[0], links[0], own_slab = vmem_call(
+        functools.partial(slab_kernel, side),
+        (
+            jax.ShapeDtypeStruct(field.shape, BF16),
+            jax.ShapeDtypeStruct((cells, modes), F32),
+            jax.ShapeDtypeStruct((18 * cells, modes), BF16),
+        ),
+        [pltpu.VMEM(link.shape, F32)],
+        10**6,
+    )(field, link)
 
     norm_scale = 1.0 / math.sqrt(6.0 * 4.0 * planes * spaces * side * side)
     rows_shape = jax.ShapeDtypeStruct((count, width), BF16)
     trace_shape = jax.ShapeDtypeStruct((8, 128), F32)
-    elements, operator, own_first, early = vmem_call(
-        functools.partial(elementals_kernel, cells, side, norm_scale, spaces, spins),
+    elements = vmem_call(
+        functools.partial(elementals_kernel, side, norm_scale, spaces),
+        jax.ShapeDtypeStruct((3, 2, modes, modes), F32),
+        [
+            pltpu.VMEM((6 * cells * spaces, 6 * modes), BF16),
+            pltpu.VMEM((spaces - 1,) + link.shape, F32),
+            pltpu.VMEM((spaces - 1, cells, modes), F32),
+        ],
+        10**10,
+    )(own_slab, *fields, *links)
+    operator, own_first, early, rows_copy = vmem_call(
+        functools.partial(operator_kernel, spaces, spins),
         (
-            jax.ShapeDtypeStruct((3, 2, modes, modes), F32),
             jax.ShapeDtypeStruct((4 * modes, 4 * modes), BF16),
             rows_shape,
             trace_shape,
+            rows_shape,
         ),
-        [
-            pltpu.VMEM((6 * cells * spaces, 6 * modes), BF16),
-            pltpu.VMEM((3, 2, modes, modes), F32),
-        ],
-        10**10,
+        [],
+        10**8,
         smem=(0,),
-    )(derivative_dirs, own_rows, *slabs)
+    )(derivative_dirs, elements, own_rows)
 
     next_first = from_offset(own_first, "tm", 1)
 
-    far_rows, held_first = lax.optimization_barrier((far_rows, own_first))
+    far_rows, held_rows, held_first = lax.optimization_barrier((far_rows, rows_copy, own_first))
     blocks = []
-    for at, block in enumerate([own_rows] + far_rows):
+    for at, block in enumerate([held_rows] + far_rows):
         blocks += [block]
         pieces = PIECES if at else 1
         for step in range(1, spins):
@@ -321,44 +430,37 @@
 
     next_second = from_offset(second, "tm", 1)
 
-    rows, columns = modes // spaces, modes // spins
-    share = lax.dynamic_slice(
-        elements,
-        (0, 0, lax.axis_index("space") * rows, lax.axis_index("spin") * columns),
-        (3, 2, rows, columns),
-    )
-    elementals = jnp.transpose(share, (2, 0, 1, 3))
-
-    chain, traces = vmem_call(
-        functools.partial(third_kernel, spaces, spins),
+    turned, weights, elementals = vmem_call(
+        functools.partial(turn_kernel, spaces, spins),
         (
-            jax.ShapeDtypeStruct((count, width), BF16),
-            jax.ShapeDtypeStruct((-(-slots // 8) * 8, 128), F32),
+            rows_shape,
+            trace_shape,
+            jax.ShapeDtypeStruct((modes // spaces, 3, 2, modes // spins), F32),
         ),
+        [pltpu.VMEM((max(count, 128), width), F32)],
+        10**6,
+        smem=(0,),
+    )(insert_offsets, source_times[None, :], first, elements)
+    shares = vmem_call(
+        share_kernel,
+        jax.ShapeDtypeStruct((2, source_times.shape[0]), F32),
         [],
-        3 * 10**8,
-    )(next_second, first, early)
+        10**6,
+    )(weights, next_second, turned, early)
+    chain = vmem_call(third_kernel, rows_shape, [], 10**8)(next_second, first)
 
     group = spaces * spins
-    parts = [traces] + [from_offset(traces, ("space", "spin"), step) for step in range(1, group)]
-    traces = functools.reduce(lambda a, b: a + b, parts)
+    parts = [shares] + [from_offset(shares, ("space", "spin"), step) for step in range(1, group)]
+    shares = functools.reduce(lambda a, b: a + b, parts)
+    shares, chain = lax.optimization_barrier((shares, chain))
     if slots & (slots - 1):
-        parts = [lax.psum(traces, "tm")]
+        shares = lax.psum(shares, "tm")
     else:
         step = 1
         while step < slots:
-            other = lax.ppermute(traces, "tm", [(i ^ step, i) for i in range(slots)])
-            parts = [traces, other]
-            traces = traces + other
+            shares = shares + lax.ppermute(shares, "tm", [(i ^ step, i) for i in range(slots)])
             step *= 2
-    correlator = vmem_call(
-        correlator_kernel,
-        jax.ShapeDtypeStruct((2, source_times.shape[0]), F32),
-        [],
-        10**5,
-        smem=(0,),
-    )(insert_offsets, source_times[None, :], *parts)
-    return (elementals[None], chain[None], correlator.T)
+    return (elementals[None], chain[None], shares.T)
 
 
 def solution(mesh):

time: 42.2 us -> 40 us (0.948)
  waiting for transfers between devices: 14.9 us -> 11.7 us
  local copies, waits for them, and re-layouts: 3.04 us -> 1.64 us
  Pallas kernels: 5.56 us -> 6.72 us
  starting transfers between devices: 17.8 us -> 18.4 us
  other arithmetic: 0.02 us -> 0.57 us
    ppermute x10 -> x11, waiting for transfers between devices: 10.6 us -> 6.53 us  [from_offset(): lax.ppermute(block, axis, [((i + distance) % count, i) for i in range(cou...]
    pallas_call x5 -> x8, Pallas kernels: 5.56 us -> 6.72 us  [call(): pl.pallas_call(kernel, out_shape=out_shape, in_specs=specs, out_specs=out...]
    unnamed x12, local copies, waits for them, and re-layouts: 2.68 us -> 1.63 us
    ppermute x2, waiting for transfers between devices: 4.33 us -> 5.2 us  [on_device(): lax.ppermute(shares, 'tm', [(i ^ step, i) for i in range(slots)])]
    transpose x0 -> x1, other arithmetic: none -> 0.56 us  [on_device(): return (elementals[None], chain[None], shares.T)]
    ppermute x10 -> x11, starting transfers between devices: 15 us -> 15.5 us  [from_offset(): lax.ppermute(block, axis, [((i + distance) % count, i) for i in range(cou...]
  transfers between devices with their start and end apart: 12 -> 13, of which waited for: 11 -> 8; matrix products, arithmetic and copies ran while one was open for 2% -> 0% of each run, Pallas kernels for 6% -> 15%
where the time goes in v3:
time: 40 us; the launch traced here: 39.8 us
  starting transfers between devices  18.4 us (46%)
  waiting for transfers between devices  11.7 us (29%)
  Pallas kernels  6.72 us (17%)
  local copies, waits for them, and re-layouts  1.64 us (4%)
  between operations  0.7 us (2%)
  other arithmetic  0.57 us (1%)
    ppermute x11, starting transfers between devices, from_offset(): lax.ppermute(block, axis, [((i + distance) % count, i) for i in range(cou...  15.5 us
    pallas_call x8, Pallas kernels, call(): pl.pallas_call(kernel, out_shape=out_shape, in_specs=specs, out_specs=out...  6.72 us
    ppermute x11, waiting for transfers between devices, from_offset(): lax.ppermute(block, axis, [((i + distance) % count, i) for i in range(cou...  6.53 us
    ppermute x2, waiting for transfers between devices, on_device(): lax.ppermute(shares, 'tm', [(i ^ step, i) for i in range(slots)])  5.2 us
    ppermute x2, starting transfers between devices, on_device(): lax.ppermute(shares, 'tm', [(i ^ step, i) for i in range(slots)])  2.89 us
    unnamed x12, local copies, waits for them, and re-layouts  1.63 us
  transfers between devices with their start and end apart: 13, of which 8 were waited for; matrix products, arithmetic and copies ran while one was open for 0% of the time, Pallas kernels for 15%

profile of v3, /device:TPU:0, one launch (start us, length us, event | category | flops | bytes accessed | tf_op | source)
XLA Modules:
  0.0 39.8 jit_solution(18059143135096542958)
XLA Ops:
  0.6 3.0 %collective-permute-start = (bf16[192,128]{1,0:T(8,128)(2,1)}, bf16[192,128]{1,0:T(8,128)(2,1)S(1)}, u32[]{:S(2)}, u32[]{:S(2)}) collective-permute-start(bf16[192,128]{1,0:T(8,128)(2,1)} %bitcast.14), channel_id=1, source_target_pairs={{2,0},{0,2},{3,1},{1,3},{6,4},{4,6},{7,5},{5,7},{10,8},{8,10},{11,... | collective-permute-start | bytes 147464 | tf_op jit(solution)/shard_map/ppermute | solution.py:19
  3.7 1.9 %collective-permute-start.2 = (bf16[128,1024]{1,0:T(8,128)(2,1)}, bf16[128,1024]{1,0:T(8,128)(2,1)S(1)}, u32[]{:S(2)}, u32[]{:S(2)}) collective-permute-start(bf16[128,1024]{1,0:T(8,128)(2,1)} %bitcast.10), channel_id=1, source_target_pairs={{2,0},{0,2},{3,1},{1,3},{6,4},{4,6},{7,5},{5,7},{10,8},{8,10},{11,... | collective-permute-start | bytes 786440 | tf_op jit(solution)/shard_map/ppermute | solution.py:19
  5.7 0.8 %copy-done.1 = bf16[1,3,2,3,3,8,4]{5,6,4,3,2,1,0:T(4,128)(2,1)S(1)} copy-done((bf16[1,3,2,3,3,8,4]{5,6,4,3,2,1,0:T(4,128)(2,1)S(1)}, bf16[1,3,2,3,3,8,4]{5,6,4,3,2,1,0:T(4,128)(2,1)}, u32[]{:S(2)}) %copy-start.1) | copy-done | bytes 3480
  6.5 0.8 %copy-done.2 = bf16[1,2,3,8,2,2,128]{6,5,4,3,2,1,0:T(2,128)(2,1)S(1)} copy-done((bf16[1,2,3,8,2,2,128]{6,5,4,3,2,1,0:T(2,128)(2,1)S(1)}, bf16[1,2,3,8,2,2,128]{6,5,4,3,2,1,0:T(2,128)(2,1)}, u32[]{:S(2)}) %copy-start.2) | copy-done | bytes 49176
  7.3 0.6 %shard_map.85 = (bf16[192,128]{1,0:T(8,128)(2,1)S(1)}, f32[32,128]{1,0:T(8,128)S(1)}, bf16[576,128]{1,0:T(8,128)(2,1)S(1)}) custom-call(bf16[192,128]{1,0:T(8,128)(2,1)S(1)} %bitcast.15, bf16[54,4,8]{2,1,0:T(4,128)(2,1)S(1)} %bitcast.13), custom_call_target="tpu_custom_call" | custom-call | flops 1000000 | bytes 1048576 | tf_op jit(solution)/shard_map/pallas_call | solution.py:29
  7.8 0.8 %collective-permute-done.1.refs_3_ = bf16[54,4,8]{2,1,0:T(4,128)(2,1)S(1)} collective-permute-done((bf16[54,4,8]{2,1,0:T(4,128)(2,1)}, bf16[54,4,8]{2,1,0:T(4,128)(2,1)S(1)}, u32[]{:S(2)}, u32[]{:S(2)}) %collective-permute-start.1) | collective-permute-done | bytes 3488 | tf_op jit(solution)/shard_map/ppermute | solution.py:19
  8.7 1.0 %shard_map.86.elem_ref = f32[3,2,128,128]{3,2,1,0:T(8,128)S(1)} custom-call(bf16[576,128]{1,0:T(8,128)(2,1)S(1)} %get-tuple-element.20.early_ref, bf16[192,128]{1,0:T(8,128)(2,1)S(1)} %get-tuple-element.21.refs_0_, bf16[192,128]{1,0:T(8,128)(2,1)S(1)} %collective-permute-done.refs_1_, f32[32,128]{1,0:T(8,128)S(1)} %get-tuple-element.22.refs_2_, ...), custom_call_target="tpu_custom_call" | custom-call | flops 10000000000 | bytes 1048576 | tf_op jit(solution)/shard_map/pallas_call | solution.py:29
  9.7 1.0 %shard_map.87 = (bf16[512,512]{1,0:T(8,128)(2,1)S(1)}, bf16[128,1024]{1,0:T(8,128)(2,1)S(1)}, f32[8,128]{1,0:T(8,128)S(1)}, bf16[128,1024]{1,0:T(8,128)(2,1)S(1)}) custom-call(s32[3]{0:T(128)S(1)} %copy-done.5, f32[3,2,128,128]{3,2,1,0:T(8,128)S(1)} %shard_map.86.elem_ref, bf16[128,1024]{1,0:T(8,128)(2,1)S(1)} %bitcast.11), custom_call_target="tpu_custom_call" | custom-call | flops 100000000 | bytes 1048576 | tf_op jit(solution)/shard_map/pallas_call | solution.py:29
  10.7 3.6 %collective-permute-start.6 = (bf16[128,1024]{1,0:T(8,128)(2,1)S(1)}, bf16[128,1024]{1,0:T(8,128)(2,1)S(1)}, u32[]{:S(2)}, u32[]{:S(2)}) collective-permute-start(bf16[128,1024]{1,0:T(8,128)(2,1)S(1)} %get-tuple-element.26.own_ref), channel_id=1, source_target_pairs={{4,0},{8,4},{12,8},{0,12},{5,1},{9,5},{13,9},{1,13},{6,2},{10,6},{... | collective-permute-start | bytes 786440 | tf_op jit(solution)/shard_map/ppermute | solution.py:19
  14.3 0.6 %collective-permute-start.5 = (bf16[64,1024]{1,0:T(8,128)(2,1)S(1)}, bf16[64,1024]{1,0:T(8,128)(2,1)S(1)}, u32[]{:S(2)}, u32[]{:S(2)}) collective-permute-start(bf16[64,1024]{1,0:T(8,128)(2,1)S(1)} %get-tuple-element.37), channel_id=1, source_target_pairs={{1,0},{0,1},{3,2},{2,3},{5,4},{4,5},{7,6},{6,7},{9,8},{8,9},{11,10... | collective-permute-start | bytes 393224 | tf_op jit(solution)/shard_map/ppermute | solution.py:19
  15.0 1.0 %collective-permute-done.5.refs_3_ = bf16[64,1024]{1,0:T(8,128)(2,1)S(1)} collective-permute-done((bf16[64,1024]{1,0:T(8,128)(2,1)S(1)}, bf16[64,1024]{1,0:T(8,128)(2,1)S(1)}, u32[]{:S(2)}, u32[]{:S(2)}) %collective-permute-start.5) | collective-permute-done | bytes 131104 | tf_op jit(solution)/shard_map/ppermute | solution.py:19
  16.2 0.6 %shard_map.88.first_ref = bf16[512,1024]{1,0:T(8,128)(2,1)S(1)} custom-call(bf16[512,512]{1,0:T(8,128)(2,1)S(1)} %get-tuple-element.23.oper_ref, bf16[128,1024]{1,0:T(8,128)(2,1)S(1)} %get-tuple-element.26.own_ref, bf16[128,1024]{1,0:T(8,128)(2,1)S(1)} %collective-permute-done.3.refs_0_, bf16[128,1024]{1,0:T(8,128)(2,1)S(1)} %collective-permute-done.2.refs_1_, ...), custom_call_target="tpu_custom_call" | custom-call | flops 1000000 | bytes 1048576 | tf_op jit(solution)/shard_map/pallas_call | solution.py:29
  16.8 1.5 %collective-permute-done.6.next_ref = bf16[128,1024]{1,0:T(8,128)(2,1)S(1)} collective-permute-done((bf16[128,1024]{1,0:T(8,128)(2,1)S(1)}, bf16[128,1024]{1,0:T(8,128)(2,1)S(1)}, u32[]{:S(2)}, u32[]{:S(2)}) %collective-permute-start.6) | collective-permute-done | bytes 262176 | tf_op jit(solution)/shard_map/ppermute | solution.py:19
  18.4 0.5 %shard_map.90 = (bf16[128,1024]{1,0:T(8,128)(2,1)S(1)}, f32[8,128]{1,0:T(8,128)S(1)}) custom-call(bf16[128,1024]{1,0:T(8,128)(2,1)S(1)} %collective-permute-done.6.next_ref, bf16[512,1024]{1,0:T(8,128)(2,1)S(1)} %shard_map.88.first_ref, f32[8,128]{1,0:T(8,128)S(1)} %get-tuple-element.31.early_ref), custom_call_target="tpu_custom_call" | custom-call | flops 300000000 | bytes 1048576 | tf_op jit(solution)/shard_map/pallas_call | solution.py:29
  18.9 4.3 %collective-permute-start.7 = (bf16[128,1024]{1,0:T(8,128)(2,1)S(1)}, bf16[128,1024]{1,0:T(8,128)(2,1)S(1)}, u32[]{:S(2)}, u32[]{:S(2)}) collective-permute-start(bf16[128,1024]{1,0:T(8,128)(2,1)S(1)} %get-tuple-element.32), channel_id=1, source_target_pairs={{4,0},{8,4},{12,8},{0,12},{5,1},{9,5},{13,9},{1,13},{6,2},{10,6},{... | collective-permute-start | bytes 786440 | tf_op jit(solution)/shard_map/ppermute | solution.py:19
  23.2 1.5 %shard_map.89 = (bf16[128,1024]{1,0:T(8,128)(2,1)S(1)}, f32[8,128]{1,0:T(8,128)S(1)}, f32[64,3,2,64]{3,2,1,0:T(2,128)}) custom-call(s32[4]{0:T(128)S(1)} %copy-done.3, s32[1,16]{1,0:T(1,128)S(1)} %bitcast.16, bf16[512,1024]{1,0:T(8,128)(2,1)S(1)} %shard_map.88.first_ref, f32[3,2,128,128]{3,2,1,0:T(8,128)S(1)} %shard_map.86.elem_ref), custom_call_target="tpu_custom_call" | custom-call | flops 1000000 | bytes 1048576 | tf_op jit(solution)/shard_map/pallas_call | solution.py:29
  24.7 2.4 %collective-permute-done.7.second_ref = bf16[128,1024]{1,0:T(8,128)(2,1)S(1)} collective-permute-done((bf16[128,1024]{1,0:T(8,128)(2,1)S(1)}, bf16[128,1024]{1,0:T(8,128)(2,1)S(1)}, u32[]{:S(2)}, u32[]{:S(2)}) %collective-permute-start.7) | collective-permute-done | bytes 262176 | tf_op jit(solution)/shard_map/ppermute | solution.py:19
  28.0 1.4 %collective-permute-start.8 = (f32[2,16]{1,0:T(2,128)S(1)}, f32[2,16]{1,0:T(2,128)S(1)}, u32[]{:S(2)}, u32[]{:S(2)}) collective-permute-start(f32[2,16]{1,0:T(2,128)S(1)} %shard_map.91), channel_id=1, source_target_pairs={{1,0},{2,1},{3,2},{0,3},{5,4},{6,5},{7,6},{4,7},{9,8},{10,9},{11,1... | collective-permute-start | bytes 392 | tf_op jit(solution)/shard_map/ppermute | solution.py:19
  29.4 1.1 %shard_map.92 = bf16[128,1024]{1,0:T(8,128)(2,1)} custom-call(bf16[128,1024]{1,0:T(8,128)(2,1)S(1)} %collective-permute-done.7.second_ref, bf16[512,1024]{1,0:T(8,128)(2,1)S(1)} %shard_map.88.first_ref), custom_call_target="tpu_custom_call" | custom-call | flops 100000000 | bytes 1048576 | tf_op jit(solution)/shard_map/pallas_call | solution.py:29
  30.6 0.5 %collective-permute-done.9 = f32[2,16]{1,0:T(2,128)S(1)} collective-permute-done((f32[2,16]{1,0:T(2,128)S(1)}, f32[2,16]{1,0:T(2,128)S(1)}, u32[]{:S(2)}, u32[]{:S(2)}) %collective-permute-start.9) | collective-permute-done | bytes 160 | tf_op jit(solution)/shard_map/ppermute | solution.py:19
  31.2 3.6 %collective-permute-done.11 = f32[2,16]{1,0:T(2,128)S(1)} collective-permute-done((f32[2,16]{1,0:T(2,128)S(1)}, f32[2,16]{1,0:T(2,128)S(1)}, u32[]{:S(2)}, u32[]{:S(2)}) %collective-permute-start.11) | collective-permute-done | bytes 160 | tf_op jit(solution)/shard_map/ppermute | solution.py:461
  34.7 2.8 %collective-permute-start.12 = (f32[2,16]{1,0:T(2,128)S(1)}, f32[2,16]{1,0:T(2,128)S(1)}, u32[]{:S(2)}, u32[]{:S(2)}) collective-permute-start(f32[2,16]{1,0:T(2,128)S(1)} %add.18), channel_id=1, source_target_pairs={{8,0},{12,4},{0,8},{4,12},{9,1},{13,5},{1,9},{5,13},{10,2},{14,6},... | collective-permute-start | bytes 392 | tf_op jit(solution)/shard_map/ppermute | solution.py:461
  37.6 1.6 %collective-permute-done.12 = f32[2,16]{1,0:T(2,128)S(1)} collective-permute-done((f32[2,16]{1,0:T(2,128)S(1)}, f32[2,16]{1,0:T(2,128)S(1)}, u32[]{:S(2)}, u32[]{:S(2)}) %collective-permute-start.12) | collective-permute-done | bytes 160 | tf_op jit(solution)/shard_map/ppermute | solution.py:461
  39.2 0.6 %add_bitcast_fusion = f32[16,2]{0,1:T(2,128)} fusion(f32[2,16]{1,0:T(2,128)S(1)} %add.18, f32[2,16]{1,0:T(2,128)S(1)} %collective-permute-done.12), kind=kLoop, calls=%fused_computation | loop fusion | flops 32 | bytes 384 | tf_op jit(solution)/shard_map/transpose | solution.py:463
  (26 shorter events, 1.4 us)
Async XLA Ops:
  0.6 8.0 %collective-permute-start = (bf16[192,128]{1,0:T(8,128)(2,1)}, bf16[192,128]{1,0:T(8,128)(2,1)S(1)}, u32[]{:S(2)}, u32[]{:S(2)}) collective-permute-start(bf16[192,128]{1,0:T(8,128)(2,1)} %bitcast.14), channel_id=1, source_target_pairs={{2,0},{0,2},{3,1},{1,3},{6,4},{4,6},{7,5},{5,7},{10,8},{8,10},{11,... | collective-permute-start | bytes 147464 | tf_op jit(solution)/shard_map/ppermute | solution.py:19
  3.6 5.0 %collective-permute-start.1 = (bf16[54,4,8]{2,1,0:T(4,128)(2,1)}, bf16[54,4,8]{2,1,0:T(4,128)(2,1)S(1)}, u32[]{:S(2)}, u32[]{:S(2)}) collective-permute-start(bf16[54,4,8]{2,1,0:T(4,128)(2,1)} %bitcast.12), channel_id=1, source_target_pairs={{2,0},{0,2},{3,1},{1,3},{6,4},{4,6},{7,5},{5,7},{10,8},{8,10},{11,... | collective-permute-start | bytes 10376 | tf_op jit(solution)/shard_map/ppermute | solution.py:19
  3.7 10.6 %collective-permute-start.2 = (bf16[128,1024]{1,0:T(8,128)(2,1)}, bf16[128,1024]{1,0:T(8,128)(2,1)S(1)}, u32[]{:S(2)}, u32[]{:S(2)}) collective-permute-start(bf16[128,1024]{1,0:T(8,128)(2,1)} %bitcast.10), channel_id=1, source_target_pairs={{2,0},{0,2},{3,1},{1,3},{6,4},{4,6},{7,5},{5,7},{10,8},{8,10},{11,... | collective-permute-start | bytes 786440 | tf_op jit(solution)/shard_map/ppermute | solution.py:19
  5.7 0.8 %copy-start.1 = (bf16[1,3,2,3,3,8,4]{5,6,4,3,2,1,0:T(4,128)(2,1)S(1)}, bf16[1,3,2,3,3,8,4]{5,6,4,3,2,1,0:T(4,128)(2,1)}, u32[]{:S(2)}) copy-start(bf16[1,3,2,3,3,8,4]{5,6,4,3,2,1,0:T(4,128)(2,1)} %param.7) | copy-start | bytes 10372
  6.5 0.8 %copy-start.2 = (bf16[1,2,3,8,2,2,128]{6,5,4,3,2,1,0:T(2,128)(2,1)S(1)}, bf16[1,2,3,8,2,2,128]{6,5,4,3,2,1,0:T(2,128)(2,1)}, u32[]{:S(2)}) copy-start(bf16[1,2,3,8,2,2,128]{6,5,4,3,2,1,0:T(2,128)(2,1)} %param.6) | copy-start | bytes 147460
  8.6 1.0 %copy-start = (bf16[1,128,1024]{2,1,0:T(8,128)(2,1)S(1)}, bf16[1,128,1024]{2,1,0:T(8,128)(2,1)}, u32[]{:S(2)}) copy-start(bf16[1,128,1024]{2,1,0:T(8,128)(2,1)} %param.8) | copy-start | bytes 786436
  8.6 1.0 %copy-start.5 = (s32[3]{0:T(128)S(1)}, s32[3]{0:T(128)}, u32[]{:S(2)}) copy-start(s32[3]{0:T(128)} %dirs_ref.1) | copy-start | bytes 40
  10.7 7.7 %collective-permute-start.6 = (bf16[128,1024]{1,0:T(8,128)(2,1)S(1)}, bf16[128,1024]{1,0:T(8,128)(2,1)S(1)}, u32[]{:S(2)}, u32[]{:S(2)}) collective-permute-start(bf16[128,1024]{1,0:T(8,128)(2,1)S(1)} %get-tuple-element.26.own_ref), channel_id=1, source_target_pairs={{4,0},{8,4},{12,8},{0,12},{5,1},{9,5},{13,9},{1,13},{6,2},{10,6},{... | collective-permute-start | bytes 786440 | tf_op jit(solution)/shard_map/ppermute | solution.py:19
  14.3 1.9 %collective-permute-start.3 = (bf16[128,1024]{1,0:T(8,128)(2,1)S(1)}, bf16[128,1024]{1,0:T(8,128)(2,1)S(1)}, u32[]{:S(2)}, u32[]{:S(2)}) collective-permute-start(bf16[128,1024]{1,0:T(8,128)(2,1)S(1)} %get-tuple-element.27), channel_id=1, source_target_pairs={{1,0},{0,1},{3,2},{2,3},{5,4},{4,5},{7,6},{6,7},{9,8},{8,9},{11,10... | collective-permute-start | bytes 786440 | tf_op jit(solution)/shard_map/ppermute | solution.py:19
  14.3 1.7 %collective-permute-start.5 = (bf16[64,1024]{1,0:T(8,128)(2,1)S(1)}, bf16[64,1024]{1,0:T(8,128)(2,1)S(1)}, u32[]{:S(2)}, u32[]{:S(2)}) collective-permute-start(bf16[64,1024]{1,0:T(8,128)(2,1)S(1)} %get-tuple-element.37), channel_id=1, source_target_pairs={{1,0},{0,1},{3,2},{2,3},{5,4},{4,5},{7,6},{6,7},{9,8},{8,9},{11,10... | collective-permute-start | bytes 393224 | tf_op jit(solution)/shard_map/ppermute | solution.py:19
  14.9 1.3 %collective-permute-start.4 = (bf16[64,1024]{1,0:T(8,128)(2,1)S(1)}, bf16[64,1024]{1,0:T(8,128)(2,1)S(1)}, u32[]{:S(2)}, u32[]{:S(2)}) collective-permute-start(bf16[64,1024]{1,0:T(8,128)(2,1)S(1)} %get-tuple-element.38), channel_id=1, source_target_pairs={{1,0},{0,1},{3,2},{2,3},{5,4},{4,5},{7,6},{6,7},{9,8},{8,9},{11,10... | collective-permute-start | bytes 393224 | tf_op jit(solution)/shard_map/ppermute | solution.py:19
  18.9 4.3 %copy-start.3 = (s32[4]{0:T(128)S(1)}, s32[4]{0:T(128)}, u32[]{:S(2)}) copy-start(s32[4]{0:T(128)} %offsets_ref.1) | copy-start | bytes 52
  18.9 4.3 %copy-start.4 = (s32[16]{0:T(128)S(1)}, s32[16]{0:T(128)}, u32[]{:S(2)}) copy-start(s32[16]{0:T(128)} %param.9) | copy-start | bytes 196
  18.9 8.2 %collective-permute-start.7 = (bf16[128,1024]{1,0:T(8,128)(2,1)S(1)}, bf16[128,1024]{1,0:T(8,128)(2,1)S(1)}, u32[]{:S(2)}, u32[]{:S(2)}) collective-permute-start(bf16[128,1024]{1,0:T(8,128)(2,1)S(1)} %get-tuple-element.32), channel_id=1, source_target_pairs={{4,0},{8,4},{12,8},{0,12},{5,1},{9,5},{13,9},{1,13},{6,2},{10,6},{... | collective-permute-start | bytes 786440 | tf_op jit(solution)/shard_map/ppermute | solution.py:19
  27.5 3.1 %collective-permute-start.10 = (f32[2,16]{1,0:T(2,128)S(1)}, f32[2,16]{1,0:T(2,128)S(1)}, u32[]{:S(2)}, u32[]{:S(2)}) collective-permute-start(f32[2,16]{1,0:T(2,128)S(1)} %shard_map.91), channel_id=1, source_target_pairs={{3,0},{0,1},{1,2},{2,3},{7,4},{4,5},{5,6},{6,7},{11,8},{8,9},{9,10... | collective-permute-start | bytes 392 | tf_op jit(solution)/shard_map/ppermute | solution.py:19
  27.5 3.6 %collective-permute-start.9 = (f32[2,16]{1,0:T(2,128)S(1)}, f32[2,16]{1,0:T(2,128)S(1)}, u32[]{:S(2)}, u32[]{:S(2)}) collective-permute-start(f32[2,16]{1,0:T(2,128)S(1)} %shard_map.91), channel_id=1, source_target_pairs={{2,0},{3,1},{0,2},{1,3},{6,4},{7,5},{4,6},{5,7},{10,8},{11,9},{8,1... | collective-permute-start | bytes 392 | tf_op jit(solution)/shard_map/ppermute | solution.py:19
  28.0 3.1 %collective-permute-start.8 = (f32[2,16]{1,0:T(2,128)S(1)}, f32[2,16]{1,0:T(2,128)S(1)}, u32[]{:S(2)}, u32[]{:S(2)}) collective-permute-start(f32[2,16]{1,0:T(2,128)S(1)} %shard_map.91), channel_id=1, source_target_pairs={{1,0},{2,1},{3,2},{0,3},{5,4},{6,5},{7,6},{4,7},{9,8},{10,9},{11,1... | collective-permute-start | bytes 392 | tf_op jit(solution)/shard_map/ppermute | solution.py:19
  31.1 3.6 %collective-permute-start.11 = (f32[2,16]{1,0:T(2,128)S(1)}, f32[2,16]{1,0:T(2,128)S(1)}, u32[]{:S(2)}, u32[]{:S(2)}) collective-permute-start(f32[2,16]{1,0:T(2,128)S(1)} %add_add_fusion), channel_id=1, source_target_pairs={{4,0},{0,4},{12,8},{8,12},{5,1},{1,5},{13,9},{9,13},{6,2},{2,6},{1... | collective-permute-start | bytes 392 | tf_op jit(solution)/shard_map/ppermute | solution.py:461
  34.7 4.5 %collective-permute-start.12 = (f32[2,16]{1,0:T(2,128)S(1)}, f32[2,16]{1,0:T(2,128)S(1)}, u32[]{:S(2)}, u32[]{:S(2)}) collective-permute-start(f32[2,16]{1,0:T(2,128)S(1)} %add.18), channel_id=1, source_target_pairs={{8,0},{12,4},{0,8},{4,12},{9,1},{13,5},{1,9},{5,13},{10,2},{14,6},... | collective-permute-start | bytes 392 | tf_op jit(solution)/shard_map/ppermute | solution.py:461

commit v4 on v3

--- a/solution.py
+++ b/solution.py
@@ -58,13 +58,13 @@
     return jnp.where(start, moved(field, (1 - side) * stride), moved(field, stride))
 
 
-def site_links(links_ref, wide_ref, turned_ref):
+def links_kernel(links_ref, out_ref, wide_ref, turned_ref):
     coefficients, cross, planes = links_ref.shape
     wide_ref[...] = links_ref[...].astype(F32)
     for at in range(cross):
         rows = pl.ds(at, planes, stride=cross)
         turned_ref[rows, :coefficients] = wide_ref[:, at, :].T
-    return turned_ref[...]
+    out_ref[...] = turned_ref[...].astype(BF16)
 
 
 def link_at(links, direction, colour, other):
@@ -113,9 +113,9 @@
     return [ref[k * cells : (k + 1) * cells, :].astype(F32) for k in range(6)]
 
 
-def slab_kernel(side, vectors_ref, links_ref, copy_ref, turned_ref, out_ref, wide_ref):
+def slab_kernel(side, vectors_ref, links_ref, copy_ref, out_ref):
     vectors = slab_fields(vectors_ref)
-    links = site_links(links_ref, wide_ref, turned_ref)
+    links = links_ref[...].astype(F32)
     cells = links.shape[0]
     copy_ref[...] = vectors_ref[...]
     parts = across_slab(links, 0, vectors, side) + across_slab(links, 1, vectors, side)
@@ -126,7 +126,7 @@
 
 def elementals_kernel(side, scale, slabs, early_ref, *refs):
     vector_refs, link_refs, out_refs = refs[:slabs], refs[slabs : 2 * slabs], refs[2 * slabs :]
-    elem_ref, rhs_ref, wide_ref, turned_ref = out_refs
+    elem_ref, rhs_ref = out_refs
     modes = elem_ref.shape[-1]
     cells = link_refs[0].shape[0]
     sites = slabs * cells
@@ -146,11 +146,7 @@
     put(0, 0, early[:6])
     put(0, 1, early[6:12])
     vectors = [slab_fields(ref) for ref in vector_refs]
-    links = [link_refs[0][...]]
-    links += [
-        site_links(ref, wide_ref.at[at], turned_ref.at[at])
-        for at, ref in enumerate(link_refs[1:])
-    ]
+    links = [ref[...].astype(F32) for ref in link_refs]
     adjoint = [early[12:]]
     for slab in range(1, slabs):
         put(slab, 0, across_slab(links[slab], 0, vectors[slab], side))
@@ -185,7 +181,7 @@
 
 
 def operator_kernel(
-    spaces, spins, dirs_ref, elem_ref, rows_ref, oper_ref, first_ref, trace_ref, copy_ref
+    dirs_ref, elem_ref, rows_ref, oper_ref, first_ref, wide_ref, copy_ref
 ):
     modes = elem_ref.shape[-1]
     copy_ref[...] = rows_ref[...]
@@ -206,17 +202,9 @@
             oper_ref[top : top + modes, right : right + modes] = real_part
             oper_ref[bottom : bottom + modes, left : left + modes] = -real_part
             oper_ref[bottom : bottom + modes, right : right + modes] = -imag_part
-    count, width = rows_ref.shape
-    first_row = own_block(spaces, spins, 0, 0) * count
     product = times_operator(rows_ref[...], oper_ref[...])
     first_ref[...] = product.astype(BF16)
-    trace_ref[...] = at_lanes(
-        trace_ref.shape,
-        [
-            (0, diagonal_sum(product[:, : width // 2], first_row)),
-            (1, diagonal_sum(product[:, width // 2 :], first_row)),
-        ],
-    )
+    wide_ref[...] = product
 
 
 def times_operator(rows, operator):
@@ -284,21 +272,17 @@
         at += 1
 
 
-def second_kernel(spaces, spins, next_ref, first_ref, early_ref, second_ref, trace_ref):
-    count = next_ref.shape[0]
+def second_kernel(next_ref, first_ref, second_ref, wide_ref):
     order = next_ref.shape[1] // 2
-    first_row = own_block(spaces, spins, 0, 0) * count
     real_part, imag_part = times_rows(next_ref[...], first_ref[...])
     second_ref[:, :order] = real_part.astype(BF16)
     second_ref[:, order:] = imag_part.astype(BF16)
-    trace_ref[...] = early_ref[...] + at_lanes(
-        trace_ref.shape,
-        [(2, diagonal_sum(real_part, first_row)), (3, diagonal_sum(imag_part, first_row))],
-    )
+    wide_ref[:, :order] = real_part
+    wide_ref[:, order:] = imag_part
 
 
 def turn_kernel(spaces, spins, offsets_ref, times_ref, first_ref, elem_ref, *refs):
-    out_ref, weights_ref, share_ref, wide_ref = refs
+    one_ref, two_ref, out_ref, weights_ref, share_ref, trace_ref, wide_ref = refs
     count, width = out_ref.shape
     order, lanes = width // 2, wide_ref.shape[0]
     first_row = own_block(spaces, spins, 0, 0) * count
@@ -308,6 +292,11 @@
         wide_ref[:, part * order : (part + 1) * order] = block.astype(F32).T
     rows = pl.ds(pl.multiple_of(first_row - start, count), count)
     out_ref[...] = wide_ref[rows, :].astype(BF16)
+    values = []
+    for at, part_ref in enumerate((one_ref, two_ref)):
+        values.append((2 * at, diagonal_sum(part_ref[:, :order], first_row)))
+        values.append((2 * at + 1, diagonal_sum(part_ref[:, order:], first_row)))
+    trace_ref[...] = at_lanes(trace_ref.shape, values)
     lane = lax.broadcasted_iota(jnp.int32, weights_ref.shape, 1)
     row = lax.broadcasted_iota(jnp.int32, weights_ref.shape, 0)
     counts = jnp.zeros(weights_ref.shape, F32)
@@ -363,18 +352,25 @@
     field = eigenvectors.reshape((6 * cells, modes))
     fields = [field] + [from_offset(field, "space", step) for step in range(1, spaces)]
     link = jnp.swapaxes(gauge_links.reshape((54, planes, side * side)), 1, 2)
+    link = vmem_call(
+        links_kernel,
+        jax.ShapeDtypeStruct((cells, modes), BF16),
+        [pltpu.VMEM(link.shape, F32), pltpu.VMEM((cells, modes), F32)],
+        10**6,
+    )(link)
     links = [link] + [from_offset(link, "space", step) for step in range(1, spaces)]
-    far_rows = [from_offset(own_rows, "space", step) for step in range(1, spaces)]
-    fields[0], links[0], own_slab = vmem_call(
+    fields[0], own_slab = vmem_call(
         functools.partial(slab_kernel, side),
         (
             jax.ShapeDtypeStruct(field.shape, BF16),
-            jax.ShapeDtypeStruct((cells, modes), F32),
             jax.ShapeDtypeStruct((18 * cells, modes), BF16),
         ),
-        [pltpu.VMEM(link.shape, F32)],
+        [],
         10**6,
     )(field, link)
+
+    held_rows, own_slab = lax.optimization_barrier((own_rows, own_slab))
+    far_rows = [from_offset(held_rows, "space", step) for step in range(1, spaces)]
 
     norm_scale = 1.0 / math.sqrt(6.0 * 4.0 * planes * spaces * side * side)
     rows_shape = jax.ShapeDtypeStruct((count, width), BF16)
@@ -382,21 +378,13 @@
     elements = vmem_call(
         functools.partial(elementals_kernel, side, norm_scale, spaces),
         jax.ShapeDtypeStruct((3, 2, modes, modes), F32),
-        [
-            pltpu.VMEM((6 * cells * spaces, 6 * modes), BF16),
-            pltpu.VMEM((spaces - 1,) + link.shape, F32),
-            pltpu.VMEM((spaces - 1, cells, modes), F32),
-        ],
+        [pltpu.VMEM((6 * cells * spaces, 6 * modes), BF16)],
         10**10,
     )(own_slab, *fields, *links)
-    operator, own_first, early, rows_copy = vmem_call(
-        functools.partial(operator_kernel, spaces, spins),
-        (
-            jax.ShapeDtypeStruct((4 * modes, 4 * modes), BF16),
-            rows_shape,
-            trace_shape,
-            rows_shape,
-        ),
+    wide_shape = jax.ShapeDtypeStruct((count, width), F32)
+    operator, own_first, own_wide, rows_copy = vmem_call(
+        operator_kernel,
+        (jax.ShapeDtypeStruct((4 * modes, 4 * modes), BF16), rows_shape, wide_shape, rows_shape),
         [],
         10**8,
         smem=(0,),
@@ -421,26 +409,27 @@
         10**6,
     )(operator, held_first, *blocks)
 
-    second, early = vmem_call(
-        functools.partial(second_kernel, spaces, spins),
-        (rows_shape, trace_shape),
+    second, second_wide = vmem_call(
+        second_kernel,
+        (rows_shape, wide_shape),
         [],
         3 * 10**8,
-    )(next_first, first, early)
+    )(next_first, first)
 
     next_second = from_offset(second, "tm", 1)
 
-    turned, weights, elementals = vmem_call(
+    turned, weights, elementals, early = vmem_call(
         functools.partial(turn_kernel, spaces, spins),
         (
             rows_shape,
             trace_shape,
             jax.ShapeDtypeStruct((modes // spaces, 3, 2, modes // spins), F32),
+            trace_shape,
         ),
         [pltpu.VMEM((max(count, 128), width), F32)],
         10**6,
         smem=(0,),
-    )(insert_offsets, source_times[None, :], first, elements)
+    )(insert_offsets, source_times[None, :], first, elements, own_wide, second_wide)
     shares = vmem_call(
         share_kernel,
         jax.ShapeDtypeStruct((2, source_times.shape[0]), F32),

time: 40 us -> 39.5 us (0.988)
  waiting for transfers between devices: 11.7 us -> 10.9 us
  local copies, waits for them, and re-layouts: 1.64 us -> 2.29 us
    unnamed x12, local copies, waits for them, and re-layouts: 1.63 us -> 2.27 us
    ppermute x11, waiting for transfers between devices: 6.53 us -> 5.91 us  [from_offset(): lax.ppermute(block, axis, [((i + distance) % count, i) for i in range(cou...]
    pallas_call x8 -> x9, Pallas kernels: 6.72 us -> 6.38 us  [call(): pl.pallas_call(kernel, out_shape=out_shape, in_specs=specs, out_specs=out...]
  transfers between devices with their start and end apart: 13 -> 13, of which waited for: 8 -> 8; matrix products, arithmetic and copies ran while one was open for 0% -> 0% of each run, Pallas kernels for 15% -> 14%
where the time goes in v4:
time: 39.5 us; the launch traced here: 39.3 us
  starting transfers between devices  18.5 us (47%)
  waiting for transfers between devices  10.9 us (28%)
  Pallas kernels  6.38 us (16%)
  local copies, waits for them, and re-layouts  2.29 us (6%)
  between operations  0.7 us (2%)
  other arithmetic  0.57 us (1%)
    ppermute x11, starting transfers between devices, from_offset(): lax.ppermute(block, axis, [((i + distance) % count, i) for i in range(cou...  15.3 us
    pallas_call x9, Pallas kernels, call(): pl.pallas_call(kernel, out_shape=out_shape, in_specs=specs, out_specs=out...  6.38 us
    ppermute x11, waiting for transfers between devices, from_offset(): lax.ppermute(block, axis, [((i + distance) % count, i) for i in range(cou...  5.91 us
    ppermute x2, waiting for transfers between devices, on_device(): lax.ppermute(shares, 'tm', [(i ^ step, i) for i in range(slots)])  4.94 us
    ppermute x2, starting transfers between devices, on_device(): lax.ppermute(shares, 'tm', [(i ^ step, i) for i in range(slots)])  3.16 us
    unnamed x12, local copies, waits for them, and re-layouts  2.27 us
  transfers between devices with their start and end apart: 13, of which 8 were waited for; matrix products, arithmetic and copies ran while one was open for 0% of the time, Pallas kernels for 14%

profile of v4, /device:TPU:0, one launch (start us, length us, event | category | flops | bytes accessed | tf_op | source)
XLA Modules:
  0.0 39.3 jit_solution(938041905026628060)
XLA Ops:
  0.6 3.0 %collective-permute-start = (bf16[192,128]{1,0:T(8,128)(2,1)}, bf16[192,128]{1,0:T(8,128)(2,1)S(1)}, u32[]{:S(2)}, u32[]{:S(2)}) collective-permute-start(bf16[192,128]{1,0:T(8,128)(2,1)} %bitcast.13), channel_id=1, source_target_pairs={{2,0},{0,2},{3,1},{1,3},{6,4},{4,6},{7,5},{5,7},{10,8},{8,10},{11,... | collective-permute-start | bytes 147464 | tf_op jit(solution)/shard_map/ppermute | solution.py:19
  3.6 0.8 %copy-done.1 = bf16[1,3,2,3,3,8,4]{5,6,4,3,2,1,0:T(4,128)(2,1)S(1)} copy-done((bf16[1,3,2,3,3,8,4]{5,6,4,3,2,1,0:T(4,128)(2,1)S(1)}, bf16[1,3,2,3,3,8,4]{5,6,4,3,2,1,0:T(4,128)(2,1)}, u32[]{:S(2)}) %copy-start.1) | copy-done | bytes 3480
  4.6 0.6 %copy-done.2 = bf16[1,2,3,8,2,2,128]{6,5,4,3,2,1,0:T(2,128)(2,1)S(1)} copy-done((bf16[1,2,3,8,2,2,128]{6,5,4,3,2,1,0:T(2,128)(2,1)S(1)}, bf16[1,2,3,8,2,2,128]{6,5,4,3,2,1,0:T(2,128)(2,1)}, u32[]{:S(2)}) %copy-start.2) | copy-done | bytes 49176
  5.6 1.5 %collective-permute-start.2 = (bf16[128,1024]{1,0:T(8,128)(2,1)}, bf16[128,1024]{1,0:T(8,128)(2,1)S(1)}, u32[]{:S(2)}, u32[]{:S(2)}) collective-permute-start(bf16[128,1024]{1,0:T(8,128)(2,1)} %bitcast.10), channel_id=1, source_target_pairs={{2,0},{0,2},{3,1},{1,3},{6,4},{4,6},{7,5},{5,7},{10,8},{8,10},{11,... | collective-permute-start | bytes 786440 | tf_op jit(solution)/shard_map/ppermute | solution.py:19
  7.1 1.3 %collective-permute-done.1.refs_3_ = bf16[32,128]{1,0:T(8,128)(2,1)S(1)} collective-permute-done((bf16[32,128]{1,0:T(8,128)(2,1)S(1)}, bf16[32,128]{1,0:T(8,128)(2,1)S(1)}, u32[]{:S(2)}, u32[]{:S(2)}) %collective-permute-start.1) | collective-permute-done | bytes 8224 | tf_op jit(solution)/shard_map/ppermute | solution.py:19
  8.4 0.8 %shard_map.87.elem_ref = f32[3,2,128,128]{3,2,1,0:T(8,128)S(1)} custom-call(bf16[576,128]{1,0:T(8,128)(2,1)S(1)} %get-tuple-element.23.early_ref, bf16[192,128]{1,0:T(8,128)(2,1)S(1)} %get-tuple-element.24.refs_0_, bf16[192,128]{1,0:T(8,128)(2,1)S(1)} %collective-permute-done.refs_1_, bf16[32,128]{1,0:T(8,128)(2,1)S(1)} %shard_map.85.links_ref.refs_2_, ...), custom_call_target="tpu_custom_call" | custom-call | flops 10000000000 | bytes 1048576 | tf_op jit(solution)/shard_map/pallas_call | solution.py:29
  9.3 0.9 %shard_map.88 = (bf16[512,512]{1,0:T(8,128)(2,1)S(1)}, bf16[128,1024]{1,0:T(8,128)(2,1)S(1)}, f32[128,1024]{1,0:T(8,128)S(1)}, bf16[128,1024]{1,0:T(8,128)(2,1)S(1)}) custom-call(s32[3]{0:T(128)S(1)} %copy-done.5, f32[3,2,128,128]{3,2,1,0:T(8,128)S(1)} %shard_map.87.elem_ref, bf16[128,1024]{1,0:T(8,128)(2,1)S(1)} %bitcast.11), custom_call_target="tpu_custom_call" | custom-call | flops 100000000 | bytes 1048576 | tf_op jit(solution)/shard_map/pallas_call | solution.py:29
  10.2 3.7 %collective-permute-start.6 = (bf16[128,1024]{1,0:T(8,128)(2,1)S(1)}, bf16[128,1024]{1,0:T(8,128)(2,1)S(1)}, u32[]{:S(2)}, u32[]{:S(2)}) collective-permute-start(bf16[128,1024]{1,0:T(8,128)(2,1)S(1)} %get-tuple-element.29.own_ref), channel_id=1, source_target_pairs={{4,0},{8,4},{12,8},{0,12},{5,1},{9,5},{13,9},{1,13},{6,2},{10,6},{... | collective-permute-start | bytes 786440 | tf_op jit(solution)/shard_map/ppermute | solution.py:19
  13.9 0.6 %collective-permute-start.5 = (bf16[64,1024]{1,0:T(8,128)(2,1)S(1)}, bf16[64,1024]{1,0:T(8,128)(2,1)S(1)}, u32[]{:S(2)}, u32[]{:S(2)}) collective-permute-start(bf16[64,1024]{1,0:T(8,128)(2,1)S(1)} %get-tuple-element.41), channel_id=1, source_target_pairs={{1,0},{0,1},{3,2},{2,3},{5,4},{4,5},{7,6},{6,7},{9,8},{8,9},{11,10... | collective-permute-start | bytes 393224 | tf_op jit(solution)/shard_map/ppermute | solution.py:19
  14.6 1.0 %collective-permute-done.5.refs_3_ = bf16[64,1024]{1,0:T(8,128)(2,1)S(1)} collective-permute-done((bf16[64,1024]{1,0:T(8,128)(2,1)S(1)}, bf16[64,1024]{1,0:T(8,128)(2,1)S(1)}, u32[]{:S(2)}, u32[]{:S(2)}) %collective-permute-start.5) | collective-permute-done | bytes 131104 | tf_op jit(solution)/shard_map/ppermute | solution.py:19
  15.9 0.6 %shard_map.89.first_ref = bf16[512,1024]{1,0:T(8,128)(2,1)S(1)} custom-call(bf16[512,512]{1,0:T(8,128)(2,1)S(1)} %get-tuple-element.25.oper_ref, bf16[128,1024]{1,0:T(8,128)(2,1)S(1)} %get-tuple-element.29.own_ref, bf16[128,1024]{1,0:T(8,128)(2,1)S(1)} %collective-permute-done.3.refs_0_, bf16[128,1024]{1,0:T(8,128)(2,1)S(1)} %collective-permute-done.2.refs_1_, ...), custom_call_target="tpu_custom_call" | custom-call | flops 1000000 | bytes 1048576 | tf_op jit(solution)/shard_map/pallas_call | solution.py:29
  16.4 1.5 %collective-permute-done.6.next_ref = bf16[128,1024]{1,0:T(8,128)(2,1)S(1)} collective-permute-done((bf16[128,1024]{1,0:T(8,128)(2,1)S(1)}, bf16[128,1024]{1,0:T(8,128)(2,1)S(1)}, u32[]{:S(2)}, u32[]{:S(2)}) %collective-permute-start.6) | collective-permute-done | bytes 262176 | tf_op jit(solution)/shard_map/ppermute | solution.py:19
  17.9 0.4 %shard_map.90 = (bf16[128,1024]{1,0:T(8,128)(2,1)S(1)}, f32[128,1024]{1,0:T(8,128)S(1)}) custom-call(bf16[128,1024]{1,0:T(8,128)(2,1)S(1)} %collective-permute-done.6.next_ref, bf16[512,1024]{1,0:T(8,128)(2,1)S(1)} %shard_map.89.first_ref), custom_call_target="tpu_custom_call" | custom-call | flops 300000000 | bytes 1048576 | tf_op jit(solution)/shard_map/pallas_call | solution.py:29
  18.4 4.3 %collective-permute-start.7 = (bf16[128,1024]{1,0:T(8,128)(2,1)S(1)}, bf16[128,1024]{1,0:T(8,128)(2,1)S(1)}, u32[]{:S(2)}, u32[]{:S(2)}) collective-permute-start(bf16[128,1024]{1,0:T(8,128)(2,1)S(1)} %get-tuple-element.36), channel_id=1, source_target_pairs={{4,0},{8,4},{12,8},{0,12},{5,1},{9,5},{13,9},{1,13},{6,2},{10,6},{... | collective-permute-start | bytes 786440 | tf_op jit(solution)/shard_map/ppermute | solution.py:19
  22.7 0.7 %copy-done.3 = s32[4]{0:T(128)S(1)} copy-done((s32[4]{0:T(128)S(1)}, s32[4]{0:T(128)}, u32[]{:S(2)}) %copy-start.3) | copy-done | bytes 40
  23.4 1.6 %shard_map.91 = (bf16[128,1024]{1,0:T(8,128)(2,1)S(1)}, f32[8,128]{1,0:T(8,128)S(1)}, f32[64,3,2,64]{3,2,1,0:T(2,128)}, f32[8,128]{1,0:T(8,128)S(1)}) custom-call(s32[4]{0:T(128)S(1)} %copy-done.3, s32[1,16]{1,0:T(1,128)S(1)} %bitcast.15, bf16[512,1024]{1,0:T(8,128)(2,1)S(1)} %shard_map.89.first_ref, f32[3,2,128,128]{3,2,1,0:T(8,128)S(1)} %shard_map.87.elem_ref, ...), custom_call_target="tpu_custom_call" | custom-call | flops 1000000 | bytes 1048576 | tf_op jit(solution)/shard_map/pallas_call | solution.py:29
  25.0 1.6 %collective-permute-done.7.second_ref = bf16[128,1024]{1,0:T(8,128)(2,1)S(1)} collective-permute-done((bf16[128,1024]{1,0:T(8,128)(2,1)S(1)}, bf16[128,1024]{1,0:T(8,128)(2,1)S(1)}, u32[]{:S(2)}, u32[]{:S(2)}) %collective-permute-start.7) | collective-permute-done | bytes 262176 | tf_op jit(solution)/shard_map/ppermute | solution.py:19
  27.0 0.8 %collective-permute-start.9 = (f32[2,16]{1,0:T(2,128)S(1)}, f32[2,16]{1,0:T(2,128)S(1)}, u32[]{:S(2)}, u32[]{:S(2)}) collective-permute-start(f32[2,16]{1,0:T(2,128)S(1)} %shard_map.92), channel_id=1, source_target_pairs={{2,0},{3,1},{0,2},{1,3},{6,4},{7,5},{4,6},{5,7},{10,8},{11,9},{8,1... | collective-permute-start | bytes 392 | tf_op jit(solution)/shard_map/ppermute | solution.py:19
  27.7 1.4 %collective-permute-start.8 = (f32[2,16]{1,0:T(2,128)S(1)}, f32[2,16]{1,0:T(2,128)S(1)}, u32[]{:S(2)}, u32[]{:S(2)}) collective-permute-start(f32[2,16]{1,0:T(2,128)S(1)} %shard_map.92), channel_id=1, source_target_pairs={{1,0},{2,1},{3,2},{0,3},{5,4},{6,5},{7,6},{4,7},{9,8},{10,9},{11,1... | collective-permute-start | bytes 392 | tf_op jit(solution)/shard_map/ppermute | solution.py:19
  29.2 1.1 %shard_map.93 = bf16[128,1024]{1,0:T(8,128)(2,1)} custom-call(bf16[128,1024]{1,0:T(8,128)(2,1)S(1)} %collective-permute-done.7.second_ref, bf16[512,1024]{1,0:T(8,128)(2,1)S(1)} %shard_map.89.first_ref), custom_call_target="tpu_custom_call" | custom-call | flops 100000000 | bytes 1048576 | tf_op jit(solution)/shard_map/pallas_call | solution.py:29
  30.9 3.3 %collective-permute-done.11 = f32[2,16]{1,0:T(2,128)S(1)} collective-permute-done((f32[2,16]{1,0:T(2,128)S(1)}, f32[2,16]{1,0:T(2,128)S(1)}, u32[]{:S(2)}, u32[]{:S(2)}) %collective-permute-start.11) | collective-permute-done | bytes 160 | tf_op jit(solution)/shard_map/ppermute | solution.py:450
  34.2 2.8 %collective-permute-start.12 = (f32[2,16]{1,0:T(2,128)S(1)}, f32[2,16]{1,0:T(2,128)S(1)}, u32[]{:S(2)}, u32[]{:S(2)}) collective-permute-start(f32[2,16]{1,0:T(2,128)S(1)} %add.18), channel_id=1, source_target_pairs={{8,0},{12,4},{0,8},{4,12},{9,1},{13,5},{1,9},{5,13},{10,2},{14,6},... | collective-permute-start | bytes 392 | tf_op jit(solution)/shard_map/ppermute | solution.py:450
  37.1 1.6 %collective-permute-done.12 = f32[2,16]{1,0:T(2,128)S(1)} collective-permute-done((f32[2,16]{1,0:T(2,128)S(1)}, f32[2,16]{1,0:T(2,128)S(1)}, u32[]{:S(2)}, u32[]{:S(2)}) %collective-permute-start.12) | collective-permute-done | bytes 160 | tf_op jit(solution)/shard_map/ppermute | solution.py:450
  38.7 0.6 %add_bitcast_fusion = f32[16,2]{0,1:T(2,128)} fusion(f32[2,16]{1,0:T(2,128)S(1)} %add.18, f32[2,16]{1,0:T(2,128)S(1)} %collective-permute-done.12), kind=kLoop, calls=%fused_computation | loop fusion | flops 32 | bytes 384 | tf_op jit(solution)/shard_map/transpose | solution.py:452
  (27 shorter events, 2.0 us)
Async XLA Ops:
  0.6 7.7 %collective-permute-start = (bf16[192,128]{1,0:T(8,128)(2,1)}, bf16[192,128]{1,0:T(8,128)(2,1)S(1)}, u32[]{:S(2)}, u32[]{:S(2)}) collective-permute-start(bf16[192,128]{1,0:T(8,128)(2,1)} %bitcast.13), channel_id=1, source_target_pairs={{2,0},{0,2},{3,1},{1,3},{6,4},{4,6},{7,5},{5,7},{10,8},{8,10},{11,... | collective-permute-start | bytes 147464 | tf_op jit(solution)/shard_map/ppermute | solution.py:19
  3.6 0.8 %copy-start.1 = (bf16[1,3,2,3,3,8,4]{5,6,4,3,2,1,0:T(4,128)(2,1)S(1)}, bf16[1,3,2,3,3,8,4]{5,6,4,3,2,1,0:T(4,128)(2,1)}, u32[]{:S(2)}) copy-start(bf16[1,3,2,3,3,8,4]{5,6,4,3,2,1,0:T(4,128)(2,1)} %param.7) | copy-start | bytes 10372
  4.4 0.8 %copy-start.2 = (bf16[1,2,3,8,2,2,128]{6,5,4,3,2,1,0:T(2,128)(2,1)S(1)}, bf16[1,2,3,8,2,2,128]{6,5,4,3,2,1,0:T(2,128)(2,1)}, u32[]{:S(2)}) copy-start(bf16[1,2,3,8,2,2,128]{6,5,4,3,2,1,0:T(2,128)(2,1)} %param.6) | copy-start | bytes 147460
  4.6 3.8 %collective-permute-start.1 = (bf16[32,128]{1,0:T(8,128)(2,1)S(1)}, bf16[32,128]{1,0:T(8,128)(2,1)S(1)}, u32[]{:S(2)}, u32[]{:S(2)}) collective-permute-start(bf16[32,128]{1,0:T(8,128)(2,1)S(1)} %shard_map.85.links_ref.refs_2_), channel_id=1, source_target_pairs={{2,0},{0,2},{3,1},{1,3},{6,4},{4,6},{7,5},{5,7},{10,8},{8,10},{11,... | collective-permute-start | bytes 24584 | tf_op jit(solution)/shard_map/ppermute | solution.py:19
  5.6 8.3 %collective-permute-start.2 = (bf16[128,1024]{1,0:T(8,128)(2,1)}, bf16[128,1024]{1,0:T(8,128)(2,1)S(1)}, u32[]{:S(2)}, u32[]{:S(2)}) collective-permute-start(bf16[128,1024]{1,0:T(8,128)(2,1)} %bitcast.10), channel_id=1, source_target_pairs={{2,0},{0,2},{3,1},{1,3},{6,4},{4,6},{7,5},{5,7},{10,8},{8,10},{11,... | collective-permute-start | bytes 786440 | tf_op jit(solution)/shard_map/ppermute | solution.py:19
  8.4 1.0 %copy-start = (bf16[1,128,1024]{2,1,0:T(8,128)(2,1)S(1)}, bf16[1,128,1024]{2,1,0:T(8,128)(2,1)}, u32[]{:S(2)}) copy-start(bf16[1,128,1024]{2,1,0:T(8,128)(2,1)} %param.8) | copy-start | bytes 786436
  8.4 1.0 %copy-start.5 = (s32[3]{0:T(128)S(1)}, s32[3]{0:T(128)}, u32[]{:S(2)}) copy-start(s32[3]{0:T(128)} %dirs_ref.1) | copy-start | bytes 40
  10.2 7.7 %collective-permute-start.6 = (bf16[128,1024]{1,0:T(8,128)(2,1)S(1)}, bf16[128,1024]{1,0:T(8,128)(2,1)S(1)}, u32[]{:S(2)}, u32[]{:S(2)}) collective-permute-start(bf16[128,1024]{1,0:T(8,128)(2,1)S(1)} %get-tuple-element.29.own_ref), channel_id=1, source_target_pairs={{4,0},{8,4},{12,8},{0,12},{5,1},{9,5},{13,9},{1,13},{6,2},{10,6},{... | collective-permute-start | bytes 786440 | tf_op jit(solution)/shard_map/ppermute | solution.py:19
  13.9 1.9 %collective-permute-start.3 = (bf16[128,1024]{1,0:T(8,128)(2,1)S(1)}, bf16[128,1024]{1,0:T(8,128)(2,1)S(1)}, u32[]{:S(2)}, u32[]{:S(2)}) collective-permute-start(bf16[128,1024]{1,0:T(8,128)(2,1)S(1)} %get-tuple-element.30), channel_id=1, source_target_pairs={{1,0},{0,1},{3,2},{2,3},{5,4},{4,5},{7,6},{6,7},{9,8},{8,9},{11,10... | collective-permute-start | bytes 786440 | tf_op jit(solution)/shard_map/ppermute | solution.py:19
  13.9 1.7 %collective-permute-start.5 = (bf16[64,1024]{1,0:T(8,128)(2,1)S(1)}, bf16[64,1024]{1,0:T(8,128)(2,1)S(1)}, u32[]{:S(2)}, u32[]{:S(2)}) collective-permute-start(bf16[64,1024]{1,0:T(8,128)(2,1)S(1)} %get-tuple-element.41), channel_id=1, source_target_pairs={{1,0},{0,1},{3,2},{2,3},{5,4},{4,5},{7,6},{6,7},{9,8},{8,9},{11,10... | collective-permute-start | bytes 393224 | tf_op jit(solution)/shard_map/ppermute | solution.py:19
  14.5 1.3 %collective-permute-start.4 = (bf16[64,1024]{1,0:T(8,128)(2,1)S(1)}, bf16[64,1024]{1,0:T(8,128)(2,1)S(1)}, u32[]{:S(2)}, u32[]{:S(2)}) collective-permute-start(bf16[64,1024]{1,0:T(8,128)(2,1)S(1)} %get-tuple-element.42), channel_id=1, source_target_pairs={{1,0},{0,1},{3,2},{2,3},{5,4},{4,5},{7,6},{6,7},{9,8},{8,9},{11,10... | collective-permute-start | bytes 393224 | tf_op jit(solution)/shard_map/ppermute | solution.py:19
  18.4 8.2 %collective-permute-start.7 = (bf16[128,1024]{1,0:T(8,128)(2,1)S(1)}, bf16[128,1024]{1,0:T(8,128)(2,1)S(1)}, u32[]{:S(2)}, u32[]{:S(2)}) collective-permute-start(bf16[128,1024]{1,0:T(8,128)(2,1)S(1)} %get-tuple-element.36), channel_id=1, source_target_pairs={{4,0},{8,4},{12,8},{0,12},{5,1},{9,5},{13,9},{1,13},{6,2},{10,6},{... | collective-permute-start | bytes 786440 | tf_op jit(solution)/shard_map/ppermute | solution.py:19
  22.7 0.7 %copy-start.3 = (s32[4]{0:T(128)S(1)}, s32[4]{0:T(128)}, u32[]{:S(2)}) copy-start(s32[4]{0:T(128)} %offsets_ref.1) | copy-start | bytes 52
  22.7 0.7 %copy-start.4 = (s32[16]{0:T(128)S(1)}, s32[16]{0:T(128)}, u32[]{:S(2)}) copy-start(s32[16]{0:T(128)} %param.9) | copy-start | bytes 196
  27.0 3.3 %collective-permute-start.10 = (f32[2,16]{1,0:T(2,128)S(1)}, f32[2,16]{1,0:T(2,128)S(1)}, u32[]{:S(2)}, u32[]{:S(2)}) collective-permute-start(f32[2,16]{1,0:T(2,128)S(1)} %shard_map.92), channel_id=1, source_target_pairs={{3,0},{0,1},{1,2},{2,3},{7,4},{4,5},{5,6},{6,7},{11,8},{8,9},{9,10... | collective-permute-start | bytes 392 | tf_op jit(solution)/shard_map/ppermute | solution.py:19
  27.0 3.6 %collective-permute-start.9 = (f32[2,16]{1,0:T(2,128)S(1)}, f32[2,16]{1,0:T(2,128)S(1)}, u32[]{:S(2)}, u32[]{:S(2)}) collective-permute-start(f32[2,16]{1,0:T(2,128)S(1)} %shard_map.92), channel_id=1, source_target_pairs={{2,0},{3,1},{0,2},{1,3},{6,4},{7,5},{4,6},{5,7},{10,8},{11,9},{8,1... | collective-permute-start | bytes 392 | tf_op jit(solution)/shard_map/ppermute | solution.py:19
  27.7 2.9 %collective-permute-start.8 = (f32[2,16]{1,0:T(2,128)S(1)}, f32[2,16]{1,0:T(2,128)S(1)}, u32[]{:S(2)}, u32[]{:S(2)}) collective-permute-start(f32[2,16]{1,0:T(2,128)S(1)} %shard_map.92), channel_id=1, source_target_pairs={{1,0},{2,1},{3,2},{0,3},{5,4},{6,5},{7,6},{4,7},{9,8},{10,9},{11,1... | collective-permute-start | bytes 392 | tf_op jit(solution)/shard_map/ppermute | solution.py:19
  30.6 3.6 %collective-permute-start.11 = (f32[2,16]{1,0:T(2,128)S(1)}, f32[2,16]{1,0:T(2,128)S(1)}, u32[]{:S(2)}, u32[]{:S(2)}) collective-permute-start(f32[2,16]{1,0:T(2,128)S(1)} %add_add_fusion), channel_id=1, source_target_pairs={{4,0},{0,4},{12,8},{8,12},{5,1},{1,5},{13,9},{9,13},{6,2},{2,6},{1... | collective-permute-start | bytes 392 | tf_op jit(solution)/shard_map/ppermute | solution.py:450
  34.2 4.5 %collective-permute-start.12 = (f32[2,16]{1,0:T(2,128)S(1)}, f32[2,16]{1,0:T(2,128)S(1)}, u32[]{:S(2)}, u32[]{:S(2)}) collective-permute-start(f32[2,16]{1,0:T(2,128)S(1)} %add.18), channel_id=1, source_target_pairs={{8,0},{12,4},{0,8},{4,12},{9,1},{13,5},{1,9},{5,13},{10,2},{14,6},... | collective-permute-start | bytes 392 | tf_op jit(solution)/shard_map/ppermute | solution.py:450

commit v5 on v4

--- a/solution.py
+++ b/solution.py
@@ -17,6 +17,10 @@
 def from_offset(block, axis, distance):
     count = lax.axis_size(axis)
     return lax.ppermute(block, axis, [((i + distance) % count, i) for i in range(count)])
+
+
+def swapped(block, devices, mask):
+    return lax.ppermute(block, ("tm", "space", "spin"), [(i ^ mask, i) for i in range(devices)])
 
 
 def vmem_call(kernel, out_shape, scratch, flops, smem=()):
@@ -438,17 +442,17 @@
     )(weights, next_second, turned, early)
     chain = vmem_call(third_kernel, rows_shape, [], 10**8)(next_second, first)
 
-    group = spaces * spins
-    parts = [shares] + [from_offset(shares, ("space", "spin"), step) for step in range(1, group)]
-    shares = functools.reduce(lambda a, b: a + b, parts)
-    shares, chain = lax.optimization_barrier((shares, chain))
-    if slots & (slots - 1):
-        shares = lax.psum(shares, "tm")
+    devices = slots * spaces * spins
+    if devices & (devices - 1):
+        shares = lax.psum(shares, ("tm", "space", "spin"))
     else:
-        step = 1
-        while step < slots:
-            shares = shares + lax.ppermute(shares, "tm", [(i ^ step, i) for i in range(slots)])
-            step *= 2
+        bits = [1 << at for at in range(devices.bit_length() - 1)]
+        while bits:
+            low, high = bits[0], bits[-1]
+            bits = bits[1:-1]
+            masks = [low] if low == high else [low, high, low | high]
+            parts = [swapped(shares, devices, mask) for mask in masks]
+            shares = functools.reduce(lambda x, y: x + y, parts, shares)
     return (elementals[None], chain[None], shares.T)
 
 

time: 39.5 us -> 38.1 us (0.965)
  waiting for transfers between devices: 10.9 us -> 8.5 us
  starting transfers between devices: 18.5 us -> 19.4 us
    ppermute x2 -> x6, starting transfers between devices: 3.16 us -> 6.31 us  [swapped(): lax.ppermute(block, ('tm', 'space', 'spin'), [(i ^ mask, i) for i in rang...]
    ppermute x11 -> x8, starting transfers between devices: 15.3 us -> 13.1 us  [from_offset(): lax.ppermute(block, axis, [((i + distance) % count, i) for i in range(cou...]
    ppermute x2 -> x6, waiting for transfers between devices: 4.94 us -> 2.86 us  [swapped(): lax.ppermute(block, ('tm', 'space', 'spin'), [(i ^ mask, i) for i in rang...]
    ppermute x11 -> x8, waiting for transfers between devices: 5.91 us -> 5.64 us  [from_offset(): lax.ppermute(block, axis, [((i + distance) % count, i) for i in range(cou...]
  transfers between devices with their start and end apart: 13 -> 14, of which waited for: 8 -> 9; matrix products, arithmetic and copies ran while one was open for 0% -> 0% of each run, Pallas kernels for 14% -> 15%
where the time goes in v5:
time: 38.1 us; the launch traced here: 37.9 us
  starting transfers between devices  19.4 us (51%)
  waiting for transfers between devices  8.5 us (22%)
  Pallas kernels  6.38 us (17%)
  local copies, waits for them, and re-layouts  2.29 us (6%)
  between operations  0.7 us (2%)
  other arithmetic  0.57 us (1%)
    ppermute x8, starting transfers between devices, from_offset(): lax.ppermute(block, axis, [((i + distance) % count, i) for i in range(cou...  13.1 us
    pallas_call x9, Pallas kernels, call(): pl.pallas_call(kernel, out_shape=out_shape, in_specs=specs, out_specs=out...  6.38 us
    ppermute x6, starting transfers between devices, swapped(): lax.ppermute(block, ('tm', 'space', 'spin'), [(i ^ mask, i) for i in rang...  6.31 us
    ppermute x8, waiting for transfers between devices, from_offset(): lax.ppermute(block, axis, [((i + distance) % count, i) for i in range(cou...  5.64 us
    ppermute x6, waiting for transfers between devices, swapped(): lax.ppermute(block, ('tm', 'space', 'spin'), [(i ^ mask, i) for i in rang...  2.86 us
    unnamed x12, local copies, waits for them, and re-layouts  2.27 us
  transfers between devices with their start and end apart: 14, of which 9 were waited for; matrix products, arithmetic and copies ran while one was open for 0% of the time, Pallas kernels for 15%

profile of v5, /device:TPU:0, one launch (start us, length us, event | category | flops | bytes accessed | tf_op | source)
XLA Modules:
  0.0 37.9 jit_solution(2977324026413101006)
XLA Ops:
  0.6 3.0 %collective-permute-start = (bf16[192,128]{1,0:T(8,128)(2,1)}, bf16[192,128]{1,0:T(8,128)(2,1)S(1)}, u32[]{:S(2)}, u32[]{:S(2)}) collective-permute-start(bf16[192,128]{1,0:T(8,128)(2,1)} %bitcast.13), channel_id=1, source_target_pairs={{2,0},{0,2},{3,1},{1,3},{6,4},{4,6},{7,5},{5,7},{10,8},{8,10},{11,... | collective-permute-start | bytes 147464 | tf_op jit(solution)/shard_map/ppermute | solution.py:19
  3.6 0.8 %copy-done.1 = bf16[1,3,2,3,3,8,4]{5,6,4,3,2,1,0:T(4,128)(2,1)S(1)} copy-done((bf16[1,3,2,3,3,8,4]{5,6,4,3,2,1,0:T(4,128)(2,1)S(1)}, bf16[1,3,2,3,3,8,4]{5,6,4,3,2,1,0:T(4,128)(2,1)}, u32[]{:S(2)}) %copy-start.1) | copy-done | bytes 3480
  4.6 0.6 %copy-done.2 = bf16[1,2,3,8,2,2,128]{6,5,4,3,2,1,0:T(2,128)(2,1)S(1)} copy-done((bf16[1,2,3,8,2,2,128]{6,5,4,3,2,1,0:T(2,128)(2,1)S(1)}, bf16[1,2,3,8,2,2,128]{6,5,4,3,2,1,0:T(2,128)(2,1)}, u32[]{:S(2)}) %copy-start.2) | copy-done | bytes 49176
  5.6 1.5 %collective-permute-start.2 = (bf16[128,1024]{1,0:T(8,128)(2,1)}, bf16[128,1024]{1,0:T(8,128)(2,1)S(1)}, u32[]{:S(2)}, u32[]{:S(2)}) collective-permute-start(bf16[128,1024]{1,0:T(8,128)(2,1)} %bitcast.10), channel_id=1, source_target_pairs={{2,0},{0,2},{3,1},{1,3},{6,4},{4,6},{7,5},{5,7},{10,8},{8,10},{11,... | collective-permute-start | bytes 786440 | tf_op jit(solution)/shard_map/ppermute | solution.py:19
  7.1 1.3 %collective-permute-done.1.refs_3_ = bf16[32,128]{1,0:T(8,128)(2,1)S(1)} collective-permute-done((bf16[32,128]{1,0:T(8,128)(2,1)S(1)}, bf16[32,128]{1,0:T(8,128)(2,1)S(1)}, u32[]{:S(2)}, u32[]{:S(2)}) %collective-permute-start.1) | collective-permute-done | bytes 8224 | tf_op jit(solution)/shard_map/ppermute | solution.py:19
  8.4 0.8 %shard_map.87.elem_ref = f32[3,2,128,128]{3,2,1,0:T(8,128)S(1)} custom-call(bf16[576,128]{1,0:T(8,128)(2,1)S(1)} %get-tuple-element.21.early_ref, bf16[192,128]{1,0:T(8,128)(2,1)S(1)} %get-tuple-element.22.refs_0_, bf16[192,128]{1,0:T(8,128)(2,1)S(1)} %collective-permute-done.refs_1_, bf16[32,128]{1,0:T(8,128)(2,1)S(1)} %shard_map.85.links_ref.refs_2_, ...), custom_call_target="tpu_custom_call" | custom-call | flops 10000000000 | bytes 1048576 | tf_op jit(solution)/shard_map/pallas_call | solution.py:33
  9.3 0.9 %shard_map.88 = (bf16[512,512]{1,0:T(8,128)(2,1)S(1)}, bf16[128,1024]{1,0:T(8,128)(2,1)S(1)}, f32[128,1024]{1,0:T(8,128)S(1)}, bf16[128,1024]{1,0:T(8,128)(2,1)S(1)}) custom-call(s32[3]{0:T(128)S(1)} %copy-done.5, f32[3,2,128,128]{3,2,1,0:T(8,128)S(1)} %shard_map.87.elem_ref, bf16[128,1024]{1,0:T(8,128)(2,1)S(1)} %bitcast.11), custom_call_target="tpu_custom_call" | custom-call | flops 100000000 | bytes 1048576 | tf_op jit(solution)/shard_map/pallas_call | solution.py:33
  10.2 3.7 %collective-permute-start.6 = (bf16[128,1024]{1,0:T(8,128)(2,1)S(1)}, bf16[128,1024]{1,0:T(8,128)(2,1)S(1)}, u32[]{:S(2)}, u32[]{:S(2)}) collective-permute-start(bf16[128,1024]{1,0:T(8,128)(2,1)S(1)} %get-tuple-element.27.own_ref), channel_id=1, source_target_pairs={{4,0},{8,4},{12,8},{0,12},{5,1},{9,5},{13,9},{1,13},{6,2},{10,6},{... | collective-permute-start | bytes 786440 | tf_op jit(solution)/shard_map/ppermute | solution.py:19
  13.9 0.6 %collective-permute-start.5 = (bf16[64,1024]{1,0:T(8,128)(2,1)S(1)}, bf16[64,1024]{1,0:T(8,128)(2,1)S(1)}, u32[]{:S(2)}, u32[]{:S(2)}) collective-permute-start(bf16[64,1024]{1,0:T(8,128)(2,1)S(1)} %get-tuple-element.37), channel_id=1, source_target_pairs={{1,0},{0,1},{3,2},{2,3},{5,4},{4,5},{7,6},{6,7},{9,8},{8,9},{11,10... | collective-permute-start | bytes 393224 | tf_op jit(solution)/shard_map/ppermute | solution.py:19
  14.6 1.0 %collective-permute-done.5.refs_3_ = bf16[64,1024]{1,0:T(8,128)(2,1)S(1)} collective-permute-done((bf16[64,1024]{1,0:T(8,128)(2,1)S(1)}, bf16[64,1024]{1,0:T(8,128)(2,1)S(1)}, u32[]{:S(2)}, u32[]{:S(2)}) %collective-permute-start.5) | collective-permute-done | bytes 131104 | tf_op jit(solution)/shard_map/ppermute | solution.py:19
  15.9 0.6 %shard_map.89.first_ref = bf16[512,1024]{1,0:T(8,128)(2,1)S(1)} custom-call(bf16[512,512]{1,0:T(8,128)(2,1)S(1)} %get-tuple-element.23.oper_ref, bf16[128,1024]{1,0:T(8,128)(2,1)S(1)} %get-tuple-element.27.own_ref, bf16[128,1024]{1,0:T(8,128)(2,1)S(1)} %collective-permute-done.3.refs_0_, bf16[128,1024]{1,0:T(8,128)(2,1)S(1)} %collective-permute-done.2.refs_1_, ...), custom_call_target="tpu_custom_call" | custom-call | flops 1000000 | bytes 1048576 | tf_op jit(solution)/shard_map/pallas_call | solution.py:33
  16.4 1.5 %collective-permute-done.6.next_ref = bf16[128,1024]{1,0:T(8,128)(2,1)S(1)} collective-permute-done((bf16[128,1024]{1,0:T(8,128)(2,1)S(1)}, bf16[128,1024]{1,0:T(8,128)(2,1)S(1)}, u32[]{:S(2)}, u32[]{:S(2)}) %collective-permute-start.6) | collective-permute-done | bytes 262176 | tf_op jit(solution)/shard_map/ppermute | solution.py:19
  18.4 4.3 %collective-permute-start.7 = (bf16[128,1024]{1,0:T(8,128)(2,1)S(1)}, bf16[128,1024]{1,0:T(8,128)(2,1)S(1)}, u32[]{:S(2)}, u32[]{:S(2)}) collective-permute-start(bf16[128,1024]{1,0:T(8,128)(2,1)S(1)} %get-tuple-element.33), channel_id=1, source_target_pairs={{4,0},{8,4},{12,8},{0,12},{5,1},{9,5},{13,9},{1,13},{6,2},{10,6},{... | collective-permute-start | bytes 786440 | tf_op jit(solution)/shard_map/ppermute | solution.py:19
  22.7 0.7 %copy-done.3 = s32[4]{0:T(128)S(1)} copy-done((s32[4]{0:T(128)S(1)}, s32[4]{0:T(128)}, u32[]{:S(2)}) %copy-start.3) | copy-done | bytes 40
  23.4 1.6 %shard_map.91 = (bf16[128,1024]{1,0:T(8,128)(2,1)S(1)}, f32[8,128]{1,0:T(8,128)S(1)}, f32[64,3,2,64]{3,2,1,0:T(2,128)}, f32[8,128]{1,0:T(8,128)S(1)}) custom-call(s32[4]{0:T(128)S(1)} %copy-done.3, s32[1,16]{1,0:T(1,128)S(1)} %bitcast.15, bf16[512,1024]{1,0:T(8,128)(2,1)S(1)} %shard_map.89.first_ref, f32[3,2,128,128]{3,2,1,0:T(8,128)S(1)} %shard_map.87.elem_ref, ...), custom_call_target="tpu_custom_call" | custom-call | flops 1000000 | bytes 1048576 | tf_op jit(solution)/shard_map/pallas_call | solution.py:33
  25.0 1.6 %collective-permute-done.7.second_ref = bf16[128,1024]{1,0:T(8,128)(2,1)S(1)} collective-permute-done((bf16[128,1024]{1,0:T(8,128)(2,1)S(1)}, bf16[128,1024]{1,0:T(8,128)(2,1)S(1)}, u32[]{:S(2)}, u32[]{:S(2)}) %collective-permute-start.7) | collective-permute-done | bytes 262176 | tf_op jit(solution)/shard_map/ppermute | solution.py:19
  27.0 1.2 %collective-permute-start.9 = (f32[2,16]{1,0:T(2,128)S(1)}, f32[2,16]{1,0:T(2,128)S(1)}, u32[]{:S(2)}, u32[]{:S(2)}) collective-permute-start(f32[2,16]{1,0:T(2,128)S(1)} %shard_map.93), channel_id=1, source_target_pairs={{8,0},{9,1},{10,2},{11,3},{12,4},{13,5},{14,6},{15,7},{0,8},{1,9},... | collective-permute-start | bytes 392 | tf_op jit(solution)/shard_map/ppermute | solution.py:23
  28.2 1.6 %collective-permute-start.8 = (f32[2,16]{1,0:T(2,128)S(1)}, f32[2,16]{1,0:T(2,128)S(1)}, u32[]{:S(2)}, u32[]{:S(2)}) collective-permute-start(f32[2,16]{1,0:T(2,128)S(1)} %shard_map.93), channel_id=1, source_target_pairs={{1,0},{0,1},{3,2},{2,3},{5,4},{4,5},{7,6},{6,7},{9,8},{8,9},{11,10... | collective-permute-start | bytes 392 | tf_op jit(solution)/shard_map/ppermute | solution.py:23
  29.7 1.1 %shard_map.92 = bf16[128,1024]{1,0:T(8,128)(2,1)} custom-call(bf16[128,1024]{1,0:T(8,128)(2,1)S(1)} %collective-permute-done.7.second_ref, bf16[512,1024]{1,0:T(8,128)(2,1)S(1)} %shard_map.89.first_ref), custom_call_target="tpu_custom_call" | custom-call | flops 100000000 | bytes 1048576 | tf_op jit(solution)/shard_map/pallas_call | solution.py:33
  30.9 0.6 %collective-permute-done.9 = f32[2,16]{1,0:T(2,128)S(1)} collective-permute-done((f32[2,16]{1,0:T(2,128)S(1)}, f32[2,16]{1,0:T(2,128)S(1)}, u32[]{:S(2)}, u32[]{:S(2)}) %collective-permute-start.9) | collective-permute-done | bytes 160 | tf_op jit(solution)/shard_map/ppermute | solution.py:23
  31.5 2.1 %collective-permute-start.13 = (f32[2,16]{1,0:T(2,128)S(1)}, f32[2,16]{1,0:T(2,128)S(1)}, u32[]{:S(2)}, u32[]{:S(2)}) collective-permute-start(f32[2,16]{1,0:T(2,128)S(1)} %add_add_fusion), channel_id=1, source_target_pairs={{6,0},{7,1},{4,2},{5,3},{2,4},{3,5},{0,6},{1,7},{14,8},{15,9},{12,... | collective-permute-start | bytes 392 | tf_op jit(solution)/shard_map/ppermute | solution.py:23
  33.7 1.3 %collective-permute-start.11 = (f32[2,16]{1,0:T(2,128)S(1)}, f32[2,16]{1,0:T(2,128)S(1)}, u32[]{:S(2)}, u32[]{:S(2)}) collective-permute-start(f32[2,16]{1,0:T(2,128)S(1)} %add_add_fusion), channel_id=1, source_target_pairs={{2,0},{3,1},{0,2},{1,3},{6,4},{7,5},{4,6},{5,7},{10,8},{11,9},{8,1... | collective-permute-start | bytes 392 | tf_op jit(solution)/shard_map/ppermute | solution.py:23
  35.1 1.0 %collective-permute-done.13 = f32[2,16]{1,0:T(2,128)S(1)} collective-permute-done((f32[2,16]{1,0:T(2,128)S(1)}, f32[2,16]{1,0:T(2,128)S(1)}, u32[]{:S(2)}, u32[]{:S(2)}) %collective-permute-start.13) | collective-permute-done | bytes 160 | tf_op jit(solution)/shard_map/ppermute | solution.py:23
  36.0 1.2 %collective-permute-done.12 = f32[2,16]{1,0:T(2,128)S(1)} collective-permute-done((f32[2,16]{1,0:T(2,128)S(1)}, f32[2,16]{1,0:T(2,128)S(1)}, u32[]{:S(2)}, u32[]{:S(2)}) %collective-permute-start.12) | collective-permute-done | bytes 160 | tf_op jit(solution)/shard_map/ppermute | solution.py:23
  (28 shorter events, 2.7 us)
Async XLA Ops:
  0.6 7.7 %collective-permute-start = (bf16[192,128]{1,0:T(8,128)(2,1)}, bf16[192,128]{1,0:T(8,128)(2,1)S(1)}, u32[]{:S(2)}, u32[]{:S(2)}) collective-permute-start(bf16[192,128]{1,0:T(8,128)(2,1)} %bitcast.13), channel_id=1, source_target_pairs={{2,0},{0,2},{3,1},{1,3},{6,4},{4,6},{7,5},{5,7},{10,8},{8,10},{11,... | collective-permute-start | bytes 147464 | tf_op jit(solution)/shard_map/ppermute | solution.py:19
  3.6 0.8 %copy-start.1 = (bf16[1,3,2,3,3,8,4]{5,6,4,3,2,1,0:T(4,128)(2,1)S(1)}, bf16[1,3,2,3,3,8,4]{5,6,4,3,2,1,0:T(4,128)(2,1)}, u32[]{:S(2)}) copy-start(bf16[1,3,2,3,3,8,4]{5,6,4,3,2,1,0:T(4,128)(2,1)} %param.7) | copy-start | bytes 10372
  4.4 0.8 %copy-start.2 = (bf16[1,2,3,8,2,2,128]{6,5,4,3,2,1,0:T(2,128)(2,1)S(1)}, bf16[1,2,3,8,2,2,128]{6,5,4,3,2,1,0:T(2,128)(2,1)}, u32[]{:S(2)}) copy-start(bf16[1,2,3,8,2,2,128]{6,5,4,3,2,1,0:T(2,128)(2,1)} %param.6) | copy-start | bytes 147460
  4.6 3.8 %collective-permute-start.1 = (bf16[32,128]{1,0:T(8,128)(2,1)S(1)}, bf16[32,128]{1,0:T(8,128)(2,1)S(1)}, u32[]{:S(2)}, u32[]{:S(2)}) collective-permute-start(bf16[32,128]{1,0:T(8,128)(2,1)S(1)} %shard_map.85.links_ref.refs_2_), channel_id=1, source_target_pairs={{2,0},{0,2},{3,1},{1,3},{6,4},{4,6},{7,5},{5,7},{10,8},{8,10},{11,... | collective-permute-start | bytes 24584 | tf_op jit(solution)/shard_map/ppermute | solution.py:19
  5.6 8.3 %collective-permute-start.2 = (bf16[128,1024]{1,0:T(8,128)(2,1)}, bf16[128,1024]{1,0:T(8,128)(2,1)S(1)}, u32[]{:S(2)}, u32[]{:S(2)}) collective-permute-start(bf16[128,1024]{1,0:T(8,128)(2,1)} %bitcast.10), channel_id=1, source_target_pairs={{2,0},{0,2},{3,1},{1,3},{6,4},{4,6},{7,5},{5,7},{10,8},{8,10},{11,... | collective-permute-start | bytes 786440 | tf_op jit(solution)/shard_map/ppermute | solution.py:19
  8.4 1.0 %copy-start = (bf16[1,128,1024]{2,1,0:T(8,128)(2,1)S(1)}, bf16[1,128,1024]{2,1,0:T(8,128)(2,1)}, u32[]{:S(2)}) copy-start(bf16[1,128,1024]{2,1,0:T(8,128)(2,1)} %param.8) | copy-start | bytes 786436
  8.4 1.0 %copy-start.5 = (s32[3]{0:T(128)S(1)}, s32[3]{0:T(128)}, u32[]{:S(2)}) copy-start(s32[3]{0:T(128)} %dirs_ref.1) | copy-start | bytes 40
  10.2 7.7 %collective-permute-start.6 = (bf16[128,1024]{1,0:T(8,128)(2,1)S(1)}, bf16[128,1024]{1,0:T(8,128)(2,1)S(1)}, u32[]{:S(2)}, u32[]{:S(2)}) collective-permute-start(bf16[128,1024]{1,0:T(8,128)(2,1)S(1)} %get-tuple-element.27.own_ref), channel_id=1, source_target_pairs={{4,0},{8,4},{12,8},{0,12},{5,1},{9,5},{13,9},{1,13},{6,2},{10,6},{... | collective-permute-start | bytes 786440 | tf_op jit(solution)/shard_map/ppermute | solution.py:19
  13.9 1.9 %collective-permute-start.3 = (bf16[128,1024]{1,0:T(8,128)(2,1)S(1)}, bf16[128,1024]{1,0:T(8,128)(2,1)S(1)}, u32[]{:S(2)}, u32[]{:S(2)}) collective-permute-start(bf16[128,1024]{1,0:T(8,128)(2,1)S(1)} %get-tuple-element.28), channel_id=1, source_target_pairs={{1,0},{0,1},{3,2},{2,3},{5,4},{4,5},{7,6},{6,7},{9,8},{8,9},{11,10... | collective-permute-start | bytes 786440 | tf_op jit(solution)/shard_map/ppermute | solution.py:19
  13.9 1.7 %collective-permute-start.5 = (bf16[64,1024]{1,0:T(8,128)(2,1)S(1)}, bf16[64,1024]{1,0:T(8,128)(2,1)S(1)}, u32[]{:S(2)}, u32[]{:S(2)}) collective-permute-start(bf16[64,1024]{1,0:T(8,128)(2,1)S(1)} %get-tuple-element.37), channel_id=1, source_target_pairs={{1,0},{0,1},{3,2},{2,3},{5,4},{4,5},{7,6},{6,7},{9,8},{8,9},{11,10... | collective-permute-start | bytes 393224 | tf_op jit(solution)/shard_map/ppermute | solution.py:19
  14.5 1.3 %collective-permute-start.4 = (bf16[64,1024]{1,0:T(8,128)(2,1)S(1)}, bf16[64,1024]{1,0:T(8,128)(2,1)S(1)}, u32[]{:S(2)}, u32[]{:S(2)}) collective-permute-start(bf16[64,1024]{1,0:T(8,128)(2,1)S(1)} %get-tuple-element.38), channel_id=1, source_target_pairs={{1,0},{0,1},{3,2},{2,3},{5,4},{4,5},{7,6},{6,7},{9,8},{8,9},{11,10... | collective-permute-start | bytes 393224 | tf_op jit(solution)/shard_map/ppermute | solution.py:19
  18.4 8.2 %collective-permute-start.7 = (bf16[128,1024]{1,0:T(8,128)(2,1)S(1)}, bf16[128,1024]{1,0:T(8,128)(2,1)S(1)}, u32[]{:S(2)}, u32[]{:S(2)}) collective-permute-start(bf16[128,1024]{1,0:T(8,128)(2,1)S(1)} %get-tuple-element.33), channel_id=1, source_target_pairs={{4,0},{8,4},{12,8},{0,12},{5,1},{9,5},{13,9},{1,13},{6,2},{10,6},{... | collective-permute-start | bytes 786440 | tf_op jit(solution)/shard_map/ppermute | solution.py:19
  22.7 0.7 %copy-start.3 = (s32[4]{0:T(128)S(1)}, s32[4]{0:T(128)}, u32[]{:S(2)}) copy-start(s32[4]{0:T(128)} %offsets_ref.1) | copy-start | bytes 52
  22.7 0.7 %copy-start.4 = (s32[16]{0:T(128)S(1)}, s32[16]{0:T(128)}, u32[]{:S(2)}) copy-start(s32[16]{0:T(128)} %param.9) | copy-start | bytes 196
  27.0 3.9 %collective-permute-start.10 = (f32[2,16]{1,0:T(2,128)S(1)}, f32[2,16]{1,0:T(2,128)S(1)}, u32[]{:S(2)}, u32[]{:S(2)}) collective-permute-start(f32[2,16]{1,0:T(2,128)S(1)} %shard_map.93), channel_id=1, source_target_pairs={{9,0},{8,1},{11,2},{10,3},{13,4},{12,5},{15,6},{14,7},{1,8},{0,9},... | collective-permute-start | bytes 392 | tf_op jit(solution)/shard_map/ppermute | solution.py:23
  27.0 4.5 %collective-permute-start.9 = (f32[2,16]{1,0:T(2,128)S(1)}, f32[2,16]{1,0:T(2,128)S(1)}, u32[]{:S(2)}, u32[]{:S(2)}) collective-permute-start(f32[2,16]{1,0:T(2,128)S(1)} %shard_map.93), channel_id=1, source_target_pairs={{8,0},{9,1},{10,2},{11,3},{12,4},{13,5},{14,6},{15,7},{0,8},{1,9},... | collective-permute-start | bytes 392 | tf_op jit(solution)/shard_map/ppermute | solution.py:23
  28.2 3.3 %collective-permute-start.8 = (f32[2,16]{1,0:T(2,128)S(1)}, f32[2,16]{1,0:T(2,128)S(1)}, u32[]{:S(2)}, u32[]{:S(2)}) collective-permute-start(f32[2,16]{1,0:T(2,128)S(1)} %shard_map.93), channel_id=1, source_target_pairs={{1,0},{0,1},{3,2},{2,3},{5,4},{4,5},{7,6},{6,7},{9,8},{8,9},{11,10... | collective-permute-start | bytes 392 | tf_op jit(solution)/shard_map/ppermute | solution.py:23
  31.5 4.5 %collective-permute-start.13 = (f32[2,16]{1,0:T(2,128)S(1)}, f32[2,16]{1,0:T(2,128)S(1)}, u32[]{:S(2)}, u32[]{:S(2)}) collective-permute-start(f32[2,16]{1,0:T(2,128)S(1)} %add_add_fusion), channel_id=1, source_target_pairs={{6,0},{7,1},{4,2},{5,3},{2,4},{3,5},{0,6},{1,7},{14,8},{15,9},{12,... | collective-permute-start | bytes 392 | tf_op jit(solution)/shard_map/ppermute | solution.py:23
  33.6 3.6 %collective-permute-start.12 = (f32[2,16]{1,0:T(2,128)S(1)}, f32[2,16]{1,0:T(2,128)S(1)}, u32[]{:S(2)}, u32[]{:S(2)}) collective-permute-start(f32[2,16]{1,0:T(2,128)S(1)} %add_add_fusion), channel_id=1, source_target_pairs={{4,0},{5,1},{6,2},{7,3},{0,4},{1,5},{2,6},{3,7},{12,8},{13,9},{14,... | collective-permute-start | bytes 392 | tf_op jit(solution)/shard_map/ppermute | solution.py:23
  33.7 3.6 %collective-permute-start.11 = (f32[2,16]{1,0:T(2,128)S(1)}, f32[2,16]{1,0:T(2,128)S(1)}, u32[]{:S(2)}, u32[]{:S(2)}) collective-permute-start(f32[2,16]{1,0:T(2,128)S(1)} %add_add_fusion), channel_id=1, source_target_pairs={{2,0},{3,1},{0,2},{1,3},{6,4},{7,5},{4,6},{5,7},{10,8},{11,9},{8,1... | collective-permute-start | bytes 392 | tf_op jit(solution)/shard_map/ppermute | solution.py:23

commit v6 on v5

--- a/solution.py
+++ b/solution.py
@@ -360,7 +360,7 @@
         links_kernel,
         jax.ShapeDtypeStruct((cells, modes), BF16),
         [pltpu.VMEM(link.shape, F32), pltpu.VMEM((cells, modes), F32)],
-        10**6,
+        10**9,
     )(link)
     links = [link] + [from_offset(link, "space", step) for step in range(1, spaces)]
     fields[0], own_slab = vmem_call(

time: 38.1 us -> 37.9 us (level)
  no operation moved by 1% of the time
where the time goes in v6:
time: 37.9 us; the launch traced here: 37.7 us
  starting transfers between devices  19.4 us (51%)
  waiting for transfers between devices  8.44 us (22%)
  Pallas kernels  6.39 us (17%)
  local copies, waits for them, and re-layouts  2.13 us (6%)
  between operations  0.71 us (2%)
  other arithmetic  0.57 us (2%)
    ppermute x8, starting transfers between devices, from_offset(): lax.ppermute(block, axis, [((i + distance) % count, i) for i in range(cou...  13.1 us
    pallas_call x9, Pallas kernels, call(): pl.pallas_call(kernel, out_shape=out_shape, in_specs=specs, out_specs=out...  6.39 us
    ppermute x6, starting transfers between devices, swapped(): lax.ppermute(block, ('tm', 'space', 'spin'), [(i ^ mask, i) for i in rang...  6.31 us
    ppermute x8, waiting for transfers between devices, from_offset(): lax.ppermute(block, axis, [((i + distance) % count, i) for i in range(cou...  5.63 us
    ppermute x6, waiting for transfers between devices, swapped(): lax.ppermute(block, ('tm', 'space', 'spin'), [(i ^ mask, i) for i in rang...  2.81 us
    unnamed x12, local copies, waits for them, and re-layouts  2.11 us
  transfers between devices with their start and end apart: 14, of which 9 were waited for; matrix products, arithmetic and copies ran while one was open for 0% of the time, Pallas kernels for 15%

profile of v6, /device:TPU:0, one launch (start us, length us, event | category | flops | bytes accessed | tf_op | source)
XLA Modules:
  0.0 37.7 jit_solution(9222333406847987583)
XLA Ops:
  0.6 3.0 %collective-permute-start = (bf16[192,128]{1,0:T(8,128)(2,1)}, bf16[192,128]{1,0:T(8,128)(2,1)S(1)}, u32[]{:S(2)}, u32[]{:S(2)}) collective-permute-start(bf16[192,128]{1,0:T(8,128)(2,1)} %bitcast.12), channel_id=1, source_target_pairs={{2,0},{0,2},{3,1},{1,3},{6,4},{4,6},{7,5},{5,7},{10,8},{8,10},{11,... | collective-permute-start | bytes 147464 | tf_op jit(solution)/shard_map/ppermute | solution.py:19
  3.6 0.8 %copy-done.5 = bf16[1,3,2,3,3,8,4]{5,6,4,3,2,1,0:T(4,128)(2,1)S(1)} copy-done((bf16[1,3,2,3,3,8,4]{5,6,4,3,2,1,0:T(4,128)(2,1)S(1)}, bf16[1,3,2,3,3,8,4]{5,6,4,3,2,1,0:T(4,128)(2,1)}, u32[]{:S(2)}) %copy-start.5) | copy-done | bytes 3480
  4.6 0.6 %copy-done.1 = bf16[1,2,3,8,2,2,128]{6,5,4,3,2,1,0:T(2,128)(2,1)S(1)} copy-done((bf16[1,2,3,8,2,2,128]{6,5,4,3,2,1,0:T(2,128)(2,1)S(1)}, bf16[1,2,3,8,2,2,128]{6,5,4,3,2,1,0:T(2,128)(2,1)}, u32[]{:S(2)}) %copy-start.1) | copy-done | bytes 49176
  5.6 1.5 %collective-permute-start.2 = (bf16[128,1024]{1,0:T(8,128)(2,1)S(1)}, bf16[128,1024]{1,0:T(8,128)(2,1)S(1)}, u32[]{:S(2)}, u32[]{:S(2)}) collective-permute-start(bf16[128,1024]{1,0:T(8,128)(2,1)S(1)} %bitcast.10), channel_id=1, source_target_pairs={{2,0},{0,2},{3,1},{1,3},{6,4},{4,6},{7,5},{5,7},{10,8},{8,10},{11,... | collective-permute-start | bytes 786440 | tf_op jit(solution)/shard_map/ppermute | solution.py:19
  7.1 1.3 %collective-permute-done.1.refs_3_ = bf16[32,128]{1,0:T(8,128)(2,1)S(1)} collective-permute-done((bf16[32,128]{1,0:T(8,128)(2,1)S(1)}, bf16[32,128]{1,0:T(8,128)(2,1)S(1)}, u32[]{:S(2)}, u32[]{:S(2)}) %collective-permute-start.1) | collective-permute-done | bytes 8224 | tf_op jit(solution)/shard_map/ppermute | solution.py:19
  8.4 0.8 %shard_map.87.elem_ref = f32[3,2,128,128]{3,2,1,0:T(8,128)S(1)} custom-call(bf16[576,128]{1,0:T(8,128)(2,1)S(1)} %get-tuple-element.21.early_ref, bf16[192,128]{1,0:T(8,128)(2,1)S(1)} %get-tuple-element.22.refs_0_, bf16[192,128]{1,0:T(8,128)(2,1)S(1)} %collective-permute-done.refs_1_, bf16[32,128]{1,0:T(8,128)(2,1)S(1)} %shard_map.85.links_ref.refs_2_, ...), custom_call_target="tpu_custom_call" | custom-call | flops 10000000000 | bytes 1048576 | tf_op jit(solution)/shard_map/pallas_call | solution.py:33
  9.2 0.9 %shard_map.88 = (bf16[512,512]{1,0:T(8,128)(2,1)S(1)}, bf16[128,1024]{1,0:T(8,128)(2,1)S(1)}, f32[128,1024]{1,0:T(8,128)S(1)}, bf16[128,1024]{1,0:T(8,128)(2,1)S(1)}) custom-call(s32[3]{0:T(128)S(1)} %copy-done.4, f32[3,2,128,128]{3,2,1,0:T(8,128)S(1)} %shard_map.87.elem_ref, bf16[128,1024]{1,0:T(8,128)(2,1)S(1)} %bitcast.11), custom_call_target="tpu_custom_call" | custom-call | flops 100000000 | bytes 1048576 | tf_op jit(solution)/shard_map/pallas_call | solution.py:33
  10.1 3.7 %collective-permute-start.6 = (bf16[128,1024]{1,0:T(8,128)(2,1)S(1)}, bf16[128,1024]{1,0:T(8,128)(2,1)S(1)}, u32[]{:S(2)}, u32[]{:S(2)}) collective-permute-start(bf16[128,1024]{1,0:T(8,128)(2,1)S(1)} %get-tuple-element.27.own_ref), channel_id=1, source_target_pairs={{4,0},{8,4},{12,8},{0,12},{5,1},{9,5},{13,9},{1,13},{6,2},{10,6},{... | collective-permute-start | bytes 786440 | tf_op jit(solution)/shard_map/ppermute | solution.py:19
  13.8 0.6 %collective-permute-start.5 = (bf16[64,1024]{1,0:T(8,128)(2,1)S(1)}, bf16[64,1024]{1,0:T(8,128)(2,1)S(1)}, u32[]{:S(2)}, u32[]{:S(2)}) collective-permute-start(bf16[64,1024]{1,0:T(8,128)(2,1)S(1)} %get-tuple-element.37), channel_id=1, source_target_pairs={{1,0},{0,1},{3,2},{2,3},{5,4},{4,5},{7,6},{6,7},{9,8},{8,9},{11,10... | collective-permute-start | bytes 393224 | tf_op jit(solution)/shard_map/ppermute | solution.py:19
  14.4 1.0 %collective-permute-done.5.refs_3_ = bf16[64,1024]{1,0:T(8,128)(2,1)S(1)} collective-permute-done((bf16[64,1024]{1,0:T(8,128)(2,1)S(1)}, bf16[64,1024]{1,0:T(8,128)(2,1)S(1)}, u32[]{:S(2)}, u32[]{:S(2)}) %collective-permute-start.5) | collective-permute-done | bytes 131104 | tf_op jit(solution)/shard_map/ppermute | solution.py:19
  15.7 0.6 %shard_map.89.first_ref = bf16[512,1024]{1,0:T(8,128)(2,1)S(1)} custom-call(bf16[512,512]{1,0:T(8,128)(2,1)S(1)} %get-tuple-element.23.oper_ref, bf16[128,1024]{1,0:T(8,128)(2,1)S(1)} %get-tuple-element.27.own_ref, bf16[128,1024]{1,0:T(8,128)(2,1)S(1)} %collective-permute-done.3.refs_0_, bf16[128,1024]{1,0:T(8,128)(2,1)S(1)} %collective-permute-done.2.refs_1_, ...), custom_call_target="tpu_custom_call" | custom-call | flops 1000000 | bytes 1048576 | tf_op jit(solution)/shard_map/pallas_call | solution.py:33
  16.3 1.5 %collective-permute-done.6.next_ref = bf16[128,1024]{1,0:T(8,128)(2,1)S(1)} collective-permute-done((bf16[128,1024]{1,0:T(8,128)(2,1)S(1)}, bf16[128,1024]{1,0:T(8,128)(2,1)S(1)}, u32[]{:S(2)}, u32[]{:S(2)}) %collective-permute-start.6) | collective-permute-done | bytes 262176 | tf_op jit(solution)/shard_map/ppermute | solution.py:19
  18.2 4.3 %collective-permute-start.7 = (bf16[128,1024]{1,0:T(8,128)(2,1)S(1)}, bf16[128,1024]{1,0:T(8,128)(2,1)S(1)}, u32[]{:S(2)}, u32[]{:S(2)}) collective-permute-start(bf16[128,1024]{1,0:T(8,128)(2,1)S(1)} %get-tuple-element.33), channel_id=1, source_target_pairs={{4,0},{8,4},{12,8},{0,12},{5,1},{9,5},{13,9},{1,13},{6,2},{10,6},{... | collective-permute-start | bytes 786440 | tf_op jit(solution)/shard_map/ppermute | solution.py:19
  22.6 0.7 %copy-done.2 = s32[4]{0:T(128)S(1)} copy-done((s32[4]{0:T(128)S(1)}, s32[4]{0:T(128)}, u32[]{:S(2)}) %copy-start.2) | copy-done | bytes 40
  23.2 1.6 %shard_map.91 = (bf16[128,1024]{1,0:T(8,128)(2,1)S(1)}, f32[8,128]{1,0:T(8,128)S(1)}, f32[64,3,2,64]{3,2,1,0:T(2,128)}, f32[8,128]{1,0:T(8,128)S(1)}) custom-call(s32[4]{0:T(128)S(1)} %copy-done.2, s32[1,16]{1,0:T(1,128)S(1)} %bitcast.14, bf16[512,1024]{1,0:T(8,128)(2,1)S(1)} %shard_map.89.first_ref, f32[3,2,128,128]{3,2,1,0:T(8,128)S(1)} %shard_map.87.elem_ref, ...), custom_call_target="tpu_custom_call" | custom-call | flops 1000000 | bytes 1048576 | tf_op jit(solution)/shard_map/pallas_call | solution.py:33
  24.9 1.6 %collective-permute-done.7.second_ref = bf16[128,1024]{1,0:T(8,128)(2,1)S(1)} collective-permute-done((bf16[128,1024]{1,0:T(8,128)(2,1)S(1)}, bf16[128,1024]{1,0:T(8,128)(2,1)S(1)}, u32[]{:S(2)}, u32[]{:S(2)}) %collective-permute-start.7) | collective-permute-done | bytes 262176 | tf_op jit(solution)/shard_map/ppermute | solution.py:19
  26.8 1.1 %collective-permute-start.9 = (f32[2,16]{1,0:T(2,128)S(1)}, f32[2,16]{1,0:T(2,128)S(1)}, u32[]{:S(2)}, u32[]{:S(2)}) collective-permute-start(f32[2,16]{1,0:T(2,128)S(1)} %shard_map.93), channel_id=1, source_target_pairs={{8,0},{9,1},{10,2},{11,3},{12,4},{13,5},{14,6},{15,7},{0,8},{1,9},... | collective-permute-start | bytes 392 | tf_op jit(solution)/shard_map/ppermute | solution.py:23
  28.0 1.6 %collective-permute-start.8 = (f32[2,16]{1,0:T(2,128)S(1)}, f32[2,16]{1,0:T(2,128)S(1)}, u32[]{:S(2)}, u32[]{:S(2)}) collective-permute-start(f32[2,16]{1,0:T(2,128)S(1)} %shard_map.93), channel_id=1, source_target_pairs={{1,0},{0,1},{3,2},{2,3},{5,4},{4,5},{7,6},{6,7},{9,8},{8,9},{11,10... | collective-permute-start | bytes 392 | tf_op jit(solution)/shard_map/ppermute | solution.py:23
  29.6 1.1 %shard_map.92 = bf16[128,1024]{1,0:T(8,128)(2,1)} custom-call(bf16[128,1024]{1,0:T(8,128)(2,1)S(1)} %collective-permute-done.7.second_ref, bf16[512,1024]{1,0:T(8,128)(2,1)S(1)} %shard_map.89.first_ref), custom_call_target="tpu_custom_call" | custom-call | flops 100000000 | bytes 1048576 | tf_op jit(solution)/shard_map/pallas_call | solution.py:33
  30.7 0.6 %collective-permute-done.9 = f32[2,16]{1,0:T(2,128)S(1)} collective-permute-done((f32[2,16]{1,0:T(2,128)S(1)}, f32[2,16]{1,0:T(2,128)S(1)}, u32[]{:S(2)}, u32[]{:S(2)}) %collective-permute-start.9) | collective-permute-done | bytes 160 | tf_op jit(solution)/shard_map/ppermute | solution.py:23
  31.3 2.1 %collective-permute-start.13 = (f32[2,16]{1,0:T(2,128)S(1)}, f32[2,16]{1,0:T(2,128)S(1)}, u32[]{:S(2)}, u32[]{:S(2)}) collective-permute-start(f32[2,16]{1,0:T(2,128)S(1)} %add_add_fusion), channel_id=1, source_target_pairs={{6,0},{7,1},{4,2},{5,3},{2,4},{3,5},{0,6},{1,7},{14,8},{15,9},{12,... | collective-permute-start | bytes 392 | tf_op jit(solution)/shard_map/ppermute | solution.py:23
  33.5 1.4 %collective-permute-start.11 = (f32[2,16]{1,0:T(2,128)S(1)}, f32[2,16]{1,0:T(2,128)S(1)}, u32[]{:S(2)}, u32[]{:S(2)}) collective-permute-start(f32[2,16]{1,0:T(2,128)S(1)} %add_add_fusion), channel_id=1, source_target_pairs={{2,0},{3,1},{0,2},{1,3},{6,4},{7,5},{4,6},{5,7},{10,8},{11,9},{8,1... | collective-permute-start | bytes 392 | tf_op jit(solution)/shard_map/ppermute | solution.py:23
  34.9 1.0 %collective-permute-done.13 = f32[2,16]{1,0:T(2,128)S(1)} collective-permute-done((f32[2,16]{1,0:T(2,128)S(1)}, f32[2,16]{1,0:T(2,128)S(1)}, u32[]{:S(2)}, u32[]{:S(2)}) %collective-permute-start.13) | collective-permute-done | bytes 160 | tf_op jit(solution)/shard_map/ppermute | solution.py:23
  35.9 1.1 %collective-permute-done.12 = f32[2,16]{1,0:T(2,128)S(1)} collective-permute-done((f32[2,16]{1,0:T(2,128)S(1)}, f32[2,16]{1,0:T(2,128)S(1)}, u32[]{:S(2)}, u32[]{:S(2)}) %collective-permute-start.12) | collective-permute-done | bytes 160 | tf_op jit(solution)/shard_map/ppermute | solution.py:23
  (28 shorter events, 2.5 us)
Async XLA Ops:
  0.6 7.7 %collective-permute-start = (bf16[192,128]{1,0:T(8,128)(2,1)}, bf16[192,128]{1,0:T(8,128)(2,1)S(1)}, u32[]{:S(2)}, u32[]{:S(2)}) collective-permute-start(bf16[192,128]{1,0:T(8,128)(2,1)} %bitcast.12), channel_id=1, source_target_pairs={{2,0},{0,2},{3,1},{1,3},{6,4},{4,6},{7,5},{5,7},{10,8},{8,10},{11,... | collective-permute-start | bytes 147464 | tf_op jit(solution)/shard_map/ppermute | solution.py:19
  3.6 0.8 %copy-start.5 = (bf16[1,3,2,3,3,8,4]{5,6,4,3,2,1,0:T(4,128)(2,1)S(1)}, bf16[1,3,2,3,3,8,4]{5,6,4,3,2,1,0:T(4,128)(2,1)}, u32[]{:S(2)}) copy-start(bf16[1,3,2,3,3,8,4]{5,6,4,3,2,1,0:T(4,128)(2,1)} %param.7) | copy-start | bytes 10372
  4.4 0.8 %copy-start.1 = (bf16[1,2,3,8,2,2,128]{6,5,4,3,2,1,0:T(2,128)(2,1)S(1)}, bf16[1,2,3,8,2,2,128]{6,5,4,3,2,1,0:T(2,128)(2,1)}, u32[]{:S(2)}) copy-start(bf16[1,2,3,8,2,2,128]{6,5,4,3,2,1,0:T(2,128)(2,1)} %param.6) | copy-start | bytes 147460
  4.5 1.2 %copy-start = (bf16[1,128,1024]{2,1,0:T(8,128)(2,1)S(1)}, bf16[1,128,1024]{2,1,0:T(8,128)(2,1)}, u32[]{:S(2)}) copy-start(bf16[1,128,1024]{2,1,0:T(8,128)(2,1)} %param.8) | copy-start | bytes 786436
  4.6 3.8 %collective-permute-start.1 = (bf16[32,128]{1,0:T(8,128)(2,1)S(1)}, bf16[32,128]{1,0:T(8,128)(2,1)S(1)}, u32[]{:S(2)}, u32[]{:S(2)}) collective-permute-start(bf16[32,128]{1,0:T(8,128)(2,1)S(1)} %shard_map.85.links_ref.refs_2_), channel_id=1, source_target_pairs={{2,0},{0,2},{3,1},{1,3},{6,4},{4,6},{7,5},{5,7},{10,8},{8,10},{11,... | collective-permute-start | bytes 24584 | tf_op jit(solution)/shard_map/ppermute | solution.py:19
  5.6 8.1 %collective-permute-start.2 = (bf16[128,1024]{1,0:T(8,128)(2,1)S(1)}, bf16[128,1024]{1,0:T(8,128)(2,1)S(1)}, u32[]{:S(2)}, u32[]{:S(2)}) collective-permute-start(bf16[128,1024]{1,0:T(8,128)(2,1)S(1)} %bitcast.10), channel_id=1, source_target_pairs={{2,0},{0,2},{3,1},{1,3},{6,4},{4,6},{7,5},{5,7},{10,8},{8,10},{11,... | collective-permute-start | bytes 786440 | tf_op jit(solution)/shard_map/ppermute | solution.py:19
  8.4 0.8 %copy-start.4 = (s32[3]{0:T(128)S(1)}, s32[3]{0:T(128)}, u32[]{:S(2)}) copy-start(s32[3]{0:T(128)} %dirs_ref.1) | copy-start | bytes 40
  10.1 7.7 %collective-permute-start.6 = (bf16[128,1024]{1,0:T(8,128)(2,1)S(1)}, bf16[128,1024]{1,0:T(8,128)(2,1)S(1)}, u32[]{:S(2)}, u32[]{:S(2)}) collective-permute-start(bf16[128,1024]{1,0:T(8,128)(2,1)S(1)} %get-tuple-element.27.own_ref), channel_id=1, source_target_pairs={{4,0},{8,4},{12,8},{0,12},{5,1},{9,5},{13,9},{1,13},{6,2},{10,6},{... | collective-permute-start | bytes 786440 | tf_op jit(solution)/shard_map/ppermute | solution.py:19
  13.7 1.9 %collective-permute-start.3 = (bf16[128,1024]{1,0:T(8,128)(2,1)S(1)}, bf16[128,1024]{1,0:T(8,128)(2,1)S(1)}, u32[]{:S(2)}, u32[]{:S(2)}) collective-permute-start(bf16[128,1024]{1,0:T(8,128)(2,1)S(1)} %get-tuple-element.28), channel_id=1, source_target_pairs={{1,0},{0,1},{3,2},{2,3},{5,4},{4,5},{7,6},{6,7},{9,8},{8,9},{11,10... | collective-permute-start | bytes 786440 | tf_op jit(solution)/shard_map/ppermute | solution.py:19
  13.8 1.7 %collective-permute-start.5 = (bf16[64,1024]{1,0:T(8,128)(2,1)S(1)}, bf16[64,1024]{1,0:T(8,128)(2,1)S(1)}, u32[]{:S(2)}, u32[]{:S(2)}) collective-permute-start(bf16[64,1024]{1,0:T(8,128)(2,1)S(1)} %get-tuple-element.37), channel_id=1, source_target_pairs={{1,0},{0,1},{3,2},{2,3},{5,4},{4,5},{7,6},{6,7},{9,8},{8,9},{11,10... | collective-permute-start | bytes 393224 | tf_op jit(solution)/shard_map/ppermute | solution.py:19
  14.3 1.3 %collective-permute-start.4 = (bf16[64,1024]{1,0:T(8,128)(2,1)S(1)}, bf16[64,1024]{1,0:T(8,128)(2,1)S(1)}, u32[]{:S(2)}, u32[]{:S(2)}) collective-permute-start(bf16[64,1024]{1,0:T(8,128)(2,1)S(1)} %get-tuple-element.38), channel_id=1, source_target_pairs={{1,0},{0,1},{3,2},{2,3},{5,4},{4,5},{7,6},{6,7},{9,8},{8,9},{11,10... | collective-permute-start | bytes 393224 | tf_op jit(solution)/shard_map/ppermute | solution.py:19
  18.2 8.2 %collective-permute-start.7 = (bf16[128,1024]{1,0:T(8,128)(2,1)S(1)}, bf16[128,1024]{1,0:T(8,128)(2,1)S(1)}, u32[]{:S(2)}, u32[]{:S(2)}) collective-permute-start(bf16[128,1024]{1,0:T(8,128)(2,1)S(1)} %get-tuple-element.33), channel_id=1, source_target_pairs={{4,0},{8,4},{12,8},{0,12},{5,1},{9,5},{13,9},{1,13},{6,2},{10,6},{... | collective-permute-start | bytes 786440 | tf_op jit(solution)/shard_map/ppermute | solution.py:19
  22.6 0.7 %copy-start.2 = (s32[4]{0:T(128)S(1)}, s32[4]{0:T(128)}, u32[]{:S(2)}) copy-start(s32[4]{0:T(128)} %offsets_ref.1) | copy-start | bytes 52
  22.6 0.7 %copy-start.3 = (s32[16]{0:T(128)S(1)}, s32[16]{0:T(128)}, u32[]{:S(2)}) copy-start(s32[16]{0:T(128)} %param.9) | copy-start | bytes 196
  26.8 3.9 %collective-permute-start.10 = (f32[2,16]{1,0:T(2,128)S(1)}, f32[2,16]{1,0:T(2,128)S(1)}, u32[]{:S(2)}, u32[]{:S(2)}) collective-permute-start(f32[2,16]{1,0:T(2,128)S(1)} %shard_map.93), channel_id=1, source_target_pairs={{9,0},{8,1},{11,2},{10,3},{13,4},{12,5},{15,6},{14,7},{1,8},{0,9},... | collective-permute-start | bytes 392 | tf_op jit(solution)/shard_map/ppermute | solution.py:23
  26.8 4.5 %collective-permute-start.9 = (f32[2,16]{1,0:T(2,128)S(1)}, f32[2,16]{1,0:T(2,128)S(1)}, u32[]{:S(2)}, u32[]{:S(2)}) collective-permute-start(f32[2,16]{1,0:T(2,128)S(1)} %shard_map.93), channel_id=1, source_target_pairs={{8,0},{9,1},{10,2},{11,3},{12,4},{13,5},{14,6},{15,7},{0,8},{1,9},... | collective-permute-start | bytes 392 | tf_op jit(solution)/shard_map/ppermute | solution.py:23
  28.0 3.4 %collective-permute-start.8 = (f32[2,16]{1,0:T(2,128)S(1)}, f32[2,16]{1,0:T(2,128)S(1)}, u32[]{:S(2)}, u32[]{:S(2)}) collective-permute-start(f32[2,16]{1,0:T(2,128)S(1)} %shard_map.93), channel_id=1, source_target_pairs={{1,0},{0,1},{3,2},{2,3},{5,4},{4,5},{7,6},{6,7},{9,8},{8,9},{11,10... | collective-permute-start | bytes 392 | tf_op jit(solution)/shard_map/ppermute | solution.py:23
  31.3 4.5 %collective-permute-start.13 = (f32[2,16]{1,0:T(2,128)S(1)}, f32[2,16]{1,0:T(2,128)S(1)}, u32[]{:S(2)}, u32[]{:S(2)}) collective-permute-start(f32[2,16]{1,0:T(2,128)S(1)} %add_add_fusion), channel_id=1, source_target_pairs={{6,0},{7,1},{4,2},{5,3},{2,4},{3,5},{0,6},{1,7},{14,8},{15,9},{12,... | collective-permute-start | bytes 392 | tf_op jit(solution)/shard_map/ppermute | solution.py:23
  33.4 3.6 %collective-permute-start.12 = (f32[2,16]{1,0:T(2,128)S(1)}, f32[2,16]{1,0:T(2,128)S(1)}, u32[]{:S(2)}, u32[]{:S(2)}) collective-permute-start(f32[2,16]{1,0:T(2,128)S(1)} %add_add_fusion), channel_id=1, source_target_pairs={{4,0},{5,1},{6,2},{7,3},{0,4},{1,5},{2,6},{3,7},{12,8},{13,9},{14,... | collective-permute-start | bytes 392 | tf_op jit(solution)/shard_map/ppermute | solution.py:23
  33.5 3.6 %collective-permute-start.11 = (f32[2,16]{1,0:T(2,128)S(1)}, f32[2,16]{1,0:T(2,128)S(1)}, u32[]{:S(2)}, u32[]{:S(2)}) collective-permute-start(f32[2,16]{1,0:T(2,128)S(1)} %add_add_fusion), channel_id=1, source_target_pairs={{2,0},{3,1},{0,2},{1,3},{6,4},{7,5},{4,6},{5,7},{10,8},{11,9},{8,1... | collective-permute-start | bytes 392 | tf_op jit(solution)/shard_map/ppermute | solution.py:23

commit v7 on v6

--- a/solution.py
+++ b/solution.py
@@ -185,10 +185,9 @@
 
 
 def operator_kernel(
-    dirs_ref, elem_ref, rows_ref, oper_ref, first_ref, wide_ref, copy_ref
+    dirs_ref, elem_ref, rows_ref, oper_ref, first_ref, wide_ref
 ):
     modes = elem_ref.shape[-1]
-    copy_ref[...] = rows_ref[...]
     picked = []
     for k in range(3):
         for part in range(2):
@@ -259,25 +258,28 @@
     return place * spins + spin
 
 
-def first_kernel(spaces, spins, oper_ref, own_ref, *refs):
-    block_refs, first_ref = refs[:-1], refs[-1]
-    count = own_ref.shape[0]
-    start = pl.multiple_of(own_block(spaces, spins, 0, 0) * count, count)
-    first_ref[pl.ds(start, count), :] = own_ref[...]
-    at = 1
-    left = list(block_refs)
-    while left:
-        rows = left.pop(0)[...]
-        while rows.shape[0] < count:
-            rows = jnp.concatenate([rows, left.pop(0)[...]], axis=0)
-        product = times_operator(rows, oper_ref[...])
-        start = pl.multiple_of(own_block(spaces, spins, at // spins, at % spins) * count, count)
-        first_ref[pl.ds(start, count), :] = product.astype(BF16)
-        at += 1
-
-
-def second_kernel(next_ref, first_ref, second_ref, wide_ref):
+def first_kernel(oper_ref, *refs):
+    out_refs = list(refs[len(refs) // (PIECES + 1) :])
+    for rows_ref in refs[: len(refs) // (PIECES + 1)]:
+        product = times_operator(rows_ref[...], oper_ref[...]).astype(BF16)
+        part = product.shape[0] // PIECES
+        for piece in range(PIECES):
+            out_refs.pop(0)[...] = product[piece * part : (piece + 1) * part]
+
+
+def second_kernel(spaces, spins, next_ref, *refs):
+    block_refs, (first_ref, second_ref, wide_ref) = list(refs[:-3]), refs[-3:]
+    count = next_ref.shape[0]
     order = next_ref.shape[1] // 2
+    for at in range(spaces * spins):
+        start = own_block(spaces, spins, at // spins, at % spins) * count
+        filled = 0
+        while filled < count:
+            block_ref = block_refs.pop(0)
+            height = block_ref.shape[0]
+            rows = pl.ds(pl.multiple_of(start + filled, height), height)
+            first_ref[rows, :] = block_ref[...]
+            filled += height
     real_part, imag_part = times_rows(next_ref[...], first_ref[...])
     second_ref[:, :order] = real_part.astype(BF16)
     second_ref[:, order:] = imag_part.astype(BF16)
@@ -386,9 +388,9 @@
         10**10,
     )(own_slab, *fields, *links)
     wide_shape = jax.ShapeDtypeStruct((count, width), F32)
-    operator, own_first, own_wide, rows_copy = vmem_call(
+    operator, own_first, own_wide = vmem_call(
         operator_kernel,
-        (jax.ShapeDtypeStruct((4 * modes, 4 * modes), BF16), rows_shape, wide_shape, rows_shape),
+        (jax.ShapeDtypeStruct((4 * modes, 4 * modes), BF16), rows_shape, wide_shape),
         [],
         10**8,
         smem=(0,),
@@ -396,30 +398,23 @@
 
     next_first = from_offset(own_first, "tm", 1)
 
-    far_rows, held_rows, held_first = lax.optimization_barrier((far_rows, rows_copy, own_first))
-    blocks = []
-    for at, block in enumerate([held_rows] + far_rows):
-        blocks += [block]
-        pieces = PIECES if at else 1
+    far_rows, held_first = lax.optimization_barrier((far_rows, own_first))
+    piece_shape = jax.ShapeDtypeStruct((count // PIECES, width), BF16)
+    far_first = vmem_call(first_kernel, (piece_shape,) * (PIECES * len(far_rows)), [], 10**6)(
+        operator, *far_rows
+    )
+    blocks = [own_first] + [from_offset(held_first, "spin", step) for step in range(1, spins)]
+    for at in range(0, len(far_first), PIECES):
+        pieces = list(far_first[at : at + PIECES])
+        blocks += pieces
         for step in range(1, spins):
-            for piece in range(pieces):
-                low, high = piece * count // pieces, (piece + 1) * count // pieces
-                blocks += [from_offset(block[low:high], "spin", step)]
-    blocks = blocks[1:]
-    first = vmem_call(
-        functools.partial(first_kernel, spaces, spins),
-        jax.ShapeDtypeStruct((order, width), BF16),
-        [],
-        10**6,
-    )(operator, held_first, *blocks)
-
-    second, second_wide = vmem_call(
-        second_kernel,
-        (rows_shape, wide_shape),
+            blocks += [from_offset(piece, "spin", step) for piece in pieces]
+    first, second, second_wide = vmem_call(
+        functools.partial(second_kernel, spaces, spins),
+        (jax.ShapeDtypeStruct((order, width), BF16), rows_shape, wide_shape),
         [],
         3 * 10**8,
-    )(next_first, first)
-
+    )(next_first, *blocks)
     next_second = from_offset(second, "tm", 1)
 
     turned, weights, elementals, early = vmem_call(

time: 37.9 us -> 37.8 us (level)
  transfers between devices with their start and end apart: 14 -> 14, of which waited for: 9 -> 7; matrix products, arithmetic and copies ran while one was open for 0% -> 0% of each run, Pallas kernels for 15% -> 14%
where the time goes in v7:
time: 37.8 us; the launch traced here: 37.6 us
  starting transfers between devices  19.4 us (51%)
  waiting for transfers between devices  8.61 us (23%)
  Pallas kernels  6.18 us (16%)
  local copies, waits for them, and re-layouts  2.11 us (6%)
  between operations  0.71 us (2%)
  other arithmetic  0.57 us (2%)
    ppermute x8, starting transfers between devices, from_offset(): lax.ppermute(block, axis, [((i + distance) % count, i) for i in range(cou...  13.1 us
    ppermute x6, starting transfers between devices, swapped(): lax.ppermute(block, ('tm', 'space', 'spin'), [(i ^ mask, i) for i in rang...  6.31 us
    pallas_call x9, Pallas kernels, call(): pl.pallas_call(kernel, out_shape=out_shape, in_specs=specs, out_specs=out...  6.18 us
    ppermute x8, waiting for transfers between devices, from_offset(): lax.ppermute(block, axis, [((i + distance) % count, i) for i in range(cou...  5.94 us
    ppermute x6, waiting for transfers between devices, swapped(): lax.ppermute(block, ('tm', 'space', 'spin'), [(i ^ mask, i) for i in rang...  2.67 us
    unnamed x12, local copies, waits for them, and re-layouts  2.11 us
  transfers between devices with their start and end apart: 14, of which 7 were waited for; matrix products, arithmetic and copies ran while one was open for 0% of the time, Pallas kernels for 14%

profile of v7, /device:TPU:0, one launch (start us, length us, event | category | flops | bytes accessed | tf_op | source)
XLA Modules:
  0.0 37.6 jit_solution(6310093197484085508)
XLA Ops:
  0.6 3.0 %collective-permute-start = (bf16[192,128]{1,0:T(8,128)(2,1)}, bf16[192,128]{1,0:T(8,128)(2,1)S(1)}, u32[]{:S(2)}, u32[]{:S(2)}) collective-permute-start(bf16[192,128]{1,0:T(8,128)(2,1)} %bitcast.12), channel_id=1, source_target_pairs={{2,0},{0,2},{3,1},{1,3},{6,4},{4,6},{7,5},{5,7},{10,8},{8,10},{11,... | collective-permute-start | bytes 147464 | tf_op jit(solution)/shard_map/ppermute | solution.py:19
  3.6 0.8 %copy-done.5 = bf16[1,3,2,3,3,8,4]{5,6,4,3,2,1,0:T(4,128)(2,1)S(1)} copy-done((bf16[1,3,2,3,3,8,4]{5,6,4,3,2,1,0:T(4,128)(2,1)S(1)}, bf16[1,3,2,3,3,8,4]{5,6,4,3,2,1,0:T(4,128)(2,1)}, u32[]{:S(2)}) %copy-start.5) | copy-done | bytes 3480
  4.6 0.6 %copy-done.1 = bf16[1,2,3,8,2,2,128]{6,5,4,3,2,1,0:T(2,128)(2,1)S(1)} copy-done((bf16[1,2,3,8,2,2,128]{6,5,4,3,2,1,0:T(2,128)(2,1)S(1)}, bf16[1,2,3,8,2,2,128]{6,5,4,3,2,1,0:T(2,128)(2,1)}, u32[]{:S(2)}) %copy-start.1) | copy-done | bytes 49176
  5.6 1.5 %collective-permute-start.3 = (bf16[128,1024]{1,0:T(8,128)(2,1)S(1)}, bf16[128,1024]{1,0:T(8,128)(2,1)S(1)}, u32[]{:S(2)}, u32[]{:S(2)}) collective-permute-start(bf16[128,1024]{1,0:T(8,128)(2,1)S(1)} %bitcast.10), channel_id=1, source_target_pairs={{2,0},{0,2},{3,1},{1,3},{6,4},{4,6},{7,5},{5,7},{10,8},{8,10},{11,... | collective-permute-start | bytes 786440 | tf_op jit(solution)/shard_map/ppermute | solution.py:19
  7.1 1.3 %collective-permute-done.1.refs_3_ = bf16[32,128]{1,0:T(8,128)(2,1)S(1)} collective-permute-done((bf16[32,128]{1,0:T(8,128)(2,1)S(1)}, bf16[32,128]{1,0:T(8,128)(2,1)S(1)}, u32[]{:S(2)}, u32[]{:S(2)}) %collective-permute-start.1) | collective-permute-done | bytes 8224 | tf_op jit(solution)/shard_map/ppermute | solution.py:19
  8.4 0.8 %shard_map.87.elem_ref = f32[3,2,128,128]{3,2,1,0:T(8,128)S(1)} custom-call(bf16[576,128]{1,0:T(8,128)(2,1)S(1)} %get-tuple-element.22.early_ref, bf16[192,128]{1,0:T(8,128)(2,1)S(1)} %get-tuple-element.23.refs_0_, bf16[192,128]{1,0:T(8,128)(2,1)S(1)} %collective-permute-done.refs_1_, bf16[32,128]{1,0:T(8,128)(2,1)S(1)} %shard_map.85.links_ref.refs_2_, ...), custom_call_target="tpu_custom_call" | custom-call | flops 10000000000 | bytes 1048576 | tf_op jit(solution)/shard_map/pallas_call | solution.py:33
  9.2 0.9 %shard_map.88 = (bf16[512,512]{1,0:T(8,128)(2,1)S(1)}, bf16[128,1024]{1,0:T(8,128)(2,1)S(1)}, f32[128,1024]{1,0:T(8,128)S(1)}) custom-call(s32[3]{0:T(128)S(1)} %copy-done.4, f32[3,2,128,128]{3,2,1,0:T(8,128)S(1)} %shard_map.87.elem_ref, bf16[128,1024]{1,0:T(8,128)(2,1)S(1)} %bitcast.11), custom_call_target="tpu_custom_call" | custom-call | flops 100000000 | bytes 1048576 | tf_op jit(solution)/shard_map/pallas_call | solution.py:33
  10.1 3.7 %collective-permute-start.2 = (bf16[128,1024]{1,0:T(8,128)(2,1)S(1)}, bf16[128,1024]{1,0:T(8,128)(2,1)S(1)}, u32[]{:S(2)}, u32[]{:S(2)}) collective-permute-start(bf16[128,1024]{1,0:T(8,128)(2,1)S(1)} %get-tuple-element.26.refs_0_), channel_id=1, source_target_pairs={{4,0},{8,4},{12,8},{0,12},{5,1},{9,5},{13,9},{1,13},{6,2},{10,6},{... | collective-permute-start | bytes 786440 | tf_op jit(solution)/shard_map/ppermute | solution.py:19
  14.0 0.6 %collective-permute-start.5 = (bf16[64,1024]{1,0:T(8,128)(2,1)S(1)}, bf16[64,1024]{1,0:T(8,128)(2,1)S(1)}, u32[]{:S(2)}, u32[]{:S(2)}) collective-permute-start(bf16[64,1024]{1,0:T(8,128)(2,1)S(1)} %get-tuple-element.29.refs_2_), channel_id=1, source_target_pairs={{1,0},{0,1},{3,2},{2,3},{5,4},{4,5},{7,6},{6,7},{9,8},{8,9},{11,10... | collective-permute-start | bytes 393224 | tf_op jit(solution)/shard_map/ppermute | solution.py:19
  14.7 3.1 %collective-permute-done.2.next_ref = bf16[128,1024]{1,0:T(8,128)(2,1)S(1)} collective-permute-done((bf16[128,1024]{1,0:T(8,128)(2,1)S(1)}, bf16[128,1024]{1,0:T(8,128)(2,1)S(1)}, u32[]{:S(2)}, u32[]{:S(2)}) %collective-permute-start.2) | collective-permute-done | bytes 262176 | tf_op jit(solution)/shard_map/ppermute | solution.py:19
  17.8 0.5 %shard_map.90 = (bf16[512,1024]{1,0:T(8,128)(2,1)S(1)}, bf16[128,1024]{1,0:T(8,128)(2,1)S(1)}, f32[128,1024]{1,0:T(8,128)S(1)}) custom-call(bf16[128,1024]{1,0:T(8,128)(2,1)S(1)} %collective-permute-done.2.next_ref, bf16[128,1024]{1,0:T(8,128)(2,1)S(1)} %get-tuple-element.26.refs_0_, bf16[128,1024]{1,0:T(8,128)(2,1)S(1)} %collective-permute-done.4.refs_1_, ...), custom_call_target="tpu_custom_call" | custom-call | flops 300000000 | bytes 1048576 | tf_op jit(solution)/shard_map/pallas_call | solution.py:33
  18.3 4.3 %collective-permute-start.7 = (bf16[128,1024]{1,0:T(8,128)(2,1)S(1)}, bf16[128,1024]{1,0:T(8,128)(2,1)S(1)}, u32[]{:S(2)}, u32[]{:S(2)}) collective-permute-start(bf16[128,1024]{1,0:T(8,128)(2,1)S(1)} %get-tuple-element.35), channel_id=1, source_target_pairs={{4,0},{8,4},{12,8},{0,12},{5,1},{9,5},{13,9},{1,13},{6,2},{10,6},{... | collective-permute-start | bytes 786440 | tf_op jit(solution)/shard_map/ppermute | solution.py:19
  22.7 0.7 %copy-done.2 = s32[4]{0:T(128)S(1)} copy-done((s32[4]{0:T(128)S(1)}, s32[4]{0:T(128)}, u32[]{:S(2)}) %copy-start.2) | copy-done | bytes 40
  23.3 1.6 %shard_map.91 = (bf16[128,1024]{1,0:T(8,128)(2,1)S(1)}, f32[8,128]{1,0:T(8,128)S(1)}, f32[64,3,2,64]{3,2,1,0:T(2,128)}, f32[8,128]{1,0:T(8,128)S(1)}) custom-call(s32[4]{0:T(128)S(1)} %copy-done.2, s32[1,16]{1,0:T(1,128)S(1)} %bitcast.14, bf16[512,1024]{1,0:T(8,128)(2,1)S(1)} %get-tuple-element.31.first_ref, f32[3,2,128,128]{3,2,1,0:T(8,128)S(1)} %shard_map.87.elem_ref, ...), custom_call_target="tpu_custom_call" | custom-call | flops 1000000 | bytes 1048576 | tf_op jit(solution)/shard_map/pallas_call | solution.py:33
  25.0 1.6 %collective-permute-done.7.second_ref = bf16[128,1024]{1,0:T(8,128)(2,1)S(1)} collective-permute-done((bf16[128,1024]{1,0:T(8,128)(2,1)S(1)}, bf16[128,1024]{1,0:T(8,128)(2,1)S(1)}, u32[]{:S(2)}, u32[]{:S(2)}) %collective-permute-start.7) | collective-permute-done | bytes 262176 | tf_op jit(solution)/shard_map/ppermute | solution.py:19
  26.9 1.1 %collective-permute-start.9 = (f32[2,16]{1,0:T(2,128)S(1)}, f32[2,16]{1,0:T(2,128)S(1)}, u32[]{:S(2)}, u32[]{:S(2)}) collective-permute-start(f32[2,16]{1,0:T(2,128)S(1)} %shard_map.93), channel_id=1, source_target_pairs={{8,0},{9,1},{10,2},{11,3},{12,4},{13,5},{14,6},{15,7},{0,8},{1,9},... | collective-permute-start | bytes 392 | tf_op jit(solution)/shard_map/ppermute | solution.py:23
  28.0 1.7 %collective-permute-start.8 = (f32[2,16]{1,0:T(2,128)S(1)}, f32[2,16]{1,0:T(2,128)S(1)}, u32[]{:S(2)}, u32[]{:S(2)}) collective-permute-start(f32[2,16]{1,0:T(2,128)S(1)} %shard_map.93), channel_id=1, source_target_pairs={{1,0},{0,1},{3,2},{2,3},{5,4},{4,5},{7,6},{6,7},{9,8},{8,9},{11,10... | collective-permute-start | bytes 392 | tf_op jit(solution)/shard_map/ppermute | solution.py:23
  29.7 1.1 %shard_map.92 = bf16[128,1024]{1,0:T(8,128)(2,1)} custom-call(bf16[128,1024]{1,0:T(8,128)(2,1)S(1)} %collective-permute-done.7.second_ref, bf16[512,1024]{1,0:T(8,128)(2,1)S(1)} %get-tuple-element.31.first_ref), custom_call_target="tpu_custom_call" | custom-call | flops 100000000 | bytes 1048576 | tf_op jit(solution)/shard_map/pallas_call | solution.py:33
  30.8 0.6 %collective-permute-done.9 = f32[2,16]{1,0:T(2,128)S(1)} collective-permute-done((f32[2,16]{1,0:T(2,128)S(1)}, f32[2,16]{1,0:T(2,128)S(1)}, u32[]{:S(2)}, u32[]{:S(2)}) %collective-permute-start.9) | collective-permute-done | bytes 160 | tf_op jit(solution)/shard_map/ppermute | solution.py:23
  31.4 1.9 %collective-permute-start.13 = (f32[2,16]{1,0:T(2,128)S(1)}, f32[2,16]{1,0:T(2,128)S(1)}, u32[]{:S(2)}, u32[]{:S(2)}) collective-permute-start(f32[2,16]{1,0:T(2,128)S(1)} %add_add_fusion), channel_id=1, source_target_pairs={{6,0},{7,1},{4,2},{5,3},{2,4},{3,5},{0,6},{1,7},{14,8},{15,9},{12,... | collective-permute-start | bytes 392 | tf_op jit(solution)/shard_map/ppermute | solution.py:23
  33.5 1.5 %collective-permute-start.11 = (f32[2,16]{1,0:T(2,128)S(1)}, f32[2,16]{1,0:T(2,128)S(1)}, u32[]{:S(2)}, u32[]{:S(2)}) collective-permute-start(f32[2,16]{1,0:T(2,128)S(1)} %add_add_fusion), channel_id=1, source_target_pairs={{2,0},{3,1},{0,2},{1,3},{6,4},{7,5},{4,6},{5,7},{10,8},{11,9},{8,1... | collective-permute-start | bytes 392 | tf_op jit(solution)/shard_map/ppermute | solution.py:23
  35.0 1.0 %collective-permute-done.13 = f32[2,16]{1,0:T(2,128)S(1)} collective-permute-done((f32[2,16]{1,0:T(2,128)S(1)}, f32[2,16]{1,0:T(2,128)S(1)}, u32[]{:S(2)}, u32[]{:S(2)}) %collective-permute-start.13) | collective-permute-done | bytes 160 | tf_op jit(solution)/shard_map/ppermute | solution.py:23
  36.0 1.0 %collective-permute-done.12 = f32[2,16]{1,0:T(2,128)S(1)} collective-permute-done((f32[2,16]{1,0:T(2,128)S(1)}, f32[2,16]{1,0:T(2,128)S(1)}, u32[]{:S(2)}, u32[]{:S(2)}) %collective-permute-start.12) | collective-permute-done | bytes 160 | tf_op jit(solution)/shard_map/ppermute | solution.py:23
  37.1 0.6 %add_bitcast_fusion = f32[16,2]{0,1:T(2,128)} fusion(f32[2,16]{1,0:T(2,128)S(1)} %collective-permute-done.13, f32[2,16]{1,0:T(2,128)S(1)} %collective-permute-done.12, f32[2,16]{1,0:T(2,128)S(1)} %add_add_fusion, f32[2,16]{1,0:T(2,128)S(1)} %collective-permute-done.11), kind=kLoop, calls=%fused_computation | loop fusion | flops 96 | bytes 640 | tf_op jit(solution)/shard_map/transpose | solution.py:451
  (27 shorter events, 1.6 us)
Async XLA Ops:
  0.6 7.7 %collective-permute-start = (bf16[192,128]{1,0:T(8,128)(2,1)}, bf16[192,128]{1,0:T(8,128)(2,1)S(1)}, u32[]{:S(2)}, u32[]{:S(2)}) collective-permute-start(bf16[192,128]{1,0:T(8,128)(2,1)} %bitcast.12), channel_id=1, source_target_pairs={{2,0},{0,2},{3,1},{1,3},{6,4},{4,6},{7,5},{5,7},{10,8},{8,10},{11,... | collective-permute-start | bytes 147464 | tf_op jit(solution)/shard_map/ppermute | solution.py:19
  3.6 0.8 %copy-start.5 = (bf16[1,3,2,3,3,8,4]{5,6,4,3,2,1,0:T(4,128)(2,1)S(1)}, bf16[1,3,2,3,3,8,4]{5,6,4,3,2,1,0:T(4,128)(2,1)}, u32[]{:S(2)}) copy-start(bf16[1,3,2,3,3,8,4]{5,6,4,3,2,1,0:T(4,128)(2,1)} %param.7) | copy-start | bytes 10372
  4.4 0.8 %copy-start.1 = (bf16[1,2,3,8,2,2,128]{6,5,4,3,2,1,0:T(2,128)(2,1)S(1)}, bf16[1,2,3,8,2,2,128]{6,5,4,3,2,1,0:T(2,128)(2,1)}, u32[]{:S(2)}) copy-start(bf16[1,2,3,8,2,2,128]{6,5,4,3,2,1,0:T(2,128)(2,1)} %param.6) | copy-start | bytes 147460
  4.5 1.2 %copy-start = (bf16[1,128,1024]{2,1,0:T(8,128)(2,1)S(1)}, bf16[1,128,1024]{2,1,0:T(8,128)(2,1)}, u32[]{:S(2)}) copy-start(bf16[1,128,1024]{2,1,0:T(8,128)(2,1)} %param.8) | copy-start | bytes 786436
  4.6 3.8 %collective-permute-start.1 = (bf16[32,128]{1,0:T(8,128)(2,1)S(1)}, bf16[32,128]{1,0:T(8,128)(2,1)S(1)}, u32[]{:S(2)}, u32[]{:S(2)}) collective-permute-start(bf16[32,128]{1,0:T(8,128)(2,1)S(1)} %shard_map.85.links_ref.refs_2_), channel_id=1, source_target_pairs={{2,0},{0,2},{3,1},{1,3},{6,4},{4,6},{7,5},{5,7},{10,8},{8,10},{11,... | collective-permute-start | bytes 24584 | tf_op jit(solution)/shard_map/ppermute | solution.py:19
  5.6 8.1 %collective-permute-start.3 = (bf16[128,1024]{1,0:T(8,128)(2,1)S(1)}, bf16[128,1024]{1,0:T(8,128)(2,1)S(1)}, u32[]{:S(2)}, u32[]{:S(2)}) collective-permute-start(bf16[128,1024]{1,0:T(8,128)(2,1)S(1)} %bitcast.10), channel_id=1, source_target_pairs={{2,0},{0,2},{3,1},{1,3},{6,4},{4,6},{7,5},{5,7},{10,8},{8,10},{11,... | collective-permute-start | bytes 786440 | tf_op jit(solution)/shard_map/ppermute | solution.py:19
  8.4 0.8 %copy-start.4 = (s32[3]{0:T(128)S(1)}, s32[3]{0:T(128)}, u32[]{:S(2)}) copy-start(s32[3]{0:T(128)} %dirs_ref.1) | copy-start | bytes 40
  10.1 7.7 %collective-permute-start.2 = (bf16[128,1024]{1,0:T(8,128)(2,1)S(1)}, bf16[128,1024]{1,0:T(8,128)(2,1)S(1)}, u32[]{:S(2)}, u32[]{:S(2)}) collective-permute-start(bf16[128,1024]{1,0:T(8,128)(2,1)S(1)} %get-tuple-element.26.refs_0_), channel_id=1, source_target_pairs={{4,0},{8,4},{12,8},{0,12},{5,1},{9,5},{13,9},{1,13},{6,2},{10,6},{... | collective-permute-start | bytes 786440 | tf_op jit(solution)/shard_map/ppermute | solution.py:19
  13.7 4.1 %collective-permute-start.4 = (bf16[128,1024]{1,0:T(8,128)(2,1)S(1)}, bf16[128,1024]{1,0:T(8,128)(2,1)S(1)}, u32[]{:S(2)}, u32[]{:S(2)}) collective-permute-start(bf16[128,1024]{1,0:T(8,128)(2,1)S(1)} %get-tuple-element.26.refs_0_), channel_id=1, source_target_pairs={{1,0},{0,1},{3,2},{2,3},{5,4},{4,5},{7,6},{6,7},{9,8},{8,9},{11,10... | collective-permute-start | bytes 786440 | tf_op jit(solution)/shard_map/ppermute | solution.py:19
  14.0 3.7 %collective-permute-start.5 = (bf16[64,1024]{1,0:T(8,128)(2,1)S(1)}, bf16[64,1024]{1,0:T(8,128)(2,1)S(1)}, u32[]{:S(2)}, u32[]{:S(2)}) collective-permute-start(bf16[64,1024]{1,0:T(8,128)(2,1)S(1)} %get-tuple-element.29.refs_2_), channel_id=1, source_target_pairs={{1,0},{0,1},{3,2},{2,3},{5,4},{4,5},{7,6},{6,7},{9,8},{8,9},{11,10... | collective-permute-start | bytes 393224 | tf_op jit(solution)/shard_map/ppermute | solution.py:19
  14.6 3.2 %collective-permute-start.6 = (bf16[64,1024]{1,0:T(8,128)(2,1)S(1)}, bf16[64,1024]{1,0:T(8,128)(2,1)S(1)}, u32[]{:S(2)}, u32[]{:S(2)}) collective-permute-start(bf16[64,1024]{1,0:T(8,128)(2,1)S(1)} %get-tuple-element.30.refs_3_), channel_id=1, source_target_pairs={{1,0},{0,1},{3,2},{2,3},{5,4},{4,5},{7,6},{6,7},{9,8},{8,9},{11,10... | collective-permute-start | bytes 393224 | tf_op jit(solution)/shard_map/ppermute | solution.py:19
  18.3 8.2 %collective-permute-start.7 = (bf16[128,1024]{1,0:T(8,128)(2,1)S(1)}, bf16[128,1024]{1,0:T(8,128)(2,1)S(1)}, u32[]{:S(2)}, u32[]{:S(2)}) collective-permute-start(bf16[128,1024]{1,0:T(8,128)(2,1)S(1)} %get-tuple-element.35), channel_id=1, source_target_pairs={{4,0},{8,4},{12,8},{0,12},{5,1},{9,5},{13,9},{1,13},{6,2},{10,6},{... | collective-permute-start | bytes 786440 | tf_op jit(solution)/shard_map/ppermute | solution.py:19
  22.7 0.7 %copy-start.2 = (s32[4]{0:T(128)S(1)}, s32[4]{0:T(128)}, u32[]{:S(2)}) copy-start(s32[4]{0:T(128)} %offsets_ref.1) | copy-start | bytes 52
  22.7 0.7 %copy-start.3 = (s32[16]{0:T(128)S(1)}, s32[16]{0:T(128)}, u32[]{:S(2)}) copy-start(s32[16]{0:T(128)} %param.9) | copy-start | bytes 196
  26.9 3.9 %collective-permute-start.10 = (f32[2,16]{1,0:T(2,128)S(1)}, f32[2,16]{1,0:T(2,128)S(1)}, u32[]{:S(2)}, u32[]{:S(2)}) collective-permute-start(f32[2,16]{1,0:T(2,128)S(1)} %shard_map.93), channel_id=1, source_target_pairs={{9,0},{8,1},{11,2},{10,3},{13,4},{12,5},{15,6},{14,7},{1,8},{0,9},... | collective-permute-start | bytes 392 | tf_op jit(solution)/shard_map/ppermute | solution.py:23
  26.9 4.5 %collective-permute-start.9 = (f32[2,16]{1,0:T(2,128)S(1)}, f32[2,16]{1,0:T(2,128)S(1)}, u32[]{:S(2)}, u32[]{:S(2)}) collective-permute-start(f32[2,16]{1,0:T(2,128)S(1)} %shard_map.93), channel_id=1, source_target_pairs={{8,0},{9,1},{10,2},{11,3},{12,4},{13,5},{14,6},{15,7},{0,8},{1,9},... | collective-permute-start | bytes 392 | tf_op jit(solution)/shard_map/ppermute | solution.py:23
  28.0 3.4 %collective-permute-start.8 = (f32[2,16]{1,0:T(2,128)S(1)}, f32[2,16]{1,0:T(2,128)S(1)}, u32[]{:S(2)}, u32[]{:S(2)}) collective-permute-start(f32[2,16]{1,0:T(2,128)S(1)} %shard_map.93), channel_id=1, source_target_pairs={{1,0},{0,1},{3,2},{2,3},{5,4},{4,5},{7,6},{6,7},{9,8},{8,9},{11,10... | collective-permute-start | bytes 392 | tf_op jit(solution)/shard_map/ppermute | solution.py:23
  31.4 4.5 %collective-permute-start.13 = (f32[2,16]{1,0:T(2,128)S(1)}, f32[2,16]{1,0:T(2,128)S(1)}, u32[]{:S(2)}, u32[]{:S(2)}) collective-permute-start(f32[2,16]{1,0:T(2,128)S(1)} %add_add_fusion), channel_id=1, source_target_pairs={{6,0},{7,1},{4,2},{5,3},{2,4},{3,5},{0,6},{1,7},{14,8},{15,9},{12,... | collective-permute-start | bytes 392 | tf_op jit(solution)/shard_map/ppermute | solution.py:23
  33.4 3.6 %collective-permute-start.12 = (f32[2,16]{1,0:T(2,128)S(1)}, f32[2,16]{1,0:T(2,128)S(1)}, u32[]{:S(2)}, u32[]{:S(2)}) collective-permute-start(f32[2,16]{1,0:T(2,128)S(1)} %add_add_fusion), channel_id=1, source_target_pairs={{4,0},{5,1},{6,2},{7,3},{0,4},{1,5},{2,6},{3,7},{12,8},{13,9},{14,... | collective-permute-start | bytes 392 | tf_op jit(solution)/shard_map/ppermute | solution.py:23
  33.5 3.6 %collective-permute-start.11 = (f32[2,16]{1,0:T(2,128)S(1)}, f32[2,16]{1,0:T(2,128)S(1)}, u32[]{:S(2)}, u32[]{:S(2)}) collective-permute-start(f32[2,16]{1,0:T(2,128)S(1)} %add_add_fusion), channel_id=1, source_target_pairs={{2,0},{3,1},{0,2},{1,3},{6,4},{7,5},{4,6},{5,7},{10,8},{11,9},{8,1... | collective-permute-start | bytes 392 | tf_op jit(solution)/shard_map/ppermute | solution.py:23

commit v8 on v6

--- a/solution.py
+++ b/solution.py
@@ -440,7 +440,6 @@
         [],
         10**6,
     )(weights, next_second, turned, early)
-    chain = vmem_call(third_kernel, rows_shape, [], 10**8)(next_second, first)
 
     devices = slots * spaces * spins
     if devices & (devices - 1):
@@ -453,6 +452,9 @@
             masks = [low] if low == high else [low, high, low | high]
             parts = [swapped(shares, devices, mask) for mask in masks]
             shares = functools.reduce(lambda x, y: x + y, parts, shares)
+            if high == devices >> 1:
+                shares, next_second = lax.optimization_barrier((shares, next_second))
+    chain = vmem_call(third_kernel, rows_shape, [], 10**8)(next_second, first)
     return (elementals[None], chain[None], shares.T)
 
 

time: 37.9 us -> 37.9 us (level)
  no operation moved by 1% of the time
where the time goes in v8:
time: 37.9 us; the launch traced here: 37.7 us
  starting transfers between devices  19.4 us (51%)
  waiting for transfers between devices  8.44 us (22%)
  Pallas kernels  6.39 us (17%)
  local copies, waits for them, and re-layouts  2.13 us (6%)
  between operations  0.71 us (2%)
  other arithmetic  0.57 us (2%)
    ppermute x8, starting transfers between devices, from_offset(): lax.ppermute(block, axis, [((i + distance) % count, i) for i in range(cou...  13.1 us
    pallas_call x9, Pallas kernels, call(): pl.pallas_call(kernel, out_shape=out_shape, in_specs=specs, out_specs=out...  6.39 us
    ppermute x6, starting transfers between devices, swapped(): lax.ppermute(block, ('tm', 'space', 'spin'), [(i ^ mask, i) for i in rang...  6.31 us
    ppermute x8, waiting for transfers between devices, from_offset(): lax.ppermute(block, axis, [((i + distance) % count, i) for i in range(cou...  5.63 us
    ppermute x6, waiting for transfers between devices, swapped(): lax.ppermute(block, ('tm', 'space', 'spin'), [(i ^ mask, i) for i in rang...  2.81 us
    unnamed x12, local copies, waits for them, and re-layouts  2.11 us
  transfers between devices with their start and end apart: 14, of which 9 were waited for; matrix products, arithmetic and copies ran while one was open for 0% of the time, Pallas kernels for 15%

profile of v8, /device:TPU:0, one launch (start us, length us, event | category | flops | bytes accessed | tf_op | source)
XLA Modules:
  0.0 37.7 jit_solution(11800589408543479903)
XLA Ops:
  0.6 3.0 %collective-permute-start = (bf16[192,128]{1,0:T(8,128)(2,1)}, bf16[192,128]{1,0:T(8,128)(2,1)S(1)}, u32[]{:S(2)}, u32[]{:S(2)}) collective-permute-start(bf16[192,128]{1,0:T(8,128)(2,1)} %bitcast.12), channel_id=1, source_target_pairs={{2,0},{0,2},{3,1},{1,3},{6,4},{4,6},{7,5},{5,7},{10,8},{8,10},{11,... | collective-permute-start | bytes 147464 | tf_op jit(solution)/shard_map/ppermute | solution.py:19
  3.6 0.8 %copy-done.5 = bf16[1,3,2,3,3,8,4]{5,6,4,3,2,1,0:T(4,128)(2,1)S(1)} copy-done((bf16[1,3,2,3,3,8,4]{5,6,4,3,2,1,0:T(4,128)(2,1)S(1)}, bf16[1,3,2,3,3,8,4]{5,6,4,3,2,1,0:T(4,128)(2,1)}, u32[]{:S(2)}) %copy-start.5) | copy-done | bytes 3480
  4.6 0.6 %copy-done.1 = bf16[1,2,3,8,2,2,128]{6,5,4,3,2,1,0:T(2,128)(2,1)S(1)} copy-done((bf16[1,2,3,8,2,2,128]{6,5,4,3,2,1,0:T(2,128)(2,1)S(1)}, bf16[1,2,3,8,2,2,128]{6,5,4,3,2,1,0:T(2,128)(2,1)}, u32[]{:S(2)}) %copy-start.1) | copy-done | bytes 49176
  5.6 1.5 %collective-permute-start.2 = (bf16[128,1024]{1,0:T(8,128)(2,1)S(1)}, bf16[128,1024]{1,0:T(8,128)(2,1)S(1)}, u32[]{:S(2)}, u32[]{:S(2)}) collective-permute-start(bf16[128,1024]{1,0:T(8,128)(2,1)S(1)} %bitcast.10), channel_id=1, source_target_pairs={{2,0},{0,2},{3,1},{1,3},{6,4},{4,6},{7,5},{5,7},{10,8},{8,10},{11,... | collective-permute-start | bytes 786440 | tf_op jit(solution)/shard_map/ppermute | solution.py:19
  7.1 1.3 %collective-permute-done.1.refs_3_ = bf16[32,128]{1,0:T(8,128)(2,1)S(1)} collective-permute-done((bf16[32,128]{1,0:T(8,128)(2,1)S(1)}, bf16[32,128]{1,0:T(8,128)(2,1)S(1)}, u32[]{:S(2)}, u32[]{:S(2)}) %collective-permute-start.1) | collective-permute-done | bytes 8224 | tf_op jit(solution)/shard_map/ppermute | solution.py:19
  8.4 0.8 %shard_map.87.elem_ref = f32[3,2,128,128]{3,2,1,0:T(8,128)S(1)} custom-call(bf16[576,128]{1,0:T(8,128)(2,1)S(1)} %get-tuple-element.23.early_ref, bf16[192,128]{1,0:T(8,128)(2,1)S(1)} %get-tuple-element.24.refs_0_, bf16[192,128]{1,0:T(8,128)(2,1)S(1)} %collective-permute-done.refs_1_, bf16[32,128]{1,0:T(8,128)(2,1)S(1)} %shard_map.85.links_ref.refs_2_, ...), custom_call_target="tpu_custom_call" | custom-call | flops 10000000000 | bytes 1048576 | tf_op jit(solution)/shard_map/pallas_call | solution.py:33
  9.2 0.9 %shard_map.88 = (bf16[512,512]{1,0:T(8,128)(2,1)S(1)}, bf16[128,1024]{1,0:T(8,128)(2,1)S(1)}, f32[128,1024]{1,0:T(8,128)S(1)}, bf16[128,1024]{1,0:T(8,128)(2,1)S(1)}) custom-call(s32[3]{0:T(128)S(1)} %copy-done.4, f32[3,2,128,128]{3,2,1,0:T(8,128)S(1)} %shard_map.87.elem_ref, bf16[128,1024]{1,0:T(8,128)(2,1)S(1)} %bitcast.11), custom_call_target="tpu_custom_call" | custom-call | flops 100000000 | bytes 1048576 | tf_op jit(solution)/shard_map/pallas_call | solution.py:33
  10.1 3.7 %collective-permute-start.6 = (bf16[128,1024]{1,0:T(8,128)(2,1)S(1)}, bf16[128,1024]{1,0:T(8,128)(2,1)S(1)}, u32[]{:S(2)}, u32[]{:S(2)}) collective-permute-start(bf16[128,1024]{1,0:T(8,128)(2,1)S(1)} %get-tuple-element.29.own_ref), channel_id=1, source_target_pairs={{4,0},{8,4},{12,8},{0,12},{5,1},{9,5},{13,9},{1,13},{6,2},{10,6},{... | collective-permute-start | bytes 786440 | tf_op jit(solution)/shard_map/ppermute | solution.py:19
  13.8 0.6 %collective-permute-start.5 = (bf16[64,1024]{1,0:T(8,128)(2,1)S(1)}, bf16[64,1024]{1,0:T(8,128)(2,1)S(1)}, u32[]{:S(2)}, u32[]{:S(2)}) collective-permute-start(bf16[64,1024]{1,0:T(8,128)(2,1)S(1)} %get-tuple-element.41), channel_id=1, source_target_pairs={{1,0},{0,1},{3,2},{2,3},{5,4},{4,5},{7,6},{6,7},{9,8},{8,9},{11,10... | collective-permute-start | bytes 393224 | tf_op jit(solution)/shard_map/ppermute | solution.py:19
  14.4 1.0 %collective-permute-done.5.refs_3_ = bf16[64,1024]{1,0:T(8,128)(2,1)S(1)} collective-permute-done((bf16[64,1024]{1,0:T(8,128)(2,1)S(1)}, bf16[64,1024]{1,0:T(8,128)(2,1)S(1)}, u32[]{:S(2)}, u32[]{:S(2)}) %collective-permute-start.5) | collective-permute-done | bytes 131104 | tf_op jit(solution)/shard_map/ppermute | solution.py:19
  15.7 0.6 %shard_map.89.first_ref = bf16[512,1024]{1,0:T(8,128)(2,1)S(1)} custom-call(bf16[512,512]{1,0:T(8,128)(2,1)S(1)} %get-tuple-element.25.oper_ref, bf16[128,1024]{1,0:T(8,128)(2,1)S(1)} %get-tuple-element.29.own_ref, bf16[128,1024]{1,0:T(8,128)(2,1)S(1)} %collective-permute-done.3.refs_0_, bf16[128,1024]{1,0:T(8,128)(2,1)S(1)} %collective-permute-done.2.refs_1_, ...), custom_call_target="tpu_custom_call" | custom-call | flops 1000000 | bytes 1048576 | tf_op jit(solution)/shard_map/pallas_call | solution.py:33
  16.3 1.5 %collective-permute-done.6.next_ref = bf16[128,1024]{1,0:T(8,128)(2,1)S(1)} collective-permute-done((bf16[128,1024]{1,0:T(8,128)(2,1)S(1)}, bf16[128,1024]{1,0:T(8,128)(2,1)S(1)}, u32[]{:S(2)}, u32[]{:S(2)}) %collective-permute-start.6) | collective-permute-done | bytes 262176 | tf_op jit(solution)/shard_map/ppermute | solution.py:19
  18.2 4.3 %collective-permute-start.7 = (bf16[128,1024]{1,0:T(8,128)(2,1)S(1)}, bf16[128,1024]{1,0:T(8,128)(2,1)S(1)}, u32[]{:S(2)}, u32[]{:S(2)}) collective-permute-start(bf16[128,1024]{1,0:T(8,128)(2,1)S(1)} %get-tuple-element.36), channel_id=1, source_target_pairs={{4,0},{8,4},{12,8},{0,12},{5,1},{9,5},{13,9},{1,13},{6,2},{10,6},{... | collective-permute-start | bytes 786440 | tf_op jit(solution)/shard_map/ppermute | solution.py:19
  22.6 0.7 %copy-done.2 = s32[4]{0:T(128)S(1)} copy-done((s32[4]{0:T(128)S(1)}, s32[4]{0:T(128)}, u32[]{:S(2)}) %copy-start.2) | copy-done | bytes 40
  23.2 1.6 %shard_map.91 = (bf16[128,1024]{1,0:T(8,128)(2,1)S(1)}, f32[8,128]{1,0:T(8,128)S(1)}, f32[64,3,2,64]{3,2,1,0:T(2,128)}, f32[8,128]{1,0:T(8,128)S(1)}) custom-call(s32[4]{0:T(128)S(1)} %copy-done.2, s32[1,16]{1,0:T(1,128)S(1)} %bitcast.14, bf16[512,1024]{1,0:T(8,128)(2,1)S(1)} %shard_map.89.first_ref, f32[3,2,128,128]{3,2,1,0:T(8,128)S(1)} %shard_map.87.elem_ref, ...), custom_call_target="tpu_custom_call" | custom-call | flops 1000000 | bytes 1048576 | tf_op jit(solution)/shard_map/pallas_call | solution.py:33
  24.9 1.6 %collective-permute-done.7.second_ref = bf16[128,1024]{1,0:T(8,128)(2,1)S(1)} collective-permute-done((bf16[128,1024]{1,0:T(8,128)(2,1)S(1)}, bf16[128,1024]{1,0:T(8,128)(2,1)S(1)}, u32[]{:S(2)}, u32[]{:S(2)}) %collective-permute-start.7) | collective-permute-done | bytes 262176 | tf_op jit(solution)/shard_map/ppermute | solution.py:19
  26.8 1.1 %collective-permute-start.9 = (f32[2,16]{1,0:T(2,128)S(1)}, f32[2,16]{1,0:T(2,128)S(1)}, u32[]{:S(2)}, u32[]{:S(2)}) collective-permute-start(f32[2,16]{1,0:T(2,128)S(1)} %shard_map.92), channel_id=1, source_target_pairs={{8,0},{9,1},{10,2},{11,3},{12,4},{13,5},{14,6},{15,7},{0,8},{1,9},... | collective-permute-start | bytes 392 | tf_op jit(solution)/shard_map/ppermute | solution.py:23
  28.0 1.6 %collective-permute-start.8 = (f32[2,16]{1,0:T(2,128)S(1)}, f32[2,16]{1,0:T(2,128)S(1)}, u32[]{:S(2)}, u32[]{:S(2)}) collective-permute-start(f32[2,16]{1,0:T(2,128)S(1)} %shard_map.92), channel_id=1, source_target_pairs={{1,0},{0,1},{3,2},{2,3},{5,4},{4,5},{7,6},{6,7},{9,8},{8,9},{11,10... | collective-permute-start | bytes 392 | tf_op jit(solution)/shard_map/ppermute | solution.py:23
  29.6 1.1 %collective-permute-done.10 = f32[2,16]{1,0:T(2,128)S(1)} collective-permute-done((f32[2,16]{1,0:T(2,128)S(1)}, f32[2,16]{1,0:T(2,128)S(1)}, u32[]{:S(2)}, u32[]{:S(2)}) %collective-permute-start.10) | collective-permute-done | bytes 160 | tf_op jit(solution)/shard_map/ppermute | solution.py:23
  30.7 0.6 %collective-permute-done.9 = f32[2,16]{1,0:T(2,128)S(1)} collective-permute-done((f32[2,16]{1,0:T(2,128)S(1)}, f32[2,16]{1,0:T(2,128)S(1)}, u32[]{:S(2)}, u32[]{:S(2)}) %collective-permute-start.9) | collective-permute-done | bytes 160 | tf_op jit(solution)/shard_map/ppermute | solution.py:23
  31.3 2.1 %collective-permute-start.13 = (f32[2,16]{1,0:T(2,128)S(1)}, f32[2,16]{1,0:T(2,128)S(1)}, u32[]{:S(2)}, u32[]{:S(2)}) collective-permute-start(f32[2,16]{1,0:T(2,128)S(1)} %add_add_fusion), channel_id=1, source_target_pairs={{6,0},{7,1},{4,2},{5,3},{2,4},{3,5},{0,6},{1,7},{14,8},{15,9},{12,... | collective-permute-start | bytes 392 | tf_op jit(solution)/shard_map/ppermute | solution.py:23
  33.5 1.4 %collective-permute-start.11 = (f32[2,16]{1,0:T(2,128)S(1)}, f32[2,16]{1,0:T(2,128)S(1)}, u32[]{:S(2)}, u32[]{:S(2)}) collective-permute-start(f32[2,16]{1,0:T(2,128)S(1)} %add_add_fusion), channel_id=1, source_target_pairs={{2,0},{3,1},{0,2},{1,3},{6,4},{7,5},{4,6},{5,7},{10,8},{11,9},{8,1... | collective-permute-start | bytes 392 | tf_op jit(solution)/shard_map/ppermute | solution.py:23
  34.9 1.1 %shard_map.93 = bf16[128,1024]{1,0:T(8,128)(2,1)} custom-call(bf16[128,1024]{1,0:T(8,128)(2,1)S(1)} %collective-permute-done.7.second_ref, bf16[512,1024]{1,0:T(8,128)(2,1)S(1)} %shard_map.89.first_ref), custom_call_target="tpu_custom_call" | custom-call | flops 100000000 | bytes 1048576 | tf_op jit(solution)/shard_map/pallas_call | solution.py:33
  36.0 0.9 %collective-permute-done.12 = f32[2,16]{1,0:T(2,128)S(1)} collective-permute-done((f32[2,16]{1,0:T(2,128)S(1)}, f32[2,16]{1,0:T(2,128)S(1)}, u32[]{:S(2)}, u32[]{:S(2)}) %collective-permute-start.12) | collective-permute-done | bytes 160 | tf_op jit(solution)/shard_map/ppermute | solution.py:23
  (28 shorter events, 2.5 us)
Async XLA Ops:
  0.6 7.7 %collective-permute-start = (bf16[192,128]{1,0:T(8,128)(2,1)}, bf16[192,128]{1,0:T(8,128)(2,1)S(1)}, u32[]{:S(2)}, u32[]{:S(2)}) collective-permute-start(bf16[192,128]{1,0:T(8,128)(2,1)} %bitcast.12), channel_id=1, source_target_pairs={{2,0},{0,2},{3,1},{1,3},{6,4},{4,6},{7,5},{5,7},{10,8},{8,10},{11,... | collective-permute-start | bytes 147464 | tf_op jit(solution)/shard_map/ppermute | solution.py:19
  3.6 0.8 %copy-start.5 = (bf16[1,3,2,3,3,8,4]{5,6,4,3,2,1,0:T(4,128)(2,1)S(1)}, bf16[1,3,2,3,3,8,4]{5,6,4,3,2,1,0:T(4,128)(2,1)}, u32[]{:S(2)}) copy-start(bf16[1,3,2,3,3,8,4]{5,6,4,3,2,1,0:T(4,128)(2,1)} %param.7) | copy-start | bytes 10372
  4.4 0.8 %copy-start.1 = (bf16[1,2,3,8,2,2,128]{6,5,4,3,2,1,0:T(2,128)(2,1)S(1)}, bf16[1,2,3,8,2,2,128]{6,5,4,3,2,1,0:T(2,128)(2,1)}, u32[]{:S(2)}) copy-start(bf16[1,2,3,8,2,2,128]{6,5,4,3,2,1,0:T(2,128)(2,1)} %param.6) | copy-start | bytes 147460
  4.5 1.2 %copy-start = (bf16[1,128,1024]{2,1,0:T(8,128)(2,1)S(1)}, bf16[1,128,1024]{2,1,0:T(8,128)(2,1)}, u32[]{:S(2)}) copy-start(bf16[1,128,1024]{2,1,0:T(8,128)(2,1)} %param.8) | copy-start | bytes 786436
  4.6 3.8 %collective-permute-start.1 = (bf16[32,128]{1,0:T(8,128)(2,1)S(1)}, bf16[32,128]{1,0:T(8,128)(2,1)S(1)}, u32[]{:S(2)}, u32[]{:S(2)}) collective-permute-start(bf16[32,128]{1,0:T(8,128)(2,1)S(1)} %shard_map.85.links_ref.refs_2_), channel_id=1, source_target_pairs={{2,0},{0,2},{3,1},{1,3},{6,4},{4,6},{7,5},{5,7},{10,8},{8,10},{11,... | collective-permute-start | bytes 24584 | tf_op jit(solution)/shard_map/ppermute | solution.py:19
  5.6 8.1 %collective-permute-start.2 = (bf16[128,1024]{1,0:T(8,128)(2,1)S(1)}, bf16[128,1024]{1,0:T(8,128)(2,1)S(1)}, u32[]{:S(2)}, u32[]{:S(2)}) collective-permute-start(bf16[128,1024]{1,0:T(8,128)(2,1)S(1)} %bitcast.10), channel_id=1, source_target_pairs={{2,0},{0,2},{3,1},{1,3},{6,4},{4,6},{7,5},{5,7},{10,8},{8,10},{11,... | collective-permute-start | bytes 786440 | tf_op jit(solution)/shard_map/ppermute | solution.py:19
  8.4 0.8 %copy-start.4 = (s32[3]{0:T(128)S(1)}, s32[3]{0:T(128)}, u32[]{:S(2)}) copy-start(s32[3]{0:T(128)} %dirs_ref.1) | copy-start | bytes 40
  10.1 7.7 %collective-permute-start.6 = (bf16[128,1024]{1,0:T(8,128)(2,1)S(1)}, bf16[128,1024]{1,0:T(8,128)(2,1)S(1)}, u32[]{:S(2)}, u32[]{:S(2)}) collective-permute-start(bf16[128,1024]{1,0:T(8,128)(2,1)S(1)} %get-tuple-element.29.own_ref), channel_id=1, source_target_pairs={{4,0},{8,4},{12,8},{0,12},{5,1},{9,5},{13,9},{1,13},{6,2},{10,6},{... | collective-permute-start | bytes 786440 | tf_op jit(solution)/shard_map/ppermute | solution.py:19
  13.7 1.9 %collective-permute-start.3 = (bf16[128,1024]{1,0:T(8,128)(2,1)S(1)}, bf16[128,1024]{1,0:T(8,128)(2,1)S(1)}, u32[]{:S(2)}, u32[]{:S(2)}) collective-permute-start(bf16[128,1024]{1,0:T(8,128)(2,1)S(1)} %get-tuple-element.30), channel_id=1, source_target_pairs={{1,0},{0,1},{3,2},{2,3},{5,4},{4,5},{7,6},{6,7},{9,8},{8,9},{11,10... | collective-permute-start | bytes 786440 | tf_op jit(solution)/shard_map/ppermute | solution.py:19
  13.8 1.7 %collective-permute-start.5 = (bf16[64,1024]{1,0:T(8,128)(2,1)S(1)}, bf16[64,1024]{1,0:T(8,128)(2,1)S(1)}, u32[]{:S(2)}, u32[]{:S(2)}) collective-permute-start(bf16[64,1024]{1,0:T(8,128)(2,1)S(1)} %get-tuple-element.41), channel_id=1, source_target_pairs={{1,0},{0,1},{3,2},{2,3},{5,4},{4,5},{7,6},{6,7},{9,8},{8,9},{11,10... | collective-permute-start | bytes 393224 | tf_op jit(solution)/shard_map/ppermute | solution.py:19
  14.3 1.3 %collective-permute-start.4 = (bf16[64,1024]{1,0:T(8,128)(2,1)S(1)}, bf16[64,1024]{1,0:T(8,128)(2,1)S(1)}, u32[]{:S(2)}, u32[]{:S(2)}) collective-permute-start(bf16[64,1024]{1,0:T(8,128)(2,1)S(1)} %get-tuple-element.42), channel_id=1, source_target_pairs={{1,0},{0,1},{3,2},{2,3},{5,4},{4,5},{7,6},{6,7},{9,8},{8,9},{11,10... | collective-permute-start | bytes 393224 | tf_op jit(solution)/shard_map/ppermute | solution.py:19
  18.2 8.2 %collective-permute-start.7 = (bf16[128,1024]{1,0:T(8,128)(2,1)S(1)}, bf16[128,1024]{1,0:T(8,128)(2,1)S(1)}, u32[]{:S(2)}, u32[]{:S(2)}) collective-permute-start(bf16[128,1024]{1,0:T(8,128)(2,1)S(1)} %get-tuple-element.36), channel_id=1, source_target_pairs={{4,0},{8,4},{12,8},{0,12},{5,1},{9,5},{13,9},{1,13},{6,2},{10,6},{... | collective-permute-start | bytes 786440 | tf_op jit(solution)/shard_map/ppermute | solution.py:19
  22.6 0.7 %copy-start.2 = (s32[4]{0:T(128)S(1)}, s32[4]{0:T(128)}, u32[]{:S(2)}) copy-start(s32[4]{0:T(128)} %offsets_ref.1) | copy-start | bytes 52
  22.6 0.7 %copy-start.3 = (s32[16]{0:T(128)S(1)}, s32[16]{0:T(128)}, u32[]{:S(2)}) copy-start(s32[16]{0:T(128)} %param.9) | copy-start | bytes 196
  26.8 3.9 %collective-permute-start.10 = (f32[2,16]{1,0:T(2,128)S(1)}, f32[2,16]{1,0:T(2,128)S(1)}, u32[]{:S(2)}, u32[]{:S(2)}) collective-permute-start(f32[2,16]{1,0:T(2,128)S(1)} %shard_map.92), channel_id=1, source_target_pairs={{9,0},{8,1},{11,2},{10,3},{13,4},{12,5},{15,6},{14,7},{1,8},{0,9},... | collective-permute-start | bytes 392 | tf_op jit(solution)/shard_map/ppermute | solution.py:23
  26.8 4.5 %collective-permute-start.9 = (f32[2,16]{1,0:T(2,128)S(1)}, f32[2,16]{1,0:T(2,128)S(1)}, u32[]{:S(2)}, u32[]{:S(2)}) collective-permute-start(f32[2,16]{1,0:T(2,128)S(1)} %shard_map.92), channel_id=1, source_target_pairs={{8,0},{9,1},{10,2},{11,3},{12,4},{13,5},{14,6},{15,7},{0,8},{1,9},... | collective-permute-start | bytes 392 | tf_op jit(solution)/shard_map/ppermute | solution.py:23
  28.0 3.4 %collective-permute-start.8 = (f32[2,16]{1,0:T(2,128)S(1)}, f32[2,16]{1,0:T(2,128)S(1)}, u32[]{:S(2)}, u32[]{:S(2)}) collective-permute-start(f32[2,16]{1,0:T(2,128)S(1)} %shard_map.92), channel_id=1, source_target_pairs={{1,0},{0,1},{3,2},{2,3},{5,4},{4,5},{7,6},{6,7},{9,8},{8,9},{11,10... | collective-permute-start | bytes 392 | tf_op jit(solution)/shard_map/ppermute | solution.py:23
  31.3 4.7 %collective-permute-start.13 = (f32[2,16]{1,0:T(2,128)S(1)}, f32[2,16]{1,0:T(2,128)S(1)}, u32[]{:S(2)}, u32[]{:S(2)}) collective-permute-start(f32[2,16]{1,0:T(2,128)S(1)} %add_add_fusion), channel_id=1, source_target_pairs={{6,0},{7,1},{4,2},{5,3},{2,4},{3,5},{0,6},{1,7},{14,8},{15,9},{12,... | collective-permute-start | bytes 392 | tf_op jit(solution)/shard_map/ppermute | solution.py:23
  33.4 3.6 %collective-permute-start.12 = (f32[2,16]{1,0:T(2,128)S(1)}, f32[2,16]{1,0:T(2,128)S(1)}, u32[]{:S(2)}, u32[]{:S(2)}) collective-permute-start(f32[2,16]{1,0:T(2,128)S(1)} %add_add_fusion), channel_id=1, source_target_pairs={{4,0},{5,1},{6,2},{7,3},{0,4},{1,5},{2,6},{3,7},{12,8},{13,9},{14,... | collective-permute-start | bytes 392 | tf_op jit(solution)/shard_map/ppermute | solution.py:23
  33.5 3.6 %collective-permute-start.11 = (f32[2,16]{1,0:T(2,128)S(1)}, f32[2,16]{1,0:T(2,128)S(1)}, u32[]{:S(2)}, u32[]{:S(2)}) collective-permute-start(f32[2,16]{1,0:T(2,128)S(1)} %add_add_fusion), channel_id=1, source_target_pairs={{2,0},{3,1},{0,2},{1,3},{6,4},{7,5},{4,6},{5,7},{10,8},{11,9},{8,1... | collective-permute-start | bytes 392 | tf_op jit(solution)/shard_map/ppermute | solution.py:23

commit v9 on v7

--- a/solution.py
+++ b/solution.py
@@ -11,7 +11,7 @@
 
 F32 = jnp.float32
 BF16 = jnp.bfloat16
-PIECES = 2
+PIECES = 1
 
 
 def from_offset(block, axis, distance):

time: 37.8 us -> 37.8 us (level)
    ppermute x8 -> x7, starting transfers between devices: 13.1 us -> 13 us  [from_offset(): lax.ppermute(block, axis, [((i + distance) % count, i) for i in range(cou...]
    ppermute x8 -> x7, waiting for transfers between devices: 5.94 us -> 6.01 us  [from_offset(): lax.ppermute(block, axis, [((i + distance) % count, i) for i in range(cou...]
  transfers between devices with their start and end apart: 14 -> 13, of which waited for: 7 -> 7; matrix products, arithmetic and copies ran while one was open for 0% -> 0% of each run, Pallas kernels for 14% -> 14%
where the time goes in v9:
time: 37.8 us; the launch traced here: 37.6 us
  starting transfers between devices  19.4 us (51%)
  waiting for transfers between devices  8.69 us (23%)
  Pallas kernels  6.2 us (16%)
  local copies, waits for them, and re-layouts  2.11 us (6%)
  between operations  0.71 us (2%)
  other arithmetic  0.57 us (2%)
    ppermute x7, starting transfers between devices, from_offset(): lax.ppermute(block, axis, [((i + distance) % count, i) for i in range(cou...  13 us
    ppermute x6, starting transfers between devices, swapped(): lax.ppermute(block, ('tm', 'space', 'spin'), [(i ^ mask, i) for i in rang...  6.31 us
    pallas_call x9, Pallas kernels, call(): pl.pallas_call(kernel, out_shape=out_shape, in_specs=specs, out_specs=out...  6.2 us
    ppermute x7, waiting for transfers between devices, from_offset(): lax.ppermute(block, axis, [((i + distance) % count, i) for i in range(cou...  6.01 us
    ppermute x6, waiting for transfers between devices, swapped(): lax.ppermute(block, ('tm', 'space', 'spin'), [(i ^ mask, i) for i in rang...  2.68 us
    unnamed x12, local copies, waits for them, and re-layouts  2.11 us
  transfers between devices with their start and end apart: 13, of which 7 were waited for; matrix products, arithmetic and copies ran while one was open for 0% of the time, Pallas kernels for 14%

profile of v9, /device:TPU:0, one launch (start us, length us, event | category | flops | bytes accessed | tf_op | source)
XLA Modules:
  0.0 37.6 jit_solution(11274707524375112816)
XLA Ops:
  0.6 3.0 %collective-permute-start = (bf16[192,128]{1,0:T(8,128)(2,1)}, bf16[192,128]{1,0:T(8,128)(2,1)S(1)}, u32[]{:S(2)}, u32[]{:S(2)}) collective-permute-start(bf16[192,128]{1,0:T(8,128)(2,1)} %bitcast.12), channel_id=1, source_target_pairs={{2,0},{0,2},{3,1},{1,3},{6,4},{4,6},{7,5},{5,7},{10,8},{8,10},{11,... | collective-permute-start | bytes 147464 | tf_op jit(solution)/shard_map/ppermute | solution.py:19
  3.6 0.8 %copy-done.5 = bf16[1,3,2,3,3,8,4]{5,6,4,3,2,1,0:T(4,128)(2,1)S(1)} copy-done((bf16[1,3,2,3,3,8,4]{5,6,4,3,2,1,0:T(4,128)(2,1)S(1)}, bf16[1,3,2,3,3,8,4]{5,6,4,3,2,1,0:T(4,128)(2,1)}, u32[]{:S(2)}) %copy-start.5) | copy-done | bytes 3480
  4.6 0.6 %copy-done.1 = bf16[1,2,3,8,2,2,128]{6,5,4,3,2,1,0:T(2,128)(2,1)S(1)} copy-done((bf16[1,2,3,8,2,2,128]{6,5,4,3,2,1,0:T(2,128)(2,1)S(1)}, bf16[1,2,3,8,2,2,128]{6,5,4,3,2,1,0:T(2,128)(2,1)}, u32[]{:S(2)}) %copy-start.1) | copy-done | bytes 49176
  5.6 1.5 %collective-permute-start.3 = (bf16[128,1024]{1,0:T(8,128)(2,1)S(1)}, bf16[128,1024]{1,0:T(8,128)(2,1)S(1)}, u32[]{:S(2)}, u32[]{:S(2)}) collective-permute-start(bf16[128,1024]{1,0:T(8,128)(2,1)S(1)} %bitcast.10), channel_id=1, source_target_pairs={{2,0},{0,2},{3,1},{1,3},{6,4},{4,6},{7,5},{5,7},{10,8},{8,10},{11,... | collective-permute-start | bytes 786440 | tf_op jit(solution)/shard_map/ppermute | solution.py:19
  7.1 1.3 %collective-permute-done.1.refs_3_ = bf16[32,128]{1,0:T(8,128)(2,1)S(1)} collective-permute-done((bf16[32,128]{1,0:T(8,128)(2,1)S(1)}, bf16[32,128]{1,0:T(8,128)(2,1)S(1)}, u32[]{:S(2)}, u32[]{:S(2)}) %collective-permute-start.1) | collective-permute-done | bytes 8224 | tf_op jit(solution)/shard_map/ppermute | solution.py:19
  8.4 0.8 %shard_map.87.elem_ref = f32[3,2,128,128]{3,2,1,0:T(8,128)S(1)} custom-call(bf16[576,128]{1,0:T(8,128)(2,1)S(1)} %get-tuple-element.20.early_ref, bf16[192,128]{1,0:T(8,128)(2,1)S(1)} %get-tuple-element.21.refs_0_, bf16[192,128]{1,0:T(8,128)(2,1)S(1)} %collective-permute-done.refs_1_, bf16[32,128]{1,0:T(8,128)(2,1)S(1)} %shard_map.85.links_ref.refs_2_, ...), custom_call_target="tpu_custom_call" | custom-call | flops 10000000000 | bytes 1048576 | tf_op jit(solution)/shard_map/pallas_call | solution.py:33
  9.2 0.9 %shard_map.88 = (bf16[512,512]{1,0:T(8,128)(2,1)S(1)}, bf16[128,1024]{1,0:T(8,128)(2,1)S(1)}, f32[128,1024]{1,0:T(8,128)S(1)}) custom-call(s32[3]{0:T(128)S(1)} %copy-done.4, f32[3,2,128,128]{3,2,1,0:T(8,128)S(1)} %shard_map.87.elem_ref, bf16[128,1024]{1,0:T(8,128)(2,1)S(1)} %bitcast.11), custom_call_target="tpu_custom_call" | custom-call | flops 100000000 | bytes 1048576 | tf_op jit(solution)/shard_map/pallas_call | solution.py:33
  10.1 3.6 %collective-permute-start.2 = (bf16[128,1024]{1,0:T(8,128)(2,1)S(1)}, bf16[128,1024]{1,0:T(8,128)(2,1)S(1)}, u32[]{:S(2)}, u32[]{:S(2)}) collective-permute-start(bf16[128,1024]{1,0:T(8,128)(2,1)S(1)} %get-tuple-element.24.refs_0_), channel_id=1, source_target_pairs={{4,0},{8,4},{12,8},{0,12},{5,1},{9,5},{13,9},{1,13},{6,2},{10,6},{... | collective-permute-start | bytes 786440 | tf_op jit(solution)/shard_map/ppermute | solution.py:19
  14.1 0.6 %collective-permute-start.5 = (bf16[128,1024]{1,0:T(8,128)(2,1)S(1)}, bf16[128,1024]{1,0:T(8,128)(2,1)S(1)}, u32[]{:S(2)}, u32[]{:S(2)}) collective-permute-start(bf16[128,1024]{1,0:T(8,128)(2,1)S(1)} %shard_map.89.refs_2_), channel_id=1, source_target_pairs={{1,0},{0,1},{3,2},{2,3},{5,4},{4,5},{7,6},{6,7},{9,8},{8,9},{11,10... | collective-permute-start | bytes 786440 | tf_op jit(solution)/shard_map/ppermute | solution.py:19
  14.6 3.2 %collective-permute-done.2.next_ref = bf16[128,1024]{1,0:T(8,128)(2,1)S(1)} collective-permute-done((bf16[128,1024]{1,0:T(8,128)(2,1)S(1)}, bf16[128,1024]{1,0:T(8,128)(2,1)S(1)}, u32[]{:S(2)}, u32[]{:S(2)}) %collective-permute-start.2) | collective-permute-done | bytes 262176 | tf_op jit(solution)/shard_map/ppermute | solution.py:19
  17.8 0.5 %shard_map.90 = (bf16[512,1024]{1,0:T(8,128)(2,1)S(1)}, bf16[128,1024]{1,0:T(8,128)(2,1)S(1)}, f32[128,1024]{1,0:T(8,128)S(1)}) custom-call(bf16[128,1024]{1,0:T(8,128)(2,1)S(1)} %collective-permute-done.2.next_ref, bf16[128,1024]{1,0:T(8,128)(2,1)S(1)} %get-tuple-element.24.refs_0_, bf16[128,1024]{1,0:T(8,128)(2,1)S(1)} %collective-permute-done.4.refs_1_, ...), custom_call_target="tpu_custom_call" | custom-call | flops 300000000 | bytes 1048576 | tf_op jit(solution)/shard_map/pallas_call | solution.py:33
  18.3 4.3 %collective-permute-start.6 = (bf16[128,1024]{1,0:T(8,128)(2,1)S(1)}, bf16[128,1024]{1,0:T(8,128)(2,1)S(1)}, u32[]{:S(2)}, u32[]{:S(2)}) collective-permute-start(bf16[128,1024]{1,0:T(8,128)(2,1)S(1)} %get-tuple-element.31), channel_id=1, source_target_pairs={{4,0},{8,4},{12,8},{0,12},{5,1},{9,5},{13,9},{1,13},{6,2},{10,6},{... | collective-permute-start | bytes 786440 | tf_op jit(solution)/shard_map/ppermute | solution.py:19
  22.7 0.7 %copy-done.2 = s32[4]{0:T(128)S(1)} copy-done((s32[4]{0:T(128)S(1)}, s32[4]{0:T(128)}, u32[]{:S(2)}) %copy-start.2) | copy-done | bytes 40
  23.3 1.6 %shard_map.91 = (bf16[128,1024]{1,0:T(8,128)(2,1)S(1)}, f32[8,128]{1,0:T(8,128)S(1)}, f32[64,3,2,64]{3,2,1,0:T(2,128)}, f32[8,128]{1,0:T(8,128)S(1)}) custom-call(s32[4]{0:T(128)S(1)} %copy-done.2, s32[1,16]{1,0:T(1,128)S(1)} %bitcast.14, bf16[512,1024]{1,0:T(8,128)(2,1)S(1)} %get-tuple-element.27.first_ref, f32[3,2,128,128]{3,2,1,0:T(8,128)S(1)} %shard_map.87.elem_ref, ...), custom_call_target="tpu_custom_call" | custom-call | flops 1000000 | bytes 1048576 | tf_op jit(solution)/shard_map/pallas_call | solution.py:33
  25.0 1.6 %collective-permute-done.6.second_ref = bf16[128,1024]{1,0:T(8,128)(2,1)S(1)} collective-permute-done((bf16[128,1024]{1,0:T(8,128)(2,1)S(1)}, bf16[128,1024]{1,0:T(8,128)(2,1)S(1)}, u32[]{:S(2)}, u32[]{:S(2)}) %collective-permute-start.6) | collective-permute-done | bytes 262176 | tf_op jit(solution)/shard_map/ppermute | solution.py:19
  26.9 1.1 %collective-permute-start.8 = (f32[2,16]{1,0:T(2,128)S(1)}, f32[2,16]{1,0:T(2,128)S(1)}, u32[]{:S(2)}, u32[]{:S(2)}) collective-permute-start(f32[2,16]{1,0:T(2,128)S(1)} %shard_map.93), channel_id=1, source_target_pairs={{8,0},{9,1},{10,2},{11,3},{12,4},{13,5},{14,6},{15,7},{0,8},{1,9},... | collective-permute-start | bytes 392 | tf_op jit(solution)/shard_map/ppermute | solution.py:23
  28.0 1.7 %collective-permute-start.7 = (f32[2,16]{1,0:T(2,128)S(1)}, f32[2,16]{1,0:T(2,128)S(1)}, u32[]{:S(2)}, u32[]{:S(2)}) collective-permute-start(f32[2,16]{1,0:T(2,128)S(1)} %shard_map.93), channel_id=1, source_target_pairs={{1,0},{0,1},{3,2},{2,3},{5,4},{4,5},{7,6},{6,7},{9,8},{8,9},{11,10... | collective-permute-start | bytes 392 | tf_op jit(solution)/shard_map/ppermute | solution.py:23
  29.7 1.1 %shard_map.92 = bf16[128,1024]{1,0:T(8,128)(2,1)} custom-call(bf16[128,1024]{1,0:T(8,128)(2,1)S(1)} %collective-permute-done.6.second_ref, bf16[512,1024]{1,0:T(8,128)(2,1)S(1)} %get-tuple-element.27.first_ref), custom_call_target="tpu_custom_call" | custom-call | flops 100000000 | bytes 1048576 | tf_op jit(solution)/shard_map/pallas_call | solution.py:33
  30.8 0.6 %collective-permute-done.8 = f32[2,16]{1,0:T(2,128)S(1)} collective-permute-done((f32[2,16]{1,0:T(2,128)S(1)}, f32[2,16]{1,0:T(2,128)S(1)}, u32[]{:S(2)}, u32[]{:S(2)}) %collective-permute-start.8) | collective-permute-done | bytes 160 | tf_op jit(solution)/shard_map/ppermute | solution.py:23
  31.4 1.9 %collective-permute-start.12 = (f32[2,16]{1,0:T(2,128)S(1)}, f32[2,16]{1,0:T(2,128)S(1)}, u32[]{:S(2)}, u32[]{:S(2)}) collective-permute-start(f32[2,16]{1,0:T(2,128)S(1)} %add_add_fusion), channel_id=1, source_target_pairs={{6,0},{7,1},{4,2},{5,3},{2,4},{3,5},{0,6},{1,7},{14,8},{15,9},{12,... | collective-permute-start | bytes 392 | tf_op jit(solution)/shard_map/ppermute | solution.py:23
  33.5 1.5 %collective-permute-start.10 = (f32[2,16]{1,0:T(2,128)S(1)}, f32[2,16]{1,0:T(2,128)S(1)}, u32[]{:S(2)}, u32[]{:S(2)}) collective-permute-start(f32[2,16]{1,0:T(2,128)S(1)} %add_add_fusion), channel_id=1, source_target_pairs={{2,0},{3,1},{0,2},{1,3},{6,4},{7,5},{4,6},{5,7},{10,8},{11,9},{8,1... | collective-permute-start | bytes 392 | tf_op jit(solution)/shard_map/ppermute | solution.py:23
  35.0 1.0 %collective-permute-done.12 = f32[2,16]{1,0:T(2,128)S(1)} collective-permute-done((f32[2,16]{1,0:T(2,128)S(1)}, f32[2,16]{1,0:T(2,128)S(1)}, u32[]{:S(2)}, u32[]{:S(2)}) %collective-permute-start.12) | collective-permute-done | bytes 160 | tf_op jit(solution)/shard_map/ppermute | solution.py:23
  36.0 1.0 %collective-permute-done.11 = f32[2,16]{1,0:T(2,128)S(1)} collective-permute-done((f32[2,16]{1,0:T(2,128)S(1)}, f32[2,16]{1,0:T(2,128)S(1)}, u32[]{:S(2)}, u32[]{:S(2)}) %collective-permute-start.11) | collective-permute-done | bytes 160 | tf_op jit(solution)/shard_map/ppermute | solution.py:23
  37.1 0.6 %add_bitcast_fusion = f32[16,2]{0,1:T(2,128)} fusion(f32[2,16]{1,0:T(2,128)S(1)} %collective-permute-done.12, f32[2,16]{1,0:T(2,128)S(1)} %collective-permute-done.11, f32[2,16]{1,0:T(2,128)S(1)} %add_add_fusion, f32[2,16]{1,0:T(2,128)S(1)} %collective-permute-done.10), kind=kLoop, calls=%fused_computation | loop fusion | flops 96 | bytes 640 | tf_op jit(solution)/shard_map/transpose | solution.py:451
  (25 shorter events, 1.5 us)
Async XLA Ops:
  0.6 7.7 %collective-permute-start = (bf16[192,128]{1,0:T(8,128)(2,1)}, bf16[192,128]{1,0:T(8,128)(2,1)S(1)}, u32[]{:S(2)}, u32[]{:S(2)}) collective-permute-start(bf16[192,128]{1,0:T(8,128)(2,1)} %bitcast.12), channel_id=1, source_target_pairs={{2,0},{0,2},{3,1},{1,3},{6,4},{4,6},{7,5},{5,7},{10,8},{8,10},{11,... | collective-permute-start | bytes 147464 | tf_op jit(solution)/shard_map/ppermute | solution.py:19
  3.6 0.8 %copy-start.5 = (bf16[1,3,2,3,3,8,4]{5,6,4,3,2,1,0:T(4,128)(2,1)S(1)}, bf16[1,3,2,3,3,8,4]{5,6,4,3,2,1,0:T(4,128)(2,1)}, u32[]{:S(2)}) copy-start(bf16[1,3,2,3,3,8,4]{5,6,4,3,2,1,0:T(4,128)(2,1)} %param.7) | copy-start | bytes 10372
  4.4 0.8 %copy-start.1 = (bf16[1,2,3,8,2,2,128]{6,5,4,3,2,1,0:T(2,128)(2,1)S(1)}, bf16[1,2,3,8,2,2,128]{6,5,4,3,2,1,0:T(2,128)(2,1)}, u32[]{:S(2)}) copy-start(bf16[1,2,3,8,2,2,128]{6,5,4,3,2,1,0:T(2,128)(2,1)} %param.6) | copy-start | bytes 147460
  4.5 1.2 %copy-start = (bf16[1,128,1024]{2,1,0:T(8,128)(2,1)S(1)}, bf16[1,128,1024]{2,1,0:T(8,128)(2,1)}, u32[]{:S(2)}) copy-start(bf16[1,128,1024]{2,1,0:T(8,128)(2,1)} %param.8) | copy-start | bytes 786436
  4.6 3.8 %collective-permute-start.1 = (bf16[32,128]{1,0:T(8,128)(2,1)S(1)}, bf16[32,128]{1,0:T(8,128)(2,1)S(1)}, u32[]{:S(2)}, u32[]{:S(2)}) collective-permute-start(bf16[32,128]{1,0:T(8,128)(2,1)S(1)} %shard_map.85.links_ref.refs_2_), channel_id=1, source_target_pairs={{2,0},{0,2},{3,1},{1,3},{6,4},{4,6},{7,5},{5,7},{10,8},{8,10},{11,... | collective-permute-start | bytes 24584 | tf_op jit(solution)/shard_map/ppermute | solution.py:19
  5.6 8.1 %collective-permute-start.3 = (bf16[128,1024]{1,0:T(8,128)(2,1)S(1)}, bf16[128,1024]{1,0:T(8,128)(2,1)S(1)}, u32[]{:S(2)}, u32[]{:S(2)}) collective-permute-start(bf16[128,1024]{1,0:T(8,128)(2,1)S(1)} %bitcast.10), channel_id=1, source_target_pairs={{2,0},{0,2},{3,1},{1,3},{6,4},{4,6},{7,5},{5,7},{10,8},{8,10},{11,... | collective-permute-start | bytes 786440 | tf_op jit(solution)/shard_map/ppermute | solution.py:19
  8.4 0.8 %copy-start.4 = (s32[3]{0:T(128)S(1)}, s32[3]{0:T(128)}, u32[]{:S(2)}) copy-start(s32[3]{0:T(128)} %dirs_ref.1) | copy-start | bytes 40
  10.1 7.7 %collective-permute-start.2 = (bf16[128,1024]{1,0:T(8,128)(2,1)S(1)}, bf16[128,1024]{1,0:T(8,128)(2,1)S(1)}, u32[]{:S(2)}, u32[]{:S(2)}) collective-permute-start(bf16[128,1024]{1,0:T(8,128)(2,1)S(1)} %get-tuple-element.24.refs_0_), channel_id=1, source_target_pairs={{4,0},{8,4},{12,8},{0,12},{5,1},{9,5},{13,9},{1,13},{6,2},{10,6},{... | collective-permute-start | bytes 786440 | tf_op jit(solution)/shard_map/ppermute | solution.py:19
  13.7 4.0 %collective-permute-start.4 = (bf16[128,1024]{1,0:T(8,128)(2,1)S(1)}, bf16[128,1024]{1,0:T(8,128)(2,1)S(1)}, u32[]{:S(2)}, u32[]{:S(2)}) collective-permute-start(bf16[128,1024]{1,0:T(8,128)(2,1)S(1)} %get-tuple-element.24.refs_0_), channel_id=1, source_target_pairs={{1,0},{0,1},{3,2},{2,3},{5,4},{4,5},{7,6},{6,7},{9,8},{8,9},{11,10... | collective-permute-start | bytes 786440 | tf_op jit(solution)/shard_map/ppermute | solution.py:19
  14.1 3.7 %collective-permute-start.5 = (bf16[128,1024]{1,0:T(8,128)(2,1)S(1)}, bf16[128,1024]{1,0:T(8,128)(2,1)S(1)}, u32[]{:S(2)}, u32[]{:S(2)}) collective-permute-start(bf16[128,1024]{1,0:T(8,128)(2,1)S(1)} %shard_map.89.refs_2_), channel_id=1, source_target_pairs={{1,0},{0,1},{3,2},{2,3},{5,4},{4,5},{7,6},{6,7},{9,8},{8,9},{11,10... | collective-permute-start | bytes 786440 | tf_op jit(solution)/shard_map/ppermute | solution.py:19
  18.3 8.2 %collective-permute-start.6 = (bf16[128,1024]{1,0:T(8,128)(2,1)S(1)}, bf16[128,1024]{1,0:T(8,128)(2,1)S(1)}, u32[]{:S(2)}, u32[]{:S(2)}) collective-permute-start(bf16[128,1024]{1,0:T(8,128)(2,1)S(1)} %get-tuple-element.31), channel_id=1, source_target_pairs={{4,0},{8,4},{12,8},{0,12},{5,1},{9,5},{13,9},{1,13},{6,2},{10,6},{... | collective-permute-start | bytes 786440 | tf_op jit(solution)/shard_map/ppermute | solution.py:19
  22.7 0.7 %copy-start.2 = (s32[4]{0:T(128)S(1)}, s32[4]{0:T(128)}, u32[]{:S(2)}) copy-start(s32[4]{0:T(128)} %offsets_ref.1) | copy-start | bytes 52
  22.7 0.7 %copy-start.3 = (s32[16]{0:T(128)S(1)}, s32[16]{0:T(128)}, u32[]{:S(2)}) copy-start(s32[16]{0:T(128)} %param.9) | copy-start | bytes 196
  26.9 3.9 %collective-permute-start.9 = (f32[2,16]{1,0:T(2,128)S(1)}, f32[2,16]{1,0:T(2,128)S(1)}, u32[]{:S(2)}, u32[]{:S(2)}) collective-permute-start(f32[2,16]{1,0:T(2,128)S(1)} %shard_map.93), channel_id=1, source_target_pairs={{9,0},{8,1},{11,2},{10,3},{13,4},{12,5},{15,6},{14,7},{1,8},{0,9},... | collective-permute-start | bytes 392 | tf_op jit(solution)/shard_map/ppermute | solution.py:23
  26.9 4.5 %collective-permute-start.8 = (f32[2,16]{1,0:T(2,128)S(1)}, f32[2,16]{1,0:T(2,128)S(1)}, u32[]{:S(2)}, u32[]{:S(2)}) collective-permute-start(f32[2,16]{1,0:T(2,128)S(1)} %shard_map.93), channel_id=1, source_target_pairs={{8,0},{9,1},{10,2},{11,3},{12,4},{13,5},{14,6},{15,7},{0,8},{1,9},... | collective-permute-start | bytes 392 | tf_op jit(solution)/shard_map/ppermute | solution.py:23
  28.0 3.4 %collective-permute-start.7 = (f32[2,16]{1,0:T(2,128)S(1)}, f32[2,16]{1,0:T(2,128)S(1)}, u32[]{:S(2)}, u32[]{:S(2)}) collective-permute-start(f32[2,16]{1,0:T(2,128)S(1)} %shard_map.93), channel_id=1, source_target_pairs={{1,0},{0,1},{3,2},{2,3},{5,4},{4,5},{7,6},{6,7},{9,8},{8,9},{11,10... | collective-permute-start | bytes 392 | tf_op jit(solution)/shard_map/ppermute | solution.py:23
  31.4 4.5 %collective-permute-start.12 = (f32[2,16]{1,0:T(2,128)S(1)}, f32[2,16]{1,0:T(2,128)S(1)}, u32[]{:S(2)}, u32[]{:S(2)}) collective-permute-start(f32[2,16]{1,0:T(2,128)S(1)} %add_add_fusion), channel_id=1, source_target_pairs={{6,0},{7,1},{4,2},{5,3},{2,4},{3,5},{0,6},{1,7},{14,8},{15,9},{12,... | collective-permute-start | bytes 392 | tf_op jit(solution)/shard_map/ppermute | solution.py:23
  33.4 3.6 %collective-permute-start.11 = (f32[2,16]{1,0:T(2,128)S(1)}, f32[2,16]{1,0:T(2,128)S(1)}, u32[]{:S(2)}, u32[]{:S(2)}) collective-permute-start(f32[2,16]{1,0:T(2,128)S(1)} %add_add_fusion), channel_id=1, source_target_pairs={{4,0},{5,1},{6,2},{7,3},{0,4},{1,5},{2,6},{3,7},{12,8},{13,9},{14,... | collective-permute-start | bytes 392 | tf_op jit(solution)/shard_map/ppermute | solution.py:23
  33.5 3.6 %collective-permute-start.10 = (f32[2,16]{1,0:T(2,128)S(1)}, f32[2,16]{1,0:T(2,128)S(1)}, u32[]{:S(2)}, u32[]{:S(2)}) collective-permute-start(f32[2,16]{1,0:T(2,128)S(1)} %add_add_fusion), channel_id=1, source_target_pairs={{2,0},{3,1},{0,2},{1,3},{6,4},{7,5},{4,6},{5,7},{10,8},{11,9},{8,1... | collective-permute-start | bytes 392 | tf_op jit(solution)/shard_map/ppermute | solution.py:23
